TPU v7x, 512 devices: a whole 4x4x16 slice. The times are simulated.
512 devices in a mesh: param: 32 (over z, core), ex: 16 (over y, x).
Axes of the slice: x: 4, y: 4, z: 16, core: 2. Of those that a mesh axis runs over, the one named last changes fastest.
Arguments:
- activations: bfloat16 [32, 1024, 4096], P('ex', None, 'param'), may hold values from -6 to 6
- out_grad: bfloat16 [32, 1024, 4096], P('ex', 'param'), may hold values from -6 to 6
- sign_bits: int32 [4096, 4096], P('param'), may hold values from 0 to 1
- sample_index: int32 [8192], replicated, may hold values from 0 to 16777215, as said below
Outputs:
- features: float32 [32, 8192], P('ex', 'param')
- gram: float32 [32, 32], P('ex')
Inputs may be any that keep to these rules, and one draw needn't show every extreme that they name: `sample_index`: feature k samples a coordinate of the k // 256-th of the 32 consecutive blocks of 524288 coordinates.
All inputs are finite; a program needn't handle non-finite values.
Results may differ from a plain program's by a relative error of at most 0.0003.
Values may be sent and summed in bfloat16 or wider, within the bound.
No kernel may reach another device: no remote copies, remote signals or barrier semaphores. Data moves between devices by JAX's collectives and lax.ppermute only.
A program may use at most 64 MiB of HBM per device.

v0:
```python
import jax
import jax.numpy as jnp
import numpy as np
from jax import lax
from jax.sharding import PartitionSpec as P


def sylvester(order):
    table = np.ones((1, 1), np.float32)
    base = np.array([[1.0, 1.0], [1.0, -1.0]], np.float32)
    while table.shape[0] < order:
        table = np.kron(table, base)
    return table


def make_adder(act_rows, piece):
    return jnp.einsum("etr,etd->erd", act_rows, piece, preferred_element_type=jnp.float32)


def local_transform(signed):
    count, rows, width = signed.shape
    inner = min(width, 128)
    outer = width // inner
    hp = lax.Precision.HIGHEST
    row_table = jnp.asarray(sylvester(rows), jnp.float32)
    small = jnp.asarray(sylvester(inner), jnp.float32)
    large = jnp.asarray(sylvester(outer), jnp.float32)
    mixed = jnp.einsum("sr,erd->esd", row_table, signed, precision=hp)
    mixed = mixed.reshape(count, rows, outer, inner)
    mixed = jnp.einsum("ermn,nk->ermk", mixed, small, precision=hp)
    mixed = jnp.einsum("ermn,am->eran", mixed, large, precision=hp)
    return mixed.reshape(count, rows * width)


def per_device(activations, out_grad, sign_bits, sample_index):
    count, seq_len, rows = activations.shape
    width = out_grad.shape[2]
    devices = lax.axis_size("param")
    me = lax.axis_index("param")
    grad = make_adder(activations, lax.all_gather(out_grad, "param", axis=1, tiled=True))
    signed = jnp.where(sign_bits[None] == 1, grad, -grad)
    mixed = local_transform(signed)
    block = rows * width
    local_index = sample_index % block
    picked = jnp.take(mixed, local_index, axis=1)
    feature_count = picked.shape[1]
    per = feature_count // devices
    grouped = picked.reshape(count, devices, per)
    table = jnp.asarray(sylvester(devices), jnp.float32)
    column = lax.dynamic_slice_in_dim(table, me, 1, 1)[:, 0]
    terms = grouped * column[None, :, None]
    summed = lax.psum_scatter(terms, "param", scatter_dimension=1, tiled=True).reshape(count, per)
    scale = 1.0 / (width * float(seq_len) ** 0.5)
    features = summed * scale
    everyone = lax.all_gather(features, "ex", axis=0, tiled=True)
    inner = jnp.dot(features, everyone.T, precision=lax.Precision.HIGHEST)
    gram = lax.psum(inner, "param") / feature_count
    return (features, gram)


def solution(mesh):
    return jax.shard_map(
        per_device,
        mesh=mesh,
        in_specs=(P("ex", None, "param"), P("ex", "param", None), P("param", None), P()),
        out_specs=(P("ex", "param"), P("ex", None)),
        check_vma=False,
    )
```

profile of v0, /device:TPU:1, one launch (start us, length us, event | category | flops | bytes accessed | tf_op | source)
XLA Modules:
  0.0 523.2 jit_solution(5749648933232891881)
XLA Ops:
  7.2 0.0 copy-start
  7.2 0.0 all-gather.3.cloned.1.call-start
  7.2 0.7 all-gather.3.cloned.1.call-update
  7.9 0.0 all-reduce.3.cloned.1.call-start
  8.0 0.8 compare_and_fusion
  8.8 0.9 dynamic-slice_reduce_fusion
  9.7 0.8 broadcast_clamp_fusion
  10.5 1.9 broadcast_compare_fusion
  12.4 0.0 copy-start.2
  12.4 110.3 %all-gather.3.cloned.1.call-done = bf16[2,1024,4096]{2,1,0:T(8,128)(2,1)} async-done(((bf16[2,32,4096]{2,1,0:T(8,128)(2,1)}), bf16[2,1024,4096]{2,1,0:T(8,128)(2,1)}) %all-gather.3.cloned.1.call-update) | async-done | bytes 16777232 | tf_op jit(solution)/shard_map/all_gather | solution.py:40
  122.7 0.0 copy-done
  122.7 8.2 %fusion.6 = f32[2,128,4096]{2,1,0:T(8,128)S(1)} fusion(bf16[2,1024,128]{2,1,0:T(8,128)(2,1)S(1)} %copy-done, bf16[2,1024,4096]{2,1,0:T(8,128)(2,1)} %all-gather.3.cloned.1.call-done), kind=kOutput, calls=%fused_computation.20 | convolution fusion | flops 2147483648 | bytes 21495808 | tf_op jit(solution)/shard_map/etr,etd->erd/dot_general | solution.py:17
  130.9 0.0 copy-done.2
  130.9 8.5 %fusion = f32[2,4096,128]{2,1,0:T(8,128)} fusion(f32[128,128,1]{1,0,2:T(8,128)S(1)} %copy-done.2, f32[2,128,4096]{2,1,0:T(8,128)S(1)} %fusion.6, pred[128,4096]{1,0:T(8,128)(4,1)S(1)} %broadcast_compare_fusion), kind=kOutput, calls=%fused_computation.2 | convolution fusion | flops 1612709888 | bytes 8978432 | tf_op jit(solution)/shard_map/sr,erd->esd/dot_general | solution.py:28
  139.4 5.5 %copy.18 = f32[2,128,32,128]{3,2,1,0:T(8,128)} copy(f32[2,128,32,128]{1,3,2,0:T(8,128)} %bitcast.34) | data formatting | bytes 8388608 | tf_op jit(solution)/shard_map/reshape | solution.py:29
  144.9 0.0 copy-done.1
  144.9 6.3 %fusion.7 = f32[2,128,32,128]{3,2,1,0:T(8,128)S(1)} fusion(f32[2,128,32,128]{3,2,1,0:T(8,128)} %copy.18, f32[128,128,1,1]{1,0,3,2:T(8,128)S(1)} %copy-done.1), kind=kOutput, calls=%fused_computation.21 | convolution fusion | flops 1610612736 | bytes 8454144 | tf_op jit(solution)/shard_map/ermn,nk->ermk/dot_general | solution.py:30
  151.3 0.0 copy-done.3
  151.3 3.9 fusion.8
  155.1 16.4 %copy.32 = f32[1,2,4096,128]{3,1,2,0:T(2,128)} copy(f32[1,2,4096,128]{3,2,1,0:T(8,128)S(1)} %bitcast.35) | data formatting | bytes 8388608
  171.5 91.2 %gather_fusion = f32[8192,2]{0,1:T(2,128)S(1)} fusion(f32[2,524288]{1,0:T(2,128)} %bitcast.33, s32[8192]{0:T(1024)S(1)} %broadcast_clamp_fusion), kind=kCustom, calls=%fused_computation | custom fusion | bytes 163840 | tf_op jit(solution)/shard_map/jit(_take)/gather | solution.py:45
  262.6 0.7 select_multiply_fusion
  263.4 0.0 all-reduce.3.cloned.1.call-update
  263.4 1.3 dynamic-slice
  264.7 179.8 %all-reduce.3.cloned.1.call-done = f32[2,32,256]{2,0,1:T(2,128)} async-done(((f32[2,32,256]{2,0,1:T(2,128)}), f32[2,32,256]{2,0,1:T(2,128)}) %all-reduce.3.cloned.1.call-update) | async-done | bytes 65552
  444.4 1.3 dynamic-slice_multiply_fusion
  445.8 17.7 %all-gather = f32[32,1,256]{2,1,0:T(1,128)S(1)} all-gather(f32[2,1,256]{2,1,0:T(1,128)S(1)} %copy.20), channel_id=2, replica_groups=mesh['param'=32,'ex'=16] {'ex'}, dimensions={0}, use_global_device_ids=true | all-gather | bytes 34816 | tf_op jit(solution)/shard_map/all_gather | solution.py:55
  463.4 1.3 fusion.17
  464.8 0.1 fusion.3
  464.9 50.9 %psum.7 = f32[2,32]{1,0:T(2,128)S(1)} all-reduce(f32[2,32]{1,0:T(2,128)S(1)} %fusion.3), channel_id=1, replica_groups=mesh['param'=32,'ex'=16] {'param'}, use_global_device_ids=true, to_apply=%region_1.2 | all-reduce | flops 64 | bytes 512 | tf_op jit(solution)/shard_map/psum | solution.py:57
  515.8 0.6 broadcast_multiply_fusion
  516.4 0.0 copy-done.4
  (5 shorter events, 0.0 us)
Async XLA Ops:
  7.2 115.5 %copy-start = (bf16[2,1024,128]{2,1,0:T(8,128)(2,1)S(1)}, bf16[2,1024,128]{2,1,0:T(8,128)(2,1)}, u32[]{:S(2)}) copy-start(bf16[2,1024,128]{2,1,0:T(8,128)(2,1)} %param.8) | copy-start | bytes 1572868
  7.2 115.5 %all-gather.3.cloned.1.call-start = ((), (), s32[]{:S(2)}) async-start(), calls=%async_computation | async-start | bytes 17301504 | tf_op jit(solution)/shard_map/all_gather | solution.py:40
  7.9 436.5 %all-reduce.3.cloned.1.call-start = ((), (), s32[]{:S(2)}) async-start(), calls=%async_computation.1 | async-start | bytes 131072
  12.4 118.5 %copy-start.2 = (f32[128,128,1]{1,0,2:T(8,128)S(1)}, f32[128,128,1]{1,0,2:T(8,128)}, u32[]{:S(2)}) copy-start(f32[128,128,1]{1,0,2:T(8,128)} %constant.56) | copy-start | bytes 196612
  139.4 5.5 %copy-start.1 = (f32[128,128,1,1]{1,0,3,2:T(8,128)S(1)}, f32[128,128,1,1]{1,0,3,2:T(8,128)}, u32[]{:S(2)}) copy-start(f32[128,128,1,1]{1,0,3,2:T(8,128)} %constant.57) | copy-start | bytes 196612
  144.9 6.3 %copy-start.3 = (f32[32,32,1,1]{1,0,3,2:T(8,128)S(1)}, f32[32,32,1,1]{1,0,3,2:T(8,128)}, u32[]{:S(2)}) copy-start(f32[32,32,1,1]{1,0,3,2:T(8,128)} %constant.58) | copy-start | bytes 12292
  464.8 51.6 %copy-start.4 = (f32[2,256]{1,0:T(2,128)}, f32[2,256]{1,0:T(2,128)S(1)}, u32[]{:S(2)}) copy-start(f32[2,256]{1,0:T(2,128)S(1)} %fusion.17) | copy-start | bytes 6148
Sparse Core Ops, SparseCore 0:
  10.2 112.4 all-gather.2
  263.5 180.8 all-reduce.2
where the time goes:
time: 525 us; the launch traced here: 523 us
  waiting for transfers between devices  291 us (55%)
  local copies, waits for them, and re-layouts  115 us (22%)
  blocking collectives  68.6 us (13%)
  matrix products  27 us (5%)
  between operations  14.1 us (3%)
  other arithmetic  7.42 us (1%)
    unnamed x3, waiting for transfers between devices  180 us
    all_gather x1, waiting for transfers between devices, per_device(): lax.all_gather(out_grad, 'param', axis=1, tiled=True)  110 us
    gather x1, local copies, waits for them, and re-layouts, per_device(): picked = jnp.take(mixed, local_index, axis=1)  91.2 us
    psum x1, blocking collectives, per_device(): gram = lax.psum(inner, 'param') / feature_count  50.9 us
    all_gather x1, blocking collectives, per_device(): everyone = lax.all_gather(features, 'ex', axis=0, tiled=True)  17.7 us
    unnamed x12, local copies, waits for them, and re-layouts  17.6 us
  transfers between devices with their start and end apart: 2, of which 2 were waited for; matrix products, arithmetic and copies ran while one was open for 1% of the time, Pallas kernels for 0%

commit v1 on v0

v1 whole, which is shorter than its diff:
```python
import jax
import jax.numpy as jnp
import numpy as np
from jax import lax
from jax.experimental import pallas as pl
from jax.experimental.pallas import tpu as pltpu
from jax.sharding import PartitionSpec as P

LANES = 128


def sylvester(order):
    table = np.ones((1, 1), np.float32)
    base = np.array([[1.0, 1.0], [1.0, -1.0]], np.float32)
    while table.shape[0] < order:
        table = np.kron(table, base)
    return table


def halves(value):
    high = value.astype(jnp.bfloat16)
    low = (value - high.astype(jnp.float32)).astype(jnp.bfloat16)
    return high, low


def sampled_transform(rows_ref, grad_ref, bits_ref, pattern_ref, table_ref, ones_ref, out_ref, mixed, stage):
    examples, rows, width = grad_ref.shape
    outer = width // LANES
    wide = 4 * LANES
    pieces = width // wide

    def row_step(i, carry):
        example, piece = lax.div(i, pieces), lax.rem(i, pieces)
        columns = pl.ds(pl.multiple_of(piece * wide, wide), wide)
        value = grad_ref[example, :, columns]
        signed = jnp.where(bits_ref[:, columns] == 1, value, -value)
        out = jnp.dot(table_ref[...], jnp.concatenate(halves(signed), axis=0), preferred_element_type=jnp.float32)
        for t in range(wide // LANES):
            first = pl.multiple_of((piece * (wide // LANES) + t) * rows, rows)
            mixed[example, pl.ds(first, rows), :] = out[:, t * LANES:(t + 1) * LANES]
        return carry

    lax.fori_loop(0, examples * pieces, row_step, 0)

    def outer_step(i, carry):
        example, first = lax.div(i, rows // 8), pl.multiple_of(lax.rem(i, rows // 8) * 8, 8)
        tiles = [mixed[example, pl.ds(pl.multiple_of(m * rows + first, 8), 8), :] for m in range(outer)]
        step = 1
        while step < outer:
            tiles = [tiles[m ^ step] - tiles[m] if m & step else tiles[m] + tiles[m ^ step] for m in range(outer)]
            step *= 2
        for m in range(outer):
            mixed[example, pl.ds(pl.multiple_of(m * rows + first, 8), 8), :] = tiles[m]
        return carry

    lax.fori_loop(0, examples * (rows // 8), outer_step, 0)

    diagonal = lax.broadcasted_iota(jnp.int32, (LANES, LANES), 0) == lax.broadcasted_iota(jnp.int32, (LANES, LANES), 1)

    def sample_step(i, carry):
        for s in range(LANES):
            row = rows_ref[i * LANES + s]
            for example in range(examples):
                stage[example, pl.ds(s, 1), :] = mixed[example, pl.ds(row, 1), :]
        pattern = pattern_ref[pl.ds(pl.multiple_of(i * LANES, LANES), LANES), :].astype(jnp.float32)
        for example in range(examples):
            terms = jnp.concatenate(halves(stage[example] * pattern), axis=1)
            total = jnp.dot(terms, ones_ref[...], preferred_element_type=jnp.float32)
            out_ref[example, pl.ds(i, 1), :] = jnp.sum(jnp.where(diagonal, total, 0.0), axis=0, keepdims=True)
        return carry

    lax.fori_loop(0, out_ref.shape[1], sample_step, 0)


def local_samples(grad, sign_bits, sample_index):
    examples, rows, width = grad.shape
    count = sample_index.shape[0]
    local = sample_index % (rows * width)
    row, column = local // width, local % width
    where_row = column // LANES * rows + row
    inner = (column % LANES)[:, None] == jnp.arange(LANES, dtype=jnp.int32)[None]
    small = jnp.asarray(sylvester(LANES), jnp.bfloat16)
    pattern = jnp.dot(inner.astype(jnp.bfloat16), small, preferred_element_type=jnp.float32).astype(jnp.bfloat16)
    table = jnp.asarray(np.concatenate([sylvester(rows)] * 2, axis=1), jnp.bfloat16)
    ones = jnp.ones((2 * LANES, LANES), jnp.bfloat16)
    vmem = pl.BlockSpec(memory_space=pltpu.VMEM)
    out = pl.pallas_call(
        sampled_transform,
        out_shape=jax.ShapeDtypeStruct((examples, count // LANES, LANES), jnp.float32),
        in_specs=[pl.BlockSpec(memory_space=pltpu.SMEM)] + [vmem] * 5,
        out_specs=vmem,
        scratch_shapes=[
            pltpu.VMEM((examples, rows * width // LANES, LANES), jnp.float32),
            pltpu.VMEM((examples, LANES, LANES), jnp.float32),
        ],
        compiler_params=pltpu.CompilerParams(vmem_limit_bytes=40 * 1024 * 1024),
        name="sampled_transform",
    )(where_row, grad, sign_bits, pattern, table, ones)
    return out.reshape(examples, count)


def per_device(activations, out_grad, sign_bits, sample_index):
    count, seq_len, rows = activations.shape
    width = out_grad.shape[2]
    devices = lax.axis_size("param")
    me = lax.axis_index("param")
    gathered = lax.all_gather(out_grad, "param", axis=1, tiled=True)
    grad = jnp.einsum("etr,etd->erd", activations, gathered, preferred_element_type=jnp.float32)
    picked = local_samples(grad, sign_bits, sample_index)
    feature_count = picked.shape[1]
    per = feature_count // devices
    grouped = picked.reshape(count, devices, per).transpose(1, 0, 2)
    terms = lax.all_to_all(grouped, "param", 0, 0, tiled=True)
    table = jnp.asarray(sylvester(devices), jnp.float32)
    column = lax.dynamic_slice_in_dim(table, me, 1, 0)[0]
    scale = 1.0 / (width * float(seq_len) ** 0.5)
    features = jnp.sum(terms * column[:, None, None], axis=0) * scale
    everyone = lax.all_gather(features, "ex", axis=0, tiled=True)
    inner = jnp.dot(features, everyone.T, precision=lax.Precision.HIGHEST)
    gram = jnp.sum(lax.all_gather(inner, "param", axis=0), axis=0) / feature_count
    return (features, gram)


def solution(mesh):
    return jax.shard_map(
        per_device,
        mesh=mesh,
        in_specs=(P("ex", None, "param"), P("ex", "param", None), P("param", None), P()),
        out_specs=(P("ex", "param"), P("ex", None)),
        check_vma=False,
    )
```

time: 525 us -> 239 us (0.46)
  waiting for transfers between devices: 291 us -> 122 us
  local copies, waits for them, and re-layouts: 115 us -> 1.45 us
  Pallas kernels: 0 us -> 25 us
  blocking collectives: 68.6 us -> 52 us
  matrix products: 27 us -> 13.7 us
  starting transfers between devices: 0.08 us -> 9.17 us
  other arithmetic: 7.42 us -> 1.56 us
    unnamed x3 -> x1, waiting for transfers between devices: 180 us -> 0.68 us
    gather x1 -> x0, local copies, waits for them, and re-layouts: 91.2 us -> none  [per_device(): picked = jnp.take(mixed, local_index, axis=1)]
    psum x1 -> x0, blocking collectives: 50.9 us -> none  [per_device(): gram = lax.psum(inner, 'param') / feature_count]
    all_gather x0 -> x1, blocking collectives: none -> 33.9 us  [per_device(): lax.all_gather(inner, 'param', axis=0)]
    pallas_call x0 -> x1, Pallas kernels: none -> 25 us  [local_samples(): pl.pallas_call(sampled_transform, out_shape=jax.ShapeDtypeStruct((example...]
    unnamed x12 -> x9, local copies, waits for them, and re-layouts: 17.6 us -> 0.05 us
    dot_general x4 -> x2, matrix products: 26.9 us -> 13.5 us  [the longest x1 8.32 us: per_device(): jnp.einsum('etr,etd->erd', activations, gathered, preferred_element_type=...]
    all_to_all x0 -> x1, waiting for transfers between devices: none -> 12.4 us  [per_device(): terms = lax.all_to_all(grouped, 'param', 0, 0, tiled=True)]
  transfers between devices with their start and end apart: 2 -> 2, of which waited for: 2 -> 2; matrix products, arithmetic and copies ran while one was open for 1% -> 3% of each run, Pallas kernels for 0% -> 0%
where the time goes in v1:
time: 239 us
  waiting for transfers between devices  122 us (51%)
  blocking collectives  52 us (22%)
  Pallas kernels  25 us (10%)
  between operations  14.1 us (6%)
  matrix products  13.7 us (6%)
  starting transfers between devices  9.17 us (4%)
    all_gather x1, waiting for transfers between devices, per_device(): gathered = lax.all_gather(out_grad, 'param', axis=1, tiled=True)  109 us
    all_gather x1, blocking collectives, per_device(): lax.all_gather(inner, 'param', axis=0)  33.9 us
    pallas_call x1, Pallas kernels, local_samples(): pl.pallas_call(sampled_transform, out_shape=jax.ShapeDtypeStruct((example...  25 us
    all_gather x1, blocking collectives, per_device(): everyone = lax.all_gather(features, 'ex', axis=0, tiled=True)  18.1 us
    all_to_all x1, waiting for transfers between devices, per_device(): terms = lax.all_to_all(grouped, 'param', 0, 0, tiled=True)  12.4 us
    all_to_all x1, starting transfers between devices, per_device(): terms = lax.all_to_all(grouped, 'param', 0, 0, tiled=True)  9.13 us
    dot_general x1, matrix products, per_device(): jnp.einsum('etr,etd->erd', activations, gathered, preferred_element_type=...  8.32 us
    dot_general x1, matrix products, local_samples(): jnp.dot(inner.astype(jnp.bfloat16), small, preferred_element_type=jnp.flo...  5.23 us
  transfers between devices with their start and end apart: 2, of which 2 were waited for; matrix products, arithmetic and copies ran while one was open for 3% of the time, Pallas kernels for 0%

profile of v1, /device:TPU:1, one launch (start us, length us, event | category | flops | bytes accessed | tf_op | source)
XLA Modules:
  0.0 238.8 jit_solution(10073955043375318384)
XLA Ops:
  7.2 0.0 copy-start
  7.2 0.0 all-gather.5.cloned.1.call-start
  7.2 0.7 all-gather.5.cloned.1.call-update
  7.9 0.8 add_select_fusion
  8.8 5.2 %convolution_convert_fusion.pattern_ref = bf16[8192,128]{1,0:T(8,128)(2,1)S(1)} fusion(bf16[128,128]{1,0:T(8,128)(2,1)} %constant.84.clone, s32[8192]{0:T(1024)S(1)} %get-tuple-element.2), kind=kOutput, calls=%fused_computation | convolution fusion | flops 270532608 | bytes 2162688 | tf_op jit(solution)/shard_map/dot_general | solution.py:83
  14.0 0.0 copy-start.2
  14.0 108.7 %all-gather.5.cloned.1.call-done = bf16[2,1024,4096]{2,1,0:T(8,128)(2,1)} async-done(((bf16[2,32,4096]{2,1,0:T(8,128)(2,1)}), bf16[2,1024,4096]{2,1,0:T(8,128)(2,1)}) %all-gather.5.cloned.1.call-update) | async-done | bytes 16777232 | tf_op jit(solution)/shard_map/all_gather | solution.py:107
  122.7 0.0 copy-done
  122.7 0.0 copy-start.1
  122.7 8.3 %fusion.6.grad_ref = f32[2,128,4096]{2,1,0:T(8,128)S(1)} fusion(bf16[2,1024,128]{2,1,0:T(8,128)(2,1)S(1)} %copy-done, bf16[2,1024,4096]{2,1,0:T(8,128)(2,1)} %all-gather.5.cloned.1.call-done), kind=kOutput, calls=%fused_computation.30 | convolution fusion | flops 2147483648 | bytes 21495808 | tf_op jit(solution)/shard_map/etr,etd->erd/dot_general | solution.py:108
  131.1 0.0 copy-done.2
  131.1 0.0 copy-done.1
  131.1 25.0 %sampled_transform.1 = f32[2,64,128]{2,1,0:T(8,128)S(1)} custom-call(s32[8192]{0:T(1024)S(1)} %get-tuple-element.3.rows_ref, f32[2,128,4096]{2,1,0:T(8,128)S(1)} %fusion.6.grad_ref, s32[128,4096]{1,0:T(8,128)S(1)} %copy-done.1, bf16[8192,128]{1,0:T(8,128)(2,1)S(1)} %convolution_convert_fusion.pattern_ref, bf16[128,256]{1,0:T(8,128)(2,1)S(1)} %copy-done.2, ...), custom_call_target="tpu_custom_call" | custom-call | tf_op jit(solution)/shard_map/sampled_transform/pallas_call | solution.py:87
  156.1 0.7 copy.14
  156.8 9.1 %all-to-all-start = ((f32[32,2,256]{2,1,0:T(2,128)}), f32[32,2,256]{2,1,0:T(2,128)S(1)}, u32[]{:S(2)}, u32[]{:S(2)}) async-start(f32[32,2,256]{2,1,0:T(2,128)} %bitcast.13), calls=%async_computation | async-start | bytes 131072 | tf_op jit(solution)/shard_map/all_to_all | solution.py:113
  165.9 0.7 dynamic-slice_bitcast_fusion
  166.6 12.4 %all-to-all-done = f32[32,2,256]{2,1,0:T(2,128)S(1)} async-done(((f32[32,2,256]{2,1,0:T(2,128)}), f32[32,2,256]{2,1,0:T(2,128)S(1)}, u32[]{:S(2)}, u32[]{:S(2)}) %all-to-all-start) | async-done | bytes 65568 | tf_op jit(solution)/shard_map/all_to_all | solution.py:113
  179.0 0.1 multiply_reduce_fusion
  179.1 0.0 copy-start.3
  179.1 18.1 %all-gather.1 = f32[16,2,256]{2,1,0:T(2,128)S(1)} all-gather(f32[1,2,256]{2,1,0:T(2,128)S(1)} %fusion.12), channel_id=1, replica_groups=mesh['param'=32,'ex'=16] {'ex'}, dimensions={0}, use_global_device_ids=true | all-gather | bytes 34816 | tf_op jit(solution)/shard_map/all_gather | solution.py:118
  197.2 0.1 convolution_bitcast_fusion
  197.4 33.9 %all-gather.2 = f32[32,2,32]{2,1,0:T(2,128)S(1)} all-gather(f32[1,2,32]{2,1,0:T(2,128)S(1)} %convolution_bitcast_fusion), channel_id=2, replica_groups=mesh['param'=32,'ex'=16] {'param'}, dimensions={0}, use_global_device_ids=true | all-gather | bytes 8448 | tf_op jit(solution)/shard_map/all_gather | solution.py:120
  231.4 0.6 broadcast_multiply_fusion.1
  231.9 0.0 copy-done.3
  (6 shorter events, 0.1 us)
Async XLA Ops:
  7.2 115.5 %copy-start = (bf16[2,1024,128]{2,1,0:T(8,128)(2,1)S(1)}, bf16[2,1024,128]{2,1,0:T(8,128)(2,1)}, u32[]{:S(2)}) copy-start(bf16[2,1024,128]{2,1,0:T(8,128)(2,1)} %param.7) | copy-start | bytes 1572868
  7.2 115.5 %all-gather.5.cloned.1.call-start = ((), (), s32[]{:S(2)}) async-start(), calls=%async_computation.1 | async-start | bytes 17301504 | tf_op jit(solution)/shard_map/all_gather | solution.py:107
  14.0 117.1 %copy-start.2 = (bf16[128,256]{1,0:T(8,128)(2,1)S(1)}, bf16[128,256]{1,0:T(8,128)(2,1)}, u32[]{:S(2)}) copy-start(bf16[128,256]{1,0:T(8,128)(2,1)} %constant.85.clone.table_ref) | copy-start | bytes 196612
  122.7 8.4 %copy-start.1 = (s32[128,4096]{1,0:T(8,128)S(1)}, s32[128,4096]{1,0:T(8,128)}, u32[]{:S(2)}) copy-start(s32[128,4096]{1,0:T(8,128)} %bits_ref.1) | copy-start | bytes 6291460
  156.8 22.2 %all-to-all-start = ((f32[32,2,256]{2,1,0:T(2,128)}), f32[32,2,256]{2,1,0:T(2,128)S(1)}, u32[]{:S(2)}, u32[]{:S(2)}) async-start(f32[32,2,256]{2,1,0:T(2,128)} %bitcast.13), calls=%async_computation | async-start | bytes 131072 | tf_op jit(solution)/shard_map/all_to_all | solution.py:113
  179.1 52.8 %copy-start.3 = (f32[2,256]{1,0:T(2,128)}, f32[2,256]{1,0:T(2,128)S(1)}, u32[]{:S(2)}) copy-start(f32[2,256]{1,0:T(2,128)S(1)} %broadcast_multiply_fusion) | copy-start | bytes 6148
Sparse Core Ops, SparseCore 0:
  10.2 112.4 all-gather.4

commit v2 on v0

v2 whole, which is shorter than its diff:
```python
import jax
import jax.numpy as jnp
import numpy as np
from jax import lax
from jax.experimental import pallas as pl
from jax.experimental.pallas import tpu as pltpu
from jax.sharding import Mesh, PartitionSpec as P

LANES = 128
WIDE = 512


def sylvester(order):
    table = np.ones((1, 1), np.float32)
    base = np.array([[1.0, 1.0], [1.0, -1.0]], np.float32)
    while table.shape[0] < order:
        table = np.kron(table, base)
    return table


def halves(value):
    high = value.astype(jnp.bfloat16)
    low = (value - high.astype(jnp.float32)).astype(jnp.bfloat16)
    return high, low


def sampled_gradient(rows_ref, act_ref, grd_ref, near_ref, far_ref, pattern_ref, table_ref, ones_ref, out_ref, mixed, stage):
    rows = act_ref.shape[0]
    outer = mixed.shape[0] // rows
    piece = pl.program_id(0)

    value = jnp.dot(act_ref[...], grd_ref[...], preferred_element_type=jnp.float32)
    near, far = value[: rows // 2], value[rows // 2:]
    near = jnp.where(near_ref[...] == 1, near, -near)
    far = jnp.where(far_ref[...] == 1, far, -far)
    parts = [part for half in zip(halves(near), halves(far)) for part in half]
    out = jnp.dot(table_ref[...], jnp.concatenate(parts, axis=0), preferred_element_type=jnp.float32)
    for t in range(WIDE // LANES):
        first = pl.multiple_of((piece * (WIDE // LANES) + t) * rows, rows)
        mixed[pl.ds(first, rows), :] = out[:, t * LANES:(t + 1) * LANES]

    @pl.when(piece == pl.num_programs(0) - 1)
    def _():
        def outer_step(i, carry):
            first = pl.multiple_of(i * 8, 8)
            tiles = [mixed[pl.ds(pl.multiple_of(m * rows + first, 8), 8), :] for m in range(outer)]
            step = 1
            while step < outer:
                tiles = [tiles[m ^ step] - tiles[m] if m & step else tiles[m] + tiles[m ^ step] for m in range(outer)]
                step *= 2
            for m in range(outer):
                mixed[pl.ds(pl.multiple_of(m * rows + first, 8), 8), :] = tiles[m]
            return carry

        lax.fori_loop(0, rows // 8, outer_step, 0)

        diagonal = lax.broadcasted_iota(jnp.int32, (LANES, LANES), 0) == lax.broadcasted_iota(jnp.int32, (LANES, LANES), 1)

        def sample_step(i, carry):
            for s in range(LANES):
                stage[pl.ds(s, 1), :] = mixed[pl.ds(rows_ref[i * LANES + s], 1), :]
            pattern = pattern_ref[pl.ds(pl.multiple_of(i * LANES, LANES), LANES), :].astype(jnp.float32)
            terms = jnp.concatenate(halves(stage[...] * pattern), axis=1)
            total = jnp.dot(terms, ones_ref[...], preferred_element_type=jnp.float32)
            out_ref[pl.ds(i, 1), :] = jnp.sum(jnp.where(diagonal, total, 0.0), axis=0, keepdims=True)
            return carry

        lax.fori_loop(0, out_ref.shape[0], sample_step, 0)


def local_samples(act, grd, near, far, core, sample_index):
    rows, tokens = act.shape
    width = grd.shape[1]
    count = sample_index.shape[0]
    local = sample_index % (rows * width)
    row, column = local // width, local % width
    where_row = column // LANES * rows + row
    inner = (column % LANES)[:, None] == jnp.arange(LANES, dtype=jnp.int32)[None]
    small = jnp.asarray(sylvester(LANES), jnp.bfloat16)
    pattern = jnp.dot(inner.astype(jnp.bfloat16), small, preferred_element_type=jnp.float32).astype(jnp.bfloat16)
    full = sylvester(rows)
    left, right = full[:, : rows // 2], full[:, rows // 2:]
    tables = np.stack([np.concatenate(pair, axis=1) for pair in ((left, right, left, right), (right, left, right, left))])
    table = lax.dynamic_index_in_dim(jnp.asarray(tables, jnp.bfloat16), core, 0, keepdims=False)
    ones = jnp.ones((2 * LANES, LANES), jnp.bfloat16)
    whole = lambda *shape: pl.BlockSpec(shape, lambda i: (0,) * len(shape))
    columns = lambda depth: pl.BlockSpec((depth, WIDE), lambda i: (0, i))
    out = pl.pallas_call(
        sampled_gradient,
        grid=(width // WIDE,),
        out_shape=jax.ShapeDtypeStruct((count // LANES, LANES), jnp.float32),
        in_specs=[
            pl.BlockSpec(memory_space=pltpu.SMEM),
            whole(rows, tokens),
            columns(tokens),
            columns(rows // 2),
            columns(rows // 2),
            whole(count, LANES),
            whole(rows, 2 * rows),
            whole(2 * LANES, LANES),
        ],
        out_specs=whole(count // LANES, LANES),
        scratch_shapes=[
            pltpu.VMEM((rows * width // LANES, LANES), jnp.float32),
            pltpu.VMEM((LANES, LANES), jnp.float32),
        ],
        compiler_params=pltpu.CompilerParams(vmem_limit_bytes=40 * 1024 * 1024),
        name="sampled_gradient",
    )(where_row, act, grd, near, far, pattern, table, ones)
    return out


def to_all(value, axes):
    size = lax.axis_size(axes)
    return lax.all_to_all(jnp.broadcast_to(value[None], (size,) + value.shape), axes, 0, 0, tiled=True)


def per_device(activations, out_grad, sign_bits, sample_index):
    count, seq_len, columns = activations.shape
    width = out_grad.shape[2]
    chips = lax.axis_size("z")
    here, core = lax.axis_index("z"), lax.axis_index("core")
    swap = [(0, 1), (1, 0)]

    mine = lambda pair: lax.dynamic_index_in_dim(pair, core, 0, keepdims=False)
    other = lambda pair: lax.ppermute(lax.dynamic_index_in_dim(pair, 1 - core, 0, keepdims=False), "core", swap)
    block = jnp.concatenate([mine(out_grad), other(out_grad)], axis=0)
    gathered = lax.all_gather(block, "z", axis=0, tiled=True)
    far = lax.ppermute(sign_bits, "core", swap)
    act = jnp.concatenate([mine(activations), other(activations)], axis=1).T
    act = act.reshape(2 * columns, chips, 2, seq_len // (2 * chips))
    act = jnp.where(core == 0, act, act[:, :, ::-1]).reshape(2 * columns, seq_len)

    terms = local_samples(act, gathered, sign_bits, far, core, sample_index)
    feature_count = sample_index.shape[0]
    per = feature_count // (2 * chips)
    terms = lax.all_to_all(terms.reshape(2 * chips, per), ("z", "core"), 0, 0, tiled=True)
    signs = lax.dynamic_index_in_dim(jnp.asarray(sylvester(chips), jnp.float32), here, 0, keepdims=False)
    scale = 1.0 / (width * float(seq_len) ** 0.5)
    features = jnp.sum(terms.reshape(chips, 2, per) * signs[:, None, None], axis=0) * scale
    everyone = to_all(features, "ex").reshape(-1, per)
    inner = jnp.dot(features, everyone.T, precision=lax.Precision.HIGHEST)
    gram = jnp.sum(to_all(inner, ("z", "core")), axis=0) / feature_count
    return (features, gram)


def solution(mesh):
    params, groups = mesh.devices.shape
    chips = Mesh(mesh.devices.reshape(params // 2, 2, groups), ("z", "core", "ex"))
    param = ("z", "core")
    return jax.shard_map(
        per_device,
        mesh=chips,
        in_specs=(P("ex", None, param), P("ex", param, None), P(param, None), P()),
        out_specs=(P("ex", param), P("ex", None)),
        check_vma=False,
    )
```

time: 525 us -> 214 us (0.41)
  waiting for transfers between devices: 291 us -> 106 us
  local copies, waits for them, and re-layouts: 115 us -> 5.72 us
  blocking collectives: 68.6 us -> 30.3 us
  Pallas kernels: 0 us -> 27.9 us
  starting transfers between devices: 0.08 us -> 22.7 us
  matrix products: 27 us -> 4.59 us
  other arithmetic: 7.42 us -> 1.93 us
    unnamed x3 -> x1, waiting for transfers between devices: 180 us -> 0.02 us
    gather x1 -> x0, local copies, waits for them, and re-layouts: 91.2 us -> none  [per_device(): picked = jnp.take(mixed, local_index, axis=1)]
    psum x1 -> x0, blocking collectives: 50.9 us -> none  [per_device(): gram = lax.psum(inner, 'param') / feature_count]
    all_to_all x0 -> x2, blocking collectives: none -> 30.3 us  [to_all(): lax.all_to_all(jnp.broadcast_to(value[None], (size,) + value.shape), axes...]
    pallas_call x0 -> x1, Pallas kernels: none -> 27.9 us  [local_samples(): pl.pallas_call(sampled_gradient, grid=(width // WIDE,), out_shape=jax.Sha...]
    dot_general x4 -> x1, matrix products: 26.9 us -> 4.47 us  [local_samples(): jnp.dot(inner.astype(jnp.bfloat16), small, preferred_element_type=jnp.flo...]
    all_gather x1 -> x0, blocking collectives: 17.7 us -> none  [per_device(): everyone = lax.all_gather(features, 'ex', axis=0, tiled=True)]
    all_gather x1, waiting for transfers between devices: 110 us -> 93.5 us  [per_device(): gathered = lax.all_gather(block, 'z', axis=0, tiled=True)]
  transfers between devices with their start and end apart: 2 -> 5, of which waited for: 2 -> 3; matrix products, arithmetic and copies ran while one was open for 1% -> 4% of each run, Pallas kernels for 0% -> 0%
where the time goes in v2:
time: 214 us; the launch traced here: 213 us
  waiting for transfers between devices  106 us (50%)
  blocking collectives  30.3 us (14%)
  Pallas kernels  27.9 us (13%)
  starting transfers between devices  22.7 us (11%)
  between operations  14.2 us (7%)
  local copies, waits for them, and re-layouts  5.72 us (3%)
  matrix products  4.59 us (2%)
    all_gather x1, waiting for transfers between devices, per_device(): gathered = lax.all_gather(block, 'z', axis=0, tiled=True)  93.5 us
    all_to_all x2, blocking collectives, to_all(): lax.all_to_all(jnp.broadcast_to(value[None], (size,) + value.shape), axes...  30.3 us
    pallas_call x1, Pallas kernels, local_samples(): pl.pallas_call(sampled_gradient, grid=(width // WIDE,), out_shape=jax.Sha...  27.9 us
    all_to_all x1, waiting for transfers between devices, per_device(): lax.all_to_all(terms.reshape(2 * chips, per), ('z', 'core'), 0, 0, tiled=...  11.3 us
    ppermute x2, starting transfers between devices, per_device(): lax.ppermute(lax.dynamic_index_in_dim(pair, 1 - core, 0, keepdims=False),...  10.8 us
    all_to_all x1, starting transfers between devices, per_device(): lax.all_to_all(terms.reshape(2 * chips, per), ('z', 'core'), 0, 0, tiled=...  9.59 us
    dot_general x1, matrix products, local_samples(): jnp.dot(inner.astype(jnp.bfloat16), small, preferred_element_type=jnp.flo...  4.47 us
  transfers between devices with their start and end apart: 5, of which 3 were waited for; matrix products, arithmetic and copies ran while one was open for 4% of the time, Pallas kernels for 0%

profile of v2, /device:TPU:1, one launch (start us, length us, event | category | flops | bytes accessed | tf_op | source)
XLA Modules:
  0.0 213.3 jit_solution(14823279768825376979)
XLA Ops:
  7.2 0.0 copy-start.1
  7.2 0.0 all-gather.2.cloned.1.call-start
  7.2 1.1 dynamic-slice_bitcast_fusion.2
  8.3 8.8 %collective-permute-start.1 = (bf16[32,4096]{1,0:T(8,128)(2,1)S(1)}, bf16[32,4096]{1,0:T(8,128)(2,1)S(1)}, u32[]{:S(2)}, u32[]{:S(2)}) collective-permute-start(bf16[32,4096]{1,0:T(8,128)(2,1)S(1)} %get-tuple-element.3), channel_id=1, source_target_pairs={{0,16},{16,0},{1,17},{17,1},{2,18},{18,2},{3,19},{19,3},{4,20},{20... | collective-permute-start | bytes 786440 | tf_op jit(solution)/shard_map/ppermute | solution.py:126
  17.1 1.1 collective-permute-done.1
  18.2 0.9 pad_maximum_fusion.1
  19.1 0.0 all-gather.2.cloned.1.call-update
  19.1 2.3 %collective-permute-start.2 = (s32[128,4096]{1,0:T(8,128)}, s32[128,4096]{1,0:T(8,128)}, u32[]{:S(2)}, u32[]{:S(2)}) collective-permute-start(s32[128,4096]{1,0:T(8,128)} %near_ref.1), channel_id=1, source_target_pairs={{0,16},{16,0},{1,17},{17,1},{2,18},{18,2},{3,19},{19,3},{4,20},{20... | collective-permute-start | bytes 6291464 | tf_op jit(solution)/shard_map/ppermute | solution.py:129
  21.4 1.1 dynamic-slice_bitcast_fusion.4
  22.5 2.0 collective-permute-start
  24.6 1.0 dynamic-slice_bitcast_fusion.table_ref
  25.5 0.1 add_select_fusion
  25.6 4.5 %convolution_convert_fusion.pattern_ref = bf16[8192,128]{1,0:T(8,128)(2,1)S(1)} fusion(bf16[128,128]{1,0:T(8,128)(2,1)S(1)} %copy-done.1, s32[8192]{0:T(1024)S(1)} %get-tuple-element.6), kind=kOutput, calls=%fused_computation | convolution fusion | flops 270532608 | bytes 2162688 | tf_op jit(solution)/shard_map/dot_general | solution.py:80
  30.1 0.0 collective-permute-done
  30.1 0.1 pad_maximum_fusion
  30.2 0.1 reverse_select_fusion
  30.3 0.2 copy.14.act_ref
  30.6 0.0 collective-permute-done.2.far_ref
  30.6 93.5 %all-gather.2.cloned.1.call-done.grd_ref = bf16[1024,4096]{1,0:T(8,128)(2,1)} async-done(((bf16[64,4096]{1,0:T(8,128)(2,1)}), bf16[1024,4096]{1,0:T(8,128)(2,1)}) %all-gather.2.cloned.1.call-update) | async-done | bytes 8388624 | tf_op jit(solution)/shard_map/all_gather | solution.py:128
  124.0 0.0 copy-start
  124.1 1.6 copy-done
  125.6 27.9 %sampled_gradient.1 = f32[64,128]{1,0:T(8,128)} custom-call(s32[8192]{0:T(1024)S(1)} %get-tuple-element.7.rows_ref, bf16[256,1024]{1,0:T(8,128)(2,1)S(1)} %copy.14.act_ref, bf16[1024,4096]{1,0:T(8,128)(2,1)} %all-gather.2.cloned.1.call-done.grd_ref, s32[128,4096]{1,0:T(8,128)S(1)} %copy-done, s32[128,4096]{1,0:T(8,128)} %collective-permute-done.2.far_ref, ...), custom_call_target="tpu_custom_call" | custom-call | tf_op jit(solution)/shard_map/sampled_gradient/pallas_call | solution.py:88
  153.5 9.6 %all-to-all-start = ((f32[32,1,256]{2,1,0:T(1,128)}), f32[32,1,256]{2,1,0:T(1,128)S(1)}, u32[]{:S(2)}, u32[]{:S(2)}) async-start(f32[32,1,256]{2,1,0:T(1,128)} %bitcast.9), calls=%async_computation | async-start | bytes 65536 | tf_op jit(solution)/shard_map/all_to_all | solution.py:137
  163.1 0.7 fusion.6
  163.8 11.3 %all-to-all-done = f32[32,1,256]{2,1,0:T(1,128)S(1)} async-done(((f32[32,1,256]{2,1,0:T(1,128)}), f32[32,1,256]{2,1,0:T(1,128)S(1)}, u32[]{:S(2)}, u32[]{:S(2)}) %all-to-all-start) | async-done | bytes 32800 | tf_op jit(solution)/shard_map/all_to_all | solution.py:137
  175.1 0.1 reduce
  175.3 0.1 multiply_reduce_fusion
  175.4 0.0 copy-start.3
  175.4 12.8 %all_to_all.19 = f32[16,2,256]{2,1,0:T(2,128)S(1)} all-to-all(f32[16,2,256]{2,1,0:T(2,128)S(1)} %broadcast_in_dim.7), channel_id=1, replica_groups=mesh['z'=16,'core'=2,'ex'=16] {'ex'}, dimensions={0} | all-to-all | bytes 65536 | tf_op jit(solution)/shard_map/all_to_all | solution.py:115
  188.2 0.1 fusion.7
  188.4 17.5 %all_to_all.20 = f32[32,2,32]{2,1,0:T(2,128)S(1)} all-to-all(f32[32,2,32]{2,1,0:T(2,128)S(1)} %broadcast_in_dim.8), channel_id=1, replica_groups=mesh['z'=16,'core'=2,'ex'=16] {'z','core'}, dimensions={0} | all-to-all | bytes 16384 | tf_op jit(solution)/shard_map/all_to_all | solution.py:115
  205.9 0.6 broadcast_multiply_fusion.1
  (11 shorter events, 0.1 us)
Async XLA Ops:
  7.2 18.5 %copy-start.1 = (bf16[128,128]{1,0:T(8,128)(2,1)S(1)}, bf16[128,128]{1,0:T(8,128)(2,1)}, u32[]{:S(2)}) copy-start(bf16[128,128]{1,0:T(8,128)(2,1)} %constant.113.clone) | copy-start | bytes 98308
  7.2 18.4 %copy-start.2 = (s32[8192]{0:T(1024)S(1)}, s32[8192]{0:T(1024)}, u32[]{:S(2)}) copy-start(s32[8192]{0:T(1024)} %param.10) | copy-start | bytes 98308
  7.2 116.8 %all-gather.2.cloned.1.call-start = ((), (), s32[]{:S(2)}) async-start(), calls=%async_computation.3 | async-start | bytes 8912896 | tf_op jit(solution)/shard_map/all_gather | solution.py:128
  8.3 9.9 %collective-permute-start.1 = (bf16[32,4096]{1,0:T(8,128)(2,1)S(1)}, bf16[32,4096]{1,0:T(8,128)(2,1)S(1)}, u32[]{:S(2)}, u32[]{:S(2)}) collective-permute-start(bf16[32,4096]{1,0:T(8,128)(2,1)S(1)} %get-tuple-element.3), channel_id=1, source_target_pairs={{0,16},{16,0},{1,17},{17,1},{2,18},{18,2},{3,19},{19,3},{4,20},{20... | collective-permute-start | bytes 786440 | tf_op jit(solution)/shard_map/ppermute | solution.py:126
  19.1 11.4 %collective-permute-start.2 = (s32[128,4096]{1,0:T(8,128)}, s32[128,4096]{1,0:T(8,128)}, u32[]{:S(2)}, u32[]{:S(2)}) collective-permute-start(s32[128,4096]{1,0:T(8,128)} %near_ref.1), channel_id=1, source_target_pairs={{0,16},{16,0},{1,17},{17,1},{2,18},{18,2},{3,19},{19,3},{4,20},{20... | collective-permute-start | bytes 6291464 | tf_op jit(solution)/shard_map/ppermute | solution.py:129
  22.5 7.6 %collective-permute-start = (bf16[1024,128]{1,0:T(8,128)(2,1)S(1)}, bf16[1024,128]{1,0:T(8,128)(2,1)S(1)}, u32[]{:S(2)}, u32[]{:S(2)}) collective-permute-start(bf16[1024,128]{1,0:T(8,128)(2,1)S(1)} %get-tuple-element.5), channel_id=1, source_target_pairs={{0,16},{16,0},{1,17},{17,1},{2,18},{18,2},{3,19},{19,3},{4,20},{20... | collective-permute-start | bytes 786440 | tf_op jit(solution)/shard_map/ppermute | solution.py:126
  124.0 1.6 copy-start
  153.5 21.6 %all-to-all-start = ((f32[32,1,256]{2,1,0:T(1,128)}), f32[32,1,256]{2,1,0:T(1,128)S(1)}, u32[]{:S(2)}, u32[]{:S(2)}) async-start(f32[32,1,256]{2,1,0:T(1,128)} %bitcast.9), calls=%async_computation | async-start | bytes 65536 | tf_op jit(solution)/shard_map/all_to_all | solution.py:137
  175.4 31.1 %copy-start.3 = (f32[2,256]{1,0:T(2,128)}, f32[2,256]{1,0:T(2,128)S(1)}, u32[]{:S(2)}) copy-start(f32[2,256]{1,0:T(2,128)S(1)} %broadcast_multiply_fusion) | copy-start | bytes 6148
Sparse Core Ops, SparseCore 0:
  19.3 104.7 all-gather.1

commit v3 on v2

--- a/solution.py
+++ b/solution.py
@@ -7,7 +7,8 @@
 from jax.sharding import Mesh, PartitionSpec as P
 
 LANES = 128
-WIDE = 512
+WIDE = 1024
+BATCH = 1024
 
 
 def sylvester(order):
@@ -31,8 +32,9 @@
 
     value = jnp.dot(act_ref[...], grd_ref[...], preferred_element_type=jnp.float32)
     near, far = value[: rows // 2], value[rows // 2:]
-    near = jnp.where(near_ref[...] == 1, near, -near)
-    far = jnp.where(far_ref[...] == 1, far, -far)
+    columns = pl.ds(pl.multiple_of(piece * WIDE, WIDE), WIDE)
+    near = jnp.where(near_ref[:, columns] == 1, near, -near)
+    far = jnp.where(far_ref[:, columns] == 1, far, -far)
     parts = [part for half in zip(halves(near), halves(far)) for part in half]
     out = jnp.dot(table_ref[...], jnp.concatenate(parts, axis=0), preferred_element_type=jnp.float32)
     for t in range(WIDE // LANES):
@@ -56,16 +58,23 @@
 
         diagonal = lax.broadcasted_iota(jnp.int32, (LANES, LANES), 0) == lax.broadcasted_iota(jnp.int32, (LANES, LANES), 1)
 
-        def sample_step(i, carry):
+        def load_step(i, carry):
+            first = pl.multiple_of(i * LANES, LANES)
             for s in range(LANES):
-                stage[pl.ds(s, 1), :] = mixed[pl.ds(rows_ref[i * LANES + s], 1), :]
-            pattern = pattern_ref[pl.ds(pl.multiple_of(i * LANES, LANES), LANES), :].astype(jnp.float32)
-            terms = jnp.concatenate(halves(stage[...] * pattern), axis=1)
-            total = jnp.dot(terms, ones_ref[...], preferred_element_type=jnp.float32)
-            out_ref[pl.ds(i, 1), :] = jnp.sum(jnp.where(diagonal, total, 0.0), axis=0, keepdims=True)
+                stage[pl.ds(first + s, 1), :] = mixed[pl.ds(rows_ref[first + s], 1), :]
             return carry
 
-        lax.fori_loop(0, out_ref.shape[0], sample_step, 0)
+        lax.fori_loop(0, stage.shape[0] // LANES, load_step, 0)
+
+        def inner_step(i, carry):
+            batch = pl.ds(pl.multiple_of(i * BATCH, BATCH), BATCH)
+            terms = jnp.concatenate(halves(stage[batch, :] * pattern_ref[batch, :].astype(jnp.float32)), axis=1)
+            total = jnp.dot(terms, ones_ref[...], preferred_element_type=jnp.float32)
+            lines = [jnp.sum(jnp.where(diagonal, total[g * LANES:(g + 1) * LANES], 0.0), axis=0, keepdims=True) for g in range(BATCH // LANES)]
+            out_ref[pl.ds(pl.multiple_of(i * (BATCH // LANES), BATCH // LANES), BATCH // LANES), :] = jnp.concatenate(lines, axis=0)
+            return carry
+
+        lax.fori_loop(0, stage.shape[0] // BATCH, inner_step, 0)
 
 
 def local_samples(act, grd, near, far, core, sample_index):
@@ -83,26 +92,25 @@
     tables = np.stack([np.concatenate(pair, axis=1) for pair in ((left, right, left, right), (right, left, right, left))])
     table = lax.dynamic_index_in_dim(jnp.asarray(tables, jnp.bfloat16), core, 0, keepdims=False)
     ones = jnp.ones((2 * LANES, LANES), jnp.bfloat16)
-    whole = lambda *shape: pl.BlockSpec(shape, lambda i: (0,) * len(shape))
-    columns = lambda depth: pl.BlockSpec((depth, WIDE), lambda i: (0, i))
+    vmem = pl.BlockSpec(memory_space=pltpu.VMEM)
     out = pl.pallas_call(
         sampled_gradient,
         grid=(width // WIDE,),
         out_shape=jax.ShapeDtypeStruct((count // LANES, LANES), jnp.float32),
         in_specs=[
             pl.BlockSpec(memory_space=pltpu.SMEM),
-            whole(rows, tokens),
-            columns(tokens),
-            columns(rows // 2),
-            columns(rows // 2),
-            whole(count, LANES),
-            whole(rows, 2 * rows),
-            whole(2 * LANES, LANES),
+            vmem,
+            pl.BlockSpec((tokens, WIDE), lambda i: (0, i)),
+            vmem,
+            vmem,
+            vmem,
+            vmem,
+            vmem,
         ],
-        out_specs=whole(count // LANES, LANES),
+        out_specs=pl.BlockSpec((count // LANES, LANES), lambda i: (0, 0)),
         scratch_shapes=[
             pltpu.VMEM((rows * width // LANES, LANES), jnp.float32),
-            pltpu.VMEM((LANES, LANES), jnp.float32),
+            pltpu.VMEM((count, LANES), jnp.float32),
         ],
         compiler_params=pltpu.CompilerParams(vmem_limit_bytes=40 * 1024 * 1024),
         name="sampled_gradient",

time: 214 us -> 204 us (0.953)
  Pallas kernels: 27.9 us -> 18.2 us
    pallas_call x1, Pallas kernels: 27.9 us -> 18.2 us  [local_samples(): pl.pallas_call(sampled_gradient, grid=(width // WIDE,), out_shape=jax.Sha...]
where the time goes in v3:
time: 204 us
  waiting for transfers between devices  106 us (52%)
  blocking collectives  30.3 us (15%)
  starting transfers between devices  22.7 us (11%)
  Pallas kernels  18.2 us (9%)
  between operations  14.2 us (7%)
  local copies, waits for them, and re-layouts  5.72 us (3%)
  matrix products  4.59 us (2%)
    all_gather x1, waiting for transfers between devices, per_device(): gathered = lax.all_gather(block, 'z', axis=0, tiled=True)  93.5 us
    all_to_all x2, blocking collectives, to_all(): lax.all_to_all(jnp.broadcast_to(value[None], (size,) + value.shape), axes...  30.3 us
    pallas_call x1, Pallas kernels, local_samples(): pl.pallas_call(sampled_gradient, grid=(width // WIDE,), out_shape=jax.Sha...  18.2 us
    all_to_all x1, waiting for transfers between devices, per_device(): lax.all_to_all(terms.reshape(2 * chips, per), ('z', 'core'), 0, 0, tiled=...  11.3 us
    ppermute x2, starting transfers between devices, per_device(): lax.ppermute(lax.dynamic_index_in_dim(pair, 1 - core, 0, keepdims=False),...  10.8 us
    all_to_all x1, starting transfers between devices, per_device(): lax.all_to_all(terms.reshape(2 * chips, per), ('z', 'core'), 0, 0, tiled=...  9.58 us
    dot_general x1, matrix products, local_samples(): jnp.dot(inner.astype(jnp.bfloat16), small, preferred_element_type=jnp.flo...  4.47 us
  transfers between devices with their start and end apart: 5, of which 3 were waited for; matrix products, arithmetic and copies ran while one was open for 4% of the time, Pallas kernels for 0%

profile of v3, /device:TPU:1, one launch (start us, length us, event | category | flops | bytes accessed | tf_op | source)
XLA Modules:
  0.0 203.7 jit_solution(18127578021965401332)
XLA Ops:
  7.2 0.0 copy-start.1
  7.2 0.0 all-gather.2.cloned.1.call-start
  7.2 1.1 dynamic-slice_bitcast_fusion.2
  8.3 8.8 %collective-permute-start.1 = (bf16[32,4096]{1,0:T(8,128)(2,1)S(1)}, bf16[32,4096]{1,0:T(8,128)(2,1)S(1)}, u32[]{:S(2)}, u32[]{:S(2)}) collective-permute-start(bf16[32,4096]{1,0:T(8,128)(2,1)S(1)} %get-tuple-element.3), channel_id=1, source_target_pairs={{0,16},{16,0},{1,17},{17,1},{2,18},{18,2},{3,19},{19,3},{4,20},{20... | collective-permute-start | bytes 786440 | tf_op jit(solution)/shard_map/ppermute | solution.py:134
  17.1 1.1 collective-permute-done.1
  18.2 0.9 pad_maximum_fusion.1
  19.1 0.0 all-gather.2.cloned.1.call-update
  19.1 2.3 %collective-permute-start.2 = (s32[128,4096]{1,0:T(8,128)}, s32[128,4096]{1,0:T(8,128)}, u32[]{:S(2)}, u32[]{:S(2)}) collective-permute-start(s32[128,4096]{1,0:T(8,128)} %near_ref.1), channel_id=1, source_target_pairs={{0,16},{16,0},{1,17},{17,1},{2,18},{18,2},{3,19},{19,3},{4,20},{20... | collective-permute-start | bytes 6291464 | tf_op jit(solution)/shard_map/ppermute | solution.py:137
  21.4 1.1 dynamic-slice_bitcast_fusion.4
  22.5 2.0 %collective-permute-start = (bf16[1024,128]{1,0:T(8,128)(2,1)S(1)}, bf16[1024,128]{1,0:T(8,128)(2,1)S(1)}, u32[]{:S(2)}, u32[]{:S(2)}) collective-permute-start(bf16[1024,128]{1,0:T(8,128)(2,1)S(1)} %get-tuple-element.5), channel_id=1, source_target_pairs={{0,16},{16,0},{1,17},{17,1},{2,18},{18,2},{3,19},{19,3},{4,20},{20... | collective-permute-start | bytes 786440 | tf_op jit(solution)/shard_map/ppermute | solution.py:134
  24.6 1.0 dynamic-slice_bitcast_fusion.table_ref
  25.5 0.1 add_select_fusion
  25.6 4.5 %convolution_convert_fusion.pattern_ref = bf16[8192,128]{1,0:T(8,128)(2,1)S(1)} fusion(bf16[128,128]{1,0:T(8,128)(2,1)S(1)} %copy-done.1, s32[8192]{0:T(1024)S(1)} %get-tuple-element.6), kind=kOutput, calls=%fused_computation | convolution fusion | flops 270532608 | bytes 2162688 | tf_op jit(solution)/shard_map/dot_general | solution.py:89
  30.1 0.0 collective-permute-done
  30.1 0.1 pad_maximum_fusion
  30.2 0.1 reverse_select_fusion
  30.3 0.2 copy.14.act_ref
  30.6 0.0 collective-permute-done.2.far_ref
  30.6 93.5 %all-gather.2.cloned.1.call-done.grd_ref = bf16[1024,4096]{1,0:T(8,128)(2,1)} async-done(((bf16[64,4096]{1,0:T(8,128)(2,1)}), bf16[1024,4096]{1,0:T(8,128)(2,1)}) %all-gather.2.cloned.1.call-update) | async-done | bytes 8388624 | tf_op jit(solution)/shard_map/all_gather | solution.py:136
  124.0 0.0 copy-start
  124.1 1.6 copy-done
  125.6 18.2 %sampled_gradient.1 = f32[64,128]{1,0:T(8,128)} custom-call(s32[8192]{0:T(1024)S(1)} %get-tuple-element.7.rows_ref, bf16[256,1024]{1,0:T(8,128)(2,1)S(1)} %copy.14.act_ref, bf16[1024,4096]{1,0:T(8,128)(2,1)} %all-gather.2.cloned.1.call-done.grd_ref, s32[128,4096]{1,0:T(8,128)S(1)} %copy-done, s32[128,4096]{1,0:T(8,128)} %collective-permute-done.2.far_ref, ...), custom_call_target="tpu_custom_call" | custom-call | tf_op jit(solution)/shard_map/sampled_gradient/pallas_call | solution.py:96
  143.9 9.6 %all-to-all-start = ((f32[32,1,256]{2,1,0:T(1,128)}), f32[32,1,256]{2,1,0:T(1,128)S(1)}, u32[]{:S(2)}, u32[]{:S(2)}) async-start(f32[32,1,256]{2,1,0:T(1,128)} %bitcast.9), calls=%async_computation | async-start | bytes 65536 | tf_op jit(solution)/shard_map/all_to_all | solution.py:145
  153.5 0.7 fusion.6
  154.2 11.3 %all-to-all-done = f32[32,1,256]{2,1,0:T(1,128)S(1)} async-done(((f32[32,1,256]{2,1,0:T(1,128)}), f32[32,1,256]{2,1,0:T(1,128)S(1)}, u32[]{:S(2)}, u32[]{:S(2)}) %all-to-all-start) | async-done | bytes 32800 | tf_op jit(solution)/shard_map/all_to_all | solution.py:145
  165.5 0.1 reduce
  165.6 0.1 multiply_reduce_fusion
  165.7 0.0 copy-start.3
  165.8 12.8 %all_to_all.19 = f32[16,2,256]{2,1,0:T(2,128)S(1)} all-to-all(f32[16,2,256]{2,1,0:T(2,128)S(1)} %broadcast_in_dim.7), channel_id=1, replica_groups=mesh['z'=16,'core'=2,'ex'=16] {'ex'}, dimensions={0} | all-to-all | bytes 65536 | tf_op jit(solution)/shard_map/all_to_all | solution.py:123
  178.6 0.1 fusion.7
  178.7 17.5 %all_to_all.20 = f32[32,2,32]{2,1,0:T(2,128)S(1)} all-to-all(f32[32,2,32]{2,1,0:T(2,128)S(1)} %broadcast_in_dim.8), channel_id=1, replica_groups=mesh['z'=16,'core'=2,'ex'=16] {'z','core'}, dimensions={0} | all-to-all | bytes 16384 | tf_op jit(solution)/shard_map/all_to_all | solution.py:123
  196.3 0.6 broadcast_multiply_fusion.1
  (11 shorter events, 0.1 us)
Async XLA Ops:
  7.2 18.5 %copy-start.1 = (bf16[128,128]{1,0:T(8,128)(2,1)S(1)}, bf16[128,128]{1,0:T(8,128)(2,1)}, u32[]{:S(2)}) copy-start(bf16[128,128]{1,0:T(8,128)(2,1)} %constant.113.clone) | copy-start | bytes 98308
  7.2 18.4 %copy-start.2 = (s32[8192]{0:T(1024)S(1)}, s32[8192]{0:T(1024)}, u32[]{:S(2)}) copy-start(s32[8192]{0:T(1024)} %param.10) | copy-start | bytes 98308
  7.2 116.8 %all-gather.2.cloned.1.call-start = ((), (), s32[]{:S(2)}) async-start(), calls=%async_computation.3 | async-start | bytes 8912896 | tf_op jit(solution)/shard_map/all_gather | solution.py:136
  8.3 9.9 %collective-permute-start.1 = (bf16[32,4096]{1,0:T(8,128)(2,1)S(1)}, bf16[32,4096]{1,0:T(8,128)(2,1)S(1)}, u32[]{:S(2)}, u32[]{:S(2)}) collective-permute-start(bf16[32,4096]{1,0:T(8,128)(2,1)S(1)} %get-tuple-element.3), channel_id=1, source_target_pairs={{0,16},{16,0},{1,17},{17,1},{2,18},{18,2},{3,19},{19,3},{4,20},{20... | collective-permute-start | bytes 786440 | tf_op jit(solution)/shard_map/ppermute | solution.py:134
  19.1 11.4 %collective-permute-start.2 = (s32[128,4096]{1,0:T(8,128)}, s32[128,4096]{1,0:T(8,128)}, u32[]{:S(2)}, u32[]{:S(2)}) collective-permute-start(s32[128,4096]{1,0:T(8,128)} %near_ref.1), channel_id=1, source_target_pairs={{0,16},{16,0},{1,17},{17,1},{2,18},{18,2},{3,19},{19,3},{4,20},{20... | collective-permute-start | bytes 6291464 | tf_op jit(solution)/shard_map/ppermute | solution.py:137
  22.5 7.6 %collective-permute-start = (bf16[1024,128]{1,0:T(8,128)(2,1)S(1)}, bf16[1024,128]{1,0:T(8,128)(2,1)S(1)}, u32[]{:S(2)}, u32[]{:S(2)}) collective-permute-start(bf16[1024,128]{1,0:T(8,128)(2,1)S(1)} %get-tuple-element.5), channel_id=1, source_target_pairs={{0,16},{16,0},{1,17},{17,1},{2,18},{18,2},{3,19},{19,3},{4,20},{20... | collective-permute-start | bytes 786440 | tf_op jit(solution)/shard_map/ppermute | solution.py:134
  124.0 1.6 copy-start
  143.9 21.6 %all-to-all-start = ((f32[32,1,256]{2,1,0:T(1,128)}), f32[32,1,256]{2,1,0:T(1,128)S(1)}, u32[]{:S(2)}, u32[]{:S(2)}) async-start(f32[32,1,256]{2,1,0:T(1,128)} %bitcast.9), calls=%async_computation | async-start | bytes 65536 | tf_op jit(solution)/shard_map/all_to_all | solution.py:145
  165.7 31.1 %copy-start.3 = (f32[2,256]{1,0:T(2,128)}, f32[2,256]{1,0:T(2,128)S(1)}, u32[]{:S(2)}) copy-start(f32[2,256]{1,0:T(2,128)S(1)} %broadcast_multiply_fusion) | copy-start | bytes 6148
Sparse Core Ops, SparseCore 0:
  19.3 104.7 all-gather.1

commit v4 on v3

--- a/solution.py
+++ b/solution.py
@@ -7,7 +7,7 @@
 from jax.sharding import Mesh, PartitionSpec as P
 
 LANES = 128
-WIDE = 1024
+WIDE = 2048
 BATCH = 1024
 
 
@@ -25,16 +25,15 @@
     return high, low
 
 
-def sampled_gradient(rows_ref, act_ref, grd_ref, near_ref, far_ref, pattern_ref, table_ref, ones_ref, out_ref, mixed, stage):
+def sampled_gradient(core_ref, rows_ref, act_ref, grd_ref, near_ref, far_ref, pattern_ref, table_ref, ones_ref, out_ref, mixed, stage):
     rows = act_ref.shape[0]
     outer = mixed.shape[0] // rows
     piece = pl.program_id(0)
 
     value = jnp.dot(act_ref[...], grd_ref[...], preferred_element_type=jnp.float32)
     near, far = value[: rows // 2], value[rows // 2:]
-    columns = pl.ds(pl.multiple_of(piece * WIDE, WIDE), WIDE)
-    near = jnp.where(near_ref[:, columns] == 1, near, -near)
-    far = jnp.where(far_ref[:, columns] == 1, far, -far)
+    near = jnp.where(near_ref[...] == 1, near, -near)
+    far = jnp.where(far_ref[...] == 1, far, -far)
     parts = [part for half in zip(halves(near), halves(far)) for part in half]
     out = jnp.dot(table_ref[...], jnp.concatenate(parts, axis=0), preferred_element_type=jnp.float32)
     for t in range(WIDE // LANES):
@@ -79,7 +78,7 @@
 
 def local_samples(act, grd, near, far, core, sample_index):
     rows, tokens = act.shape
-    width = grd.shape[1]
+    width = grd.shape[2]
     count = sample_index.shape[0]
     local = sample_index % (rows * width)
     row, column = local // width, local % width
@@ -95,26 +94,28 @@
     vmem = pl.BlockSpec(memory_space=pltpu.VMEM)
     out = pl.pallas_call(
         sampled_gradient,
-        grid=(width // WIDE,),
+        grid_spec=pltpu.PrefetchScalarGridSpec(
+            num_scalar_prefetch=2,
+            grid=(width // WIDE,),
+            in_specs=[
+                vmem,
+                pl.BlockSpec((None, tokens, WIDE), lambda i, which, _: (which[0], 0, i)),
+                pl.BlockSpec((rows // 2, WIDE), lambda i, *_: (0, i)),
+                pl.BlockSpec((rows // 2, WIDE), lambda i, *_: (0, i)),
+                vmem,
+                vmem,
+                vmem,
+            ],
+            out_specs=pl.BlockSpec((count // LANES, LANES), lambda i, *_: (0, 0)),
+            scratch_shapes=[
+                pltpu.VMEM((rows * width // LANES, LANES), jnp.float32),
+                pltpu.VMEM((count, LANES), jnp.float32),
+            ],
+        ),
         out_shape=jax.ShapeDtypeStruct((count // LANES, LANES), jnp.float32),
-        in_specs=[
-            pl.BlockSpec(memory_space=pltpu.SMEM),
-            vmem,
-            pl.BlockSpec((tokens, WIDE), lambda i: (0, i)),
-            vmem,
-            vmem,
-            vmem,
-            vmem,
-            vmem,
-        ],
-        out_specs=pl.BlockSpec((count // LANES, LANES), lambda i: (0, 0)),
-        scratch_shapes=[
-            pltpu.VMEM((rows * width // LANES, LANES), jnp.float32),
-            pltpu.VMEM((count, LANES), jnp.float32),
-        ],
         compiler_params=pltpu.CompilerParams(vmem_limit_bytes=40 * 1024 * 1024),
         name="sampled_gradient",
-    )(where_row, act, grd, near, far, pattern, table, ones)
+    )(core[None], where_row, act, grd, near, far, pattern, table, ones)
     return out
 
 
@@ -132,12 +133,9 @@
 
     mine = lambda pair: lax.dynamic_index_in_dim(pair, core, 0, keepdims=False)
     other = lambda pair: lax.ppermute(lax.dynamic_index_in_dim(pair, 1 - core, 0, keepdims=False), "core", swap)
-    block = jnp.concatenate([mine(out_grad), other(out_grad)], axis=0)
-    gathered = lax.all_gather(block, "z", axis=0, tiled=True)
+    gathered = lax.all_gather(out_grad, ("z", "core"), axis=1, tiled=True)
     far = lax.ppermute(sign_bits, "core", swap)
     act = jnp.concatenate([mine(activations), other(activations)], axis=1).T
-    act = act.reshape(2 * columns, chips, 2, seq_len // (2 * chips))
-    act = jnp.where(core == 0, act, act[:, :, ::-1]).reshape(2 * columns, seq_len)
 
     terms = local_samples(act, gathered, sign_bits, far, core, sample_index)
     feature_count = sample_index.shape[0]

time: 204 us -> 203 us (level)
  starting transfers between devices: 22.7 us -> 19.9 us
    ppermute x2 -> x1, starting transfers between devices: 10.8 us -> 1.92 us  [per_device(): lax.ppermute(lax.dynamic_index_in_dim(pair, 1 - core, 0, keepdims=False),...]
    ppermute x1, starting transfers between devices: 2.29 us -> 8.79 us  [per_device(): far = lax.ppermute(sign_bits, 'core', swap)]
    squeeze x2 -> x0, local copies, waits for them, and re-layouts: 2.14 us -> none  [per_device(): mine = lambda pair: lax.dynamic_index_in_dim(pair, core, 0, keepdims=False)]
    all_gather x1, waiting for transfers between devices: 93.5 us -> 95.6 us  [per_device(): gathered = lax.all_gather(out_grad, ('z', 'core'), axis=1, tiled=True)]
  transfers between devices with their start and end apart: 5 -> 4, of which waited for: 3 -> 2; matrix products, arithmetic and copies ran while one was open for 4% -> 5% of each run, Pallas kernels for 0% -> 0%
where the time goes in v4:
time: 203 us; the launch traced here: 202 us
  waiting for transfers between devices  108 us (53%)
  blocking collectives  30.2 us (15%)
  starting transfers between devices  19.9 us (10%)
  Pallas kernels  18.6 us (9%)
  between operations  14.2 us (7%)
  matrix products  5.35 us (3%)
  local copies, waits for them, and re-layouts  4.72 us (2%)
    all_gather x1, waiting for transfers between devices, per_device(): gathered = lax.all_gather(out_grad, ('z', 'core'), axis=1, tiled=True)  95.6 us
    all_to_all x2, blocking collectives, to_all(): lax.all_to_all(jnp.broadcast_to(value[None], (size,) + value.shape), axes...  30.2 us
    pallas_call x1, Pallas kernels, local_samples(): pl.pallas_call(sampled_gradient, grid_spec=pltpu.PrefetchScalarGridSpec(n...  18.6 us
    all_to_all x1, waiting for transfers between devices, per_device(): lax.all_to_all(terms.reshape(2 * chips, per), ('z', 'core'), 0, 0, tiled=...  11.4 us
    all_to_all x1, starting transfers between devices, per_device(): lax.all_to_all(terms.reshape(2 * chips, per), ('z', 'core'), 0, 0, tiled=...  9.13 us
    ppermute x1, starting transfers between devices, per_device(): far = lax.ppermute(sign_bits, 'core', swap)  8.79 us
    dot_general x1, matrix products, local_samples(): jnp.dot(inner.astype(jnp.bfloat16), small, preferred_element_type=jnp.flo...  5.23 us
  transfers between devices with their start and end apart: 4, of which 2 were waited for; matrix products, arithmetic and copies ran while one was open for 5% of the time, Pallas kernels for 0%

profile of v4, /device:TPU:1, one launch (start us, length us, event | category | flops | bytes accessed | tf_op | source)
XLA Modules:
  0.0 202.3 jit_solution(3244200529029768251)
XLA Ops:
  7.2 0.0 all-gather.2.cloned.1.call-start
  7.2 0.7 all-gather.2.cloned.1.call-update
  7.9 8.8 %collective-permute-start.1 = (s32[128,4096]{1,0:T(8,128)}, s32[128,4096]{1,0:T(8,128)}, u32[]{:S(2)}, u32[]{:S(2)}) collective-permute-start(s32[128,4096]{1,0:T(8,128)} %near_ref.1), channel_id=1, source_target_pairs={{0,16},{16,0},{1,17},{17,1},{2,18},{18,2},{3,19},{19,3},{4,20},{20... | collective-permute-start | bytes 6291464 | tf_op jit(solution)/shard_map/ppermute | solution.py:137
  16.7 1.1 constant_dynamic-slice_fusion.2
  17.8 0.1 copy.18
  17.9 1.9 collective-permute-start
  19.9 0.1 copy.17
  20.0 1.0 dynamic-slice_bitcast_fusion.table_ref
  21.0 0.8 add_select_fusion
  21.8 5.2 %convolution_convert_fusion.pattern_ref = bf16[8192,128]{1,0:T(8,128)(2,1)S(1)} fusion(bf16[128,128]{1,0:T(8,128)(2,1)} %constant.106.clone, s32[8192]{0:T(1024)S(1)} %get-tuple-element.4), kind=kOutput, calls=%fused_computation | convolution fusion | flops 270532608 | bytes 2162688 | tf_op jit(solution)/shard_map/dot_general | solution.py:88
  27.1 0.0 collective-permute-done
  27.1 0.0 collective-permute-done.1.far_ref
  27.1 95.6 %all-gather.2.cloned.1.call-done.grd_ref = bf16[2,1024,4096]{2,1,0:T(8,128)(2,1)} async-done(((bf16[2,32,4096]{2,1,0:T(8,128)(2,1)}), bf16[2,1024,4096]{2,1,0:T(8,128)(2,1)}) %all-gather.2.cloned.1.call-update) | async-done | bytes 16777232 | tf_op jit(solution)/shard_map/all_gather | solution.py:136
  122.7 0.0 copy-start
  122.7 1.6 copy-done
  124.3 18.6 %sampled_gradient.1 = f32[64,128]{1,0:T(8,128)} custom-call(s32[1]{0:T(128)} %bitcast.core_ref, s32[8192]{0:T(1024)S(1)} %get-tuple-element.5.rows_ref, bf16[256,1024]{1,0:T(8,128)(2,1)S(1)} %maximum_bitcast_fusion.act_ref, bf16[2,1024,4096]{2,1,0:T(8,128)(2,1)} %all-gather.2.cloned.1.call-done.grd_ref, s32[128,4096]{1,0:T(8,128)S(1)} %copy-done, ...), custom_call_target="tpu_custom_call" | custom-call | tf_op jit(solution)/shard_map/sampled_gradient/pallas_call | solution.py:95
  142.9 9.1 %all-to-all-start = ((f32[32,1,256]{2,1,0:T(1,128)}), f32[32,1,256]{2,1,0:T(1,128)S(1)}, u32[]{:S(2)}, u32[]{:S(2)}) async-start(f32[32,1,256]{2,1,0:T(1,128)} %bitcast.5), calls=%async_computation | async-start | bytes 65536 | tf_op jit(solution)/shard_map/all_to_all | solution.py:143
  152.1 0.7 fusion.6
  152.8 11.4 %all-to-all-done = f32[32,1,256]{2,1,0:T(1,128)S(1)} async-done(((f32[32,1,256]{2,1,0:T(1,128)}), f32[32,1,256]{2,1,0:T(1,128)S(1)}, u32[]{:S(2)}, u32[]{:S(2)}) %all-to-all-start) | async-done | bytes 32800 | tf_op jit(solution)/shard_map/all_to_all | solution.py:143
  164.2 0.1 reduce
  164.3 0.1 multiply_reduce_fusion
  164.4 0.0 copy-start.1
  164.4 12.8 %all_to_all.19 = f32[16,2,256]{2,1,0:T(2,128)S(1)} all-to-all(f32[16,2,256]{2,1,0:T(2,128)S(1)} %broadcast_in_dim.10), channel_id=1, replica_groups=mesh['z'=16,'core'=2,'ex'=16] {'ex'}, dimensions={0} | all-to-all | bytes 65536 | tf_op jit(solution)/shard_map/all_to_all | solution.py:124
  177.2 0.1 fusion.7
  177.4 17.4 %all_to_all.20 = f32[32,2,32]{2,1,0:T(2,128)S(1)} all-to-all(f32[32,2,32]{2,1,0:T(2,128)S(1)} %broadcast_in_dim.11), channel_id=1, replica_groups=mesh['z'=16,'core'=2,'ex'=16] {'z','core'}, dimensions={0} | all-to-all | bytes 16384 | tf_op jit(solution)/shard_map/all_to_all | solution.py:124
  194.9 0.6 broadcast_multiply_fusion.1
  195.4 0.0 copy-done.1
  (8 shorter events, 0.2 us)
Async XLA Ops:
  7.2 115.5 %all-gather.2.cloned.1.call-start = ((), (), s32[]{:S(2)}) async-start(), calls=%async_computation.3 | async-start | bytes 17301504 | tf_op jit(solution)/shard_map/all_gather | solution.py:136
  7.9 19.2 %collective-permute-start.1 = (s32[128,4096]{1,0:T(8,128)}, s32[128,4096]{1,0:T(8,128)}, u32[]{:S(2)}, u32[]{:S(2)}) collective-permute-start(s32[128,4096]{1,0:T(8,128)} %near_ref.1), channel_id=1, source_target_pairs={{0,16},{16,0},{1,17},{17,1},{2,18},{18,2},{3,19},{19,3},{4,20},{20... | collective-permute-start | bytes 6291464 | tf_op jit(solution)/shard_map/ppermute | solution.py:137
  17.9 9.1 %collective-permute-start = (bf16[1024,128]{0,1:T(8,128)(2,1)S(1)}, bf16[1024,128]{0,1:T(8,128)(2,1)S(1)}, u32[]{:S(2)}, u32[]{:S(2)}) collective-permute-start(bf16[1024,128]{0,1:T(8,128)(2,1)S(1)} %bitcast.14), channel_id=1, source_target_pairs={{0,16},{16,0},{1,17},{17,1},{2,18},{18,2},{3,19},{19,3},{4,20},{20... | collective-permute-start | bytes 786440 | tf_op jit(solution)/shard_map/ppermute | solution.py:135
  122.7 1.6 copy-start
  142.9 21.2 %all-to-all-start = ((f32[32,1,256]{2,1,0:T(1,128)}), f32[32,1,256]{2,1,0:T(1,128)S(1)}, u32[]{:S(2)}, u32[]{:S(2)}) async-start(f32[32,1,256]{2,1,0:T(1,128)} %bitcast.5), calls=%async_computation | async-start | bytes 65536 | tf_op jit(solution)/shard_map/all_to_all | solution.py:143
  164.4 31.1 %copy-start.1 = (f32[2,256]{1,0:T(2,128)}, f32[2,256]{1,0:T(2,128)S(1)}, u32[]{:S(2)}) copy-start(f32[2,256]{1,0:T(2,128)S(1)} %broadcast_multiply_fusion) | copy-start | bytes 6148
Sparse Core Ops, SparseCore 0:
  10.1 112.4 all-gather.1

commit v5 on v3

v5 whole, which is shorter than its diff:
```python
import jax
import jax.numpy as jnp
import numpy as np
from jax import lax
from jax.experimental import pallas as pl
from jax.experimental.pallas import tpu as pltpu
from jax.sharding import Mesh, PartitionSpec as P

LANES = 128
WIDE = 2048
BATCH = 1024
LOAD = 512
VMEM_MIB = 60


def sylvester(order):
    table = np.ones((1, 1), np.float32)
    base = np.array([[1.0, 1.0], [1.0, -1.0]], np.float32)
    while table.shape[0] < order:
        table = np.kron(table, base)
    return table


def halves(value):
    high = value.astype(jnp.bfloat16)
    low = (value - high.astype(jnp.float32)).astype(jnp.bfloat16)
    return high, low


def sampled_gradient(place_ref, index_ref, near_act_ref, far_act_ref, far_ref, table_ref, small_ref, near_ref, *refs):
    grd_refs, (out_ref, mixed, stage, signs, tokens, act, rows_v, rows_s, sem) = refs[:-9], refs[-9:]
    rows = act.shape[0]
    outer = mixed.shape[0] // rows
    width = outer * LANES
    piece, last = pl.program_id(0), pl.num_programs(0) - 1
    core = place_ref[0]
    row_copy = pltpu.make_async_copy(rows_v, rows_s, sem)

    @pl.when(piece == 0)
    def _():
        index = index_ref[...]
        row = (index // width) % rows
        rows_v[...] = (index % width) // LANES * rows + row
        row_copy.start()
        chips = len(grd_refs) // 2
        depth = grd_refs[0].shape[0]
        for which in range(2):
            for j in range(chips):
                source = lax.rem(place_ref[1] + j, chips) * (2 * depth) + lax.rem(core + which, 2) * depth
                source = pl.ds(pl.multiple_of(source, depth), depth)
                target = pl.ds((which * chips + j) * depth, depth)
                tokens[target, :rows // 2] = near_act_ref[core, source, :]
                tokens[target, rows // 2:] = far_act_ref[core, source, :]
        act[...] = tokens[...].T

    grd = jnp.concatenate([ref[...] for ref in grd_refs], axis=0)
    value = jnp.dot(act[...], grd, preferred_element_type=jnp.float32)
    near, far = value[: rows // 2], value[rows // 2:]
    columns = pl.ds(pl.multiple_of(piece * WIDE, WIDE), WIDE)
    near = jnp.where(near_ref[...] == 1, near, -near)
    far = jnp.where(far_ref[:, columns] == 1, far, -far)
    parts = [part for half in zip(halves(near), halves(far)) for part in half]
    out = jnp.dot(table_ref[core], jnp.concatenate(parts, axis=0), preferred_element_type=jnp.float32)
    for t in range(WIDE // LANES):
        first = pl.multiple_of((piece * (WIDE // LANES) + t) * rows, rows)
        mixed[pl.ds(first, rows), :] = out[:, t * LANES:(t + 1) * LANES]

    @pl.when(piece == last)
    def _():
        def outer_step(i, carry):
            first = pl.multiple_of(i * 8, 8)
            tiles = [mixed[pl.ds(pl.multiple_of(m * rows + first, 8), 8), :] for m in range(outer)]
            step = 1
            while step < outer:
                tiles = [tiles[m ^ step] - tiles[m] if m & step else tiles[m] + tiles[m ^ step] for m in range(outer)]
                step *= 2
            for m in range(outer):
                mixed[pl.ds(pl.multiple_of(m * rows + first, 8), 8), :] = tiles[m]
            return carry

        lax.fori_loop(0, rows // 8, outer_step, 0)

        row_copy.wait()

        across = lax.broadcasted_iota(jnp.int32, (LANES, LANES), 1)
        diagonal = lax.broadcasted_iota(jnp.int32, (LANES, LANES), 0) == across
        ones = jnp.ones((2 * LANES, LANES), jnp.bfloat16)

        def load_step(i, carry):
            first = pl.multiple_of(i * LOAD, LOAD)
            group = pl.ds(pl.multiple_of(i * (LOAD // LANES), LOAD // LANES), LOAD // LANES)
            inner = (index_ref[group, :] % LANES).astype(jnp.float32)
            spread = [jnp.where(diagonal, inner[g:g + 1, :], 0.0).astype(jnp.bfloat16) for g in range(LOAD // LANES)]
            spread = jnp.dot(jnp.concatenate(spread, axis=0), ones[:LANES], preferred_element_type=jnp.float32)
            lane = lax.broadcasted_iota(jnp.int32, (LOAD, LANES), 1).astype(jnp.float32)
            chosen = jnp.where(spread == lane, 1.0, 0.0).astype(jnp.bfloat16)
            pattern = jnp.dot(chosen, small_ref[...], preferred_element_type=jnp.float32)
            signs[pl.ds(first, LOAD), :] = pattern.astype(jnp.bfloat16)
            for s in range(LOAD):
                stage[pl.ds(first + s, 1), :] = mixed[pl.ds(rows_s[i * (LOAD // LANES) + s // LANES, s % LANES], 1), :]
            return carry

        lax.fori_loop(0, stage.shape[0] // LOAD, load_step, 0)

        def inner_step(i, carry):
            batch = pl.ds(pl.multiple_of(i * BATCH, BATCH), BATCH)
            terms = jnp.concatenate(halves(stage[batch, :] * signs[batch, :].astype(jnp.float32)), axis=1)
            total = jnp.dot(terms, ones, preferred_element_type=jnp.float32)
            lines = BATCH // LANES
            sums = [jnp.sum(jnp.where(diagonal, total[g * LANES:(g + 1) * LANES], 0.0), axis=0, keepdims=True) for g in range(lines)]
            out_ref[pl.ds(pl.multiple_of(i * lines, lines), lines), :] = jnp.concatenate(sums, axis=0)
            return carry

        lax.fori_loop(0, stage.shape[0] // BATCH, inner_step, 0)


def local_samples(near_act, far_act, blocks, near, far, core, here, sample_index):
    tokens = near_act.shape[1]
    rows = 2 * near_act.shape[2]
    width = near.shape[1]
    count = sample_index.shape[0]
    full = sylvester(rows)
    left, right = full[:, : rows // 2], full[:, rows // 2:]
    tables = np.stack([np.concatenate(pair, axis=1) for pair in ((left, right, left, right), (right, left, right, left))])
    vmem = pl.BlockSpec(memory_space=pltpu.VMEM)
    return pl.pallas_call(
        sampled_gradient,
        grid=(width // WIDE,),
        out_shape=jax.ShapeDtypeStruct((count // LANES, LANES), jnp.float32),
        in_specs=[pl.BlockSpec(memory_space=pltpu.SMEM)]
        + [vmem] * 6
        + [pl.BlockSpec((part.shape[0], WIDE), lambda i: (0, i)) for part in (near, *blocks)],
        out_specs=pl.BlockSpec((count // LANES, LANES), lambda i: (0, 0)),
        scratch_shapes=[
            pltpu.VMEM((rows * width // LANES, LANES), jnp.float32),
            pltpu.VMEM((count, LANES), jnp.float32),
            pltpu.VMEM((count, LANES), jnp.bfloat16),
            pltpu.VMEM((tokens, rows), jnp.bfloat16),
            pltpu.VMEM((rows, tokens), jnp.bfloat16),
            pltpu.VMEM((count // LANES, LANES), jnp.int32),
            pltpu.SMEM((count // LANES, LANES), jnp.int32),
            pltpu.SemaphoreType.DMA,
        ],
        compiler_params=pltpu.CompilerParams(vmem_limit_bytes=VMEM_MIB * 1024 * 1024),
        name="sampled_gradient",
    )(
        jnp.stack([core, here]).astype(jnp.int32),
        sample_index.reshape(count // LANES, LANES),
        near_act,
        far_act,
        far,
        jnp.asarray(tables, jnp.bfloat16),
        jnp.asarray(sylvester(LANES), jnp.bfloat16),
        near,
        *blocks,
    )


def around(blocks, axis):
    size = lax.axis_size(axis)
    up = [(i, (i + 1) % size) for i in range(size)]
    down = [(i, (i - 1) % size) for i in range(size)]
    ups, downs = [[[block] for block in blocks] for _ in range(2)]
    for step in range(size // 2):
        for chain in ups:
            chain.append(lax.ppermute(chain[-1], axis, up))
        if step < (size - 1) // 2:
            for chain in downs:
                chain.append(lax.ppermute(chain[-1], axis, down))
    return [part for one, two in zip(downs, ups) for part in one + two[:0:-1]]


def to_all(value, axes):
    size = lax.axis_size(axes)
    return lax.all_to_all(jnp.broadcast_to(value[None], (size,) + value.shape), axes, 0, 0, tiled=True)


def per_device(activations, out_grad, sign_bits, sample_index):
    seq_len, width = activations.shape[1], out_grad.shape[2]
    chips = lax.axis_size("z")
    here, core = lax.axis_index("z"), lax.axis_index("core")
    swap = [(0, 1), (1, 0)]

    mine = lax.dynamic_index_in_dim(out_grad, core, 0, keepdims=False)
    other = lax.ppermute(lax.dynamic_index_in_dim(out_grad, 1 - core, 0, keepdims=False), "core", swap)
    far_act = lax.ppermute(activations, "core", swap)
    far = lax.ppermute(sign_bits, "core", swap)
    blocks = around([mine, other], "z")

    terms = local_samples(activations, far_act, blocks, sign_bits, far, core, here, sample_index)
    feature_count = sample_index.shape[0]
    per = feature_count // (2 * chips)
    terms = lax.all_to_all(terms.reshape(2 * chips, per), ("z", "core"), 0, 0, tiled=True)
    signs = lax.dynamic_index_in_dim(jnp.asarray(sylvester(chips), jnp.float32), here, 0, keepdims=False)
    scale = 1.0 / (width * float(seq_len) ** 0.5)
    features = jnp.sum(terms.reshape(chips, 2, per) * signs[:, None, None], axis=0) * scale
    everyone = to_all(features, "ex").reshape(-1, per)
    inner = jnp.dot(features, everyone.T, precision=lax.Precision.HIGHEST)
    gram = jnp.sum(to_all(inner, ("z", "core")), axis=0) / feature_count
    return (features, gram)


def solution(mesh):
    params, groups = mesh.devices.shape
    chips = Mesh(mesh.devices.reshape(params // 2, 2, groups), ("z", "core", "ex"))
    param = ("z", "core")
    return jax.shard_map(
        per_device,
        mesh=chips,
        in_specs=(P("ex", None, param), P("ex", param, None), P(param, None), P()),
        out_specs=(P("ex", param), P("ex", None)),
        check_vma=False,
    )
```

time: 204 us -> 196 us (0.961)
  starting transfers between devices: 22.7 us -> 119 us
  waiting for transfers between devices: 106 us -> 20.4 us
  between operations: 14.2 us -> 1.55 us
  matrix products: 4.59 us -> 0.13 us
  local copies, waits for them, and re-layouts: 5.72 us -> 1.96 us
    all_gather x1 -> x0, waiting for transfers between devices: 93.5 us -> none  [per_device(): gathered = lax.all_gather(block, 'z', axis=0, tiled=True)]
    ppermute x2 -> x32, starting transfers between devices: 10.8 us -> 99.4 us  [the longest x14 51.5 us: around(): chain.append(lax.ppermute(chain[-1], axis, down))]
    ppermute x2 -> x32, waiting for transfers between devices: 1.14 us -> 9.22 us  [the longest x16 8.9 us: around(): chain.append(lax.ppermute(chain[-1], axis, up))]
    all_to_all x1, starting transfers between devices: 9.58 us -> 17.3 us  [per_device(): lax.all_to_all(terms.reshape(2 * chips, per), ('z', 'core'), 0, 0, tiled=...]
    dot_general x1 -> x0, matrix products: 4.47 us -> none  [local_samples(): jnp.dot(inner.astype(jnp.bfloat16), small, preferred_element_type=jnp.flo...]
    squeeze x3 -> x1, local copies, waits for them, and re-layouts: 3.12 us -> 1.07 us  [per_device(): lax.dynamic_index_in_dim(out_grad, 1 - core, 0, keepdims=False)]
  transfers between devices with their start and end apart: 5 -> 34, of which waited for: 3 -> 6; matrix products, arithmetic and copies ran while one was open for 4% -> 1% of each run, Pallas kernels for 0% -> 0%
where the time goes in v5:
time: 196 us; the launch traced here: 195 us
  starting transfers between devices  119 us (61%)
  blocking collectives  30.6 us (16%)
  waiting for transfers between devices  20.4 us (10%)
  Pallas kernels  19.3 us (10%)
  local copies, waits for them, and re-layouts  1.96 us (1%)
    ppermute x14, starting transfers between devices, around(): chain.append(lax.ppermute(chain[-1], axis, down))  51.5 us
    ppermute x16, starting transfers between devices, around(): chain.append(lax.ppermute(chain[-1], axis, up))  37.2 us
    all_to_all x2, blocking collectives, to_all(): lax.all_to_all(jnp.broadcast_to(value[None], (size,) + value.shape), axes...  30.6 us
    pallas_call x1, Pallas kernels, local_samples(): pl.pallas_call(sampled_gradient, grid=(width // WIDE,), out_shape=jax.Sha...  19.3 us
    all_to_all x1, starting transfers between devices, per_device(): lax.all_to_all(terms.reshape(2 * chips, per), ('z', 'core'), 0, 0, tiled=...  17.3 us
    all_to_all x1, waiting for transfers between devices, per_device(): lax.all_to_all(terms.reshape(2 * chips, per), ('z', 'core'), 0, 0, tiled=...  11.2 us
    ppermute x16, waiting for transfers between devices, around(): chain.append(lax.ppermute(chain[-1], axis, up))  8.9 us
    ppermute x1, starting transfers between devices, per_device(): lax.ppermute(lax.dynamic_index_in_dim(out_grad, 1 - core, 0, keepdims=Fal...  8.79 us
  transfers between devices with their start and end apart: 34, of which 6 were waited for; matrix products, arithmetic and copies ran while one was open for 1% of the time, Pallas kernels for 0%

profile of v5, /device:TPU:1, one launch (start us, length us, event | category | flops | bytes accessed | tf_op | source)
XLA Modules:
  0.0 194.7 jit_solution(16512561699961549824)
XLA Ops:
  1.7 8.8 %collective-permute-start.17 = (bf16[32,4096]{1,0:T(8,128)(2,1)S(1)}, bf16[32,4096]{1,0:T(8,128)(2,1)S(1)}, u32[]{:S(2)}, u32[]{:S(2)}) collective-permute-start(bf16[32,4096]{1,0:T(8,128)(2,1)S(1)} %get-tuple-element.2), channel_id=1, source_target_pairs={{0,16},{16,0},{1,17},{17,1},{2,18},{18,2},{3,19},{19,3},{4,20},{20... | collective-permute-start | bytes 786440 | tf_op jit(solution)/shard_map/ppermute | solution.py:185
  12.4 5.7 %collective-permute-start.2 = (bf16[32,4096]{1,0:T(8,128)(2,1)S(1)}, bf16[32,4096]{1,0:T(8,128)(2,1)S(1)}, u32[]{:S(2)}, u32[]{:S(2)}) collective-permute-start(bf16[32,4096]{1,0:T(8,128)(2,1)S(1)} %get-tuple-element.3.refs_0_), channel_id=1, source_target_pairs={{0,480},{32,0},{64,32},{96,64},{128,96},{160,128},{192,160},{224,1... | collective-permute-start | bytes 786440 | tf_op jit(solution)/shard_map/ppermute | solution.py:169
  20.1 4.6 %collective-permute-start.18 = (bf16[32,4096]{1,0:T(8,128)(2,1)S(1)}, bf16[32,4096]{1,0:T(8,128)(2,1)S(1)}, u32[]{:S(2)}, u32[]{:S(2)}) collective-permute-start(bf16[32,4096]{1,0:T(8,128)(2,1)S(1)} %collective-permute-done.17.refs_16_), channel_id=1, source_target_pairs={{0,480},{32,0},{64,32},{96,64},{128,96},{160,128},{192,160},{224,1... | collective-permute-start | bytes 786440 | tf_op jit(solution)/shard_map/ppermute | solution.py:169
  24.7 2.8 %collective-permute-start.1 = (s32[128,4096]{1,0:T(8,128)}, s32[128,4096]{1,0:T(8,128)S(1)}, u32[]{:S(2)}, u32[]{:S(2)}) collective-permute-start(s32[128,4096]{1,0:T(8,128)} %near_ref.1), channel_id=1, source_target_pairs={{0,16},{16,0},{1,17},{17,1},{2,18},{18,2},{3,19},{19,3},{4,20},{20... | collective-permute-start | bytes 6291464 | tf_op jit(solution)/shard_map/ppermute | solution.py:187
  27.5 1.9 collective-permute-start
  31.4 4.6 %collective-permute-start.3 = (bf16[32,4096]{1,0:T(8,128)(2,1)S(1)}, bf16[32,4096]{1,0:T(8,128)(2,1)S(1)}, u32[]{:S(2)}, u32[]{:S(2)}) collective-permute-start(bf16[32,4096]{1,0:T(8,128)(2,1)S(1)} %collective-permute-done.2.refs_1_), channel_id=1, source_target_pairs={{0,480},{32,0},{64,32},{96,64},{128,96},{160,128},{192,160},{224,1... | collective-permute-start | bytes 786440 | tf_op jit(solution)/shard_map/ppermute | solution.py:169
  37.9 2.0 %collective-permute-done.10.refs_14_ = bf16[32,4096]{1,0:T(8,128)(2,1)S(1)} collective-permute-done((bf16[32,4096]{1,0:T(8,128)(2,1)S(1)}, bf16[32,4096]{1,0:T(8,128)(2,1)S(1)}, u32[]{:S(2)}, u32[]{:S(2)}) %collective-permute-start.10) | collective-permute-done | bytes 262176 | tf_op jit(solution)/shard_map/ppermute | solution.py:166
  39.9 2.6 %collective-permute-start.19 = (bf16[32,4096]{1,0:T(8,128)(2,1)S(1)}, bf16[32,4096]{1,0:T(8,128)(2,1)S(1)}, u32[]{:S(2)}, u32[]{:S(2)}) collective-permute-start(bf16[32,4096]{1,0:T(8,128)(2,1)S(1)} %collective-permute-done.18.refs_17_), channel_id=1, source_target_pairs={{0,480},{32,0},{64,32},{96,64},{128,96},{160,128},{192,160},{224,1... | collective-permute-start | bytes 786440 | tf_op jit(solution)/shard_map/ppermute | solution.py:169
  42.6 2.7 %collective-permute-start.11 = (bf16[32,4096]{1,0:T(8,128)(2,1)S(1)}, bf16[32,4096]{1,0:T(8,128)(2,1)S(1)}, u32[]{:S(2)}, u32[]{:S(2)}) collective-permute-start(bf16[32,4096]{1,0:T(8,128)(2,1)S(1)} %collective-permute-done.10.refs_14_), channel_id=1, source_target_pairs={{0,32},{32,64},{64,96},{96,128},{128,160},{160,192},{192,224},{224... | collective-permute-start | bytes 786440 | tf_op jit(solution)/shard_map/ppermute | solution.py:166
  47.8 4.6 %collective-permute-start.4 = (bf16[32,4096]{1,0:T(8,128)(2,1)S(1)}, bf16[32,4096]{1,0:T(8,128)(2,1)S(1)}, u32[]{:S(2)}, u32[]{:S(2)}) collective-permute-start(bf16[32,4096]{1,0:T(8,128)(2,1)S(1)} %collective-permute-done.3.refs_2_), channel_id=1, source_target_pairs={{0,480},{32,0},{64,32},{96,64},{128,96},{160,128},{192,160},{224,1... | collective-permute-start | bytes 786440 | tf_op jit(solution)/shard_map/ppermute | solution.py:169
  52.4 2.0 %collective-permute-start.20 = (bf16[32,4096]{1,0:T(8,128)(2,1)S(1)}, bf16[32,4096]{1,0:T(8,128)(2,1)S(1)}, u32[]{:S(2)}, u32[]{:S(2)}) collective-permute-start(bf16[32,4096]{1,0:T(8,128)(2,1)S(1)} %collective-permute-done.19.refs_18_), channel_id=1, source_target_pairs={{0,480},{32,0},{64,32},{96,64},{128,96},{160,128},{192,160},{224,1... | collective-permute-start | bytes 786440 | tf_op jit(solution)/shard_map/ppermute | solution.py:169
  54.5 3.3 %collective-permute-start.12 = (bf16[32,4096]{1,0:T(8,128)(2,1)S(1)}, bf16[32,4096]{1,0:T(8,128)(2,1)S(1)}, u32[]{:S(2)}, u32[]{:S(2)}) collective-permute-start(bf16[32,4096]{1,0:T(8,128)(2,1)S(1)} %collective-permute-done.11.refs_13_), channel_id=1, source_target_pairs={{0,32},{32,64},{64,96},{96,128},{128,160},{160,192},{192,224},{224... | collective-permute-start | bytes 786440 | tf_op jit(solution)/shard_map/ppermute | solution.py:166
  59.8 4.6 %collective-permute-start.5 = (bf16[32,4096]{1,0:T(8,128)(2,1)S(1)}, bf16[32,4096]{1,0:T(8,128)(2,1)S(1)}, u32[]{:S(2)}, u32[]{:S(2)}) collective-permute-start(bf16[32,4096]{1,0:T(8,128)(2,1)S(1)} %collective-permute-done.4.refs_3_), channel_id=1, source_target_pairs={{0,480},{32,0},{64,32},{96,64},{128,96},{160,128},{192,160},{224,1... | collective-permute-start | bytes 786440 | tf_op jit(solution)/shard_map/ppermute | solution.py:169
  64.4 2.3 %collective-permute-start.21 = (bf16[32,4096]{1,0:T(8,128)(2,1)S(1)}, bf16[32,4096]{1,0:T(8,128)(2,1)S(1)}, u32[]{:S(2)}, u32[]{:S(2)}) collective-permute-start(bf16[32,4096]{1,0:T(8,128)(2,1)S(1)} %collective-permute-done.20.refs_19_), channel_id=1, source_target_pairs={{0,480},{32,0},{64,32},{96,64},{128,96},{160,128},{192,160},{224,1... | collective-permute-start | bytes 786440 | tf_op jit(solution)/shard_map/ppermute | solution.py:169
  66.7 3.0 %collective-permute-start.13 = (bf16[32,4096]{1,0:T(8,128)(2,1)S(1)}, bf16[32,4096]{1,0:T(8,128)(2,1)S(1)}, u32[]{:S(2)}, u32[]{:S(2)}) collective-permute-start(bf16[32,4096]{1,0:T(8,128)(2,1)S(1)} %collective-permute-done.12.refs_12_), channel_id=1, source_target_pairs={{0,32},{32,64},{64,96},{96,128},{128,160},{160,192},{192,224},{224... | collective-permute-start | bytes 786440 | tf_op jit(solution)/shard_map/ppermute | solution.py:166
  71.7 4.6 %collective-permute-start.6 = (bf16[32,4096]{1,0:T(8,128)(2,1)S(1)}, bf16[32,4096]{1,0:T(8,128)(2,1)S(1)}, u32[]{:S(2)}, u32[]{:S(2)}) collective-permute-start(bf16[32,4096]{1,0:T(8,128)(2,1)S(1)} %collective-permute-done.5.refs_4_), channel_id=1, source_target_pairs={{0,480},{32,0},{64,32},{96,64},{128,96},{160,128},{192,160},{224,1... | collective-permute-start | bytes 786440 | tf_op jit(solution)/shard_map/ppermute | solution.py:169
  76.3 2.3 %collective-permute-start.22 = (bf16[32,4096]{1,0:T(8,128)(2,1)S(1)}, bf16[32,4096]{1,0:T(8,128)(2,1)S(1)}, u32[]{:S(2)}, u32[]{:S(2)}) collective-permute-start(bf16[32,4096]{1,0:T(8,128)(2,1)S(1)} %collective-permute-done.21.refs_20_), channel_id=1, source_target_pairs={{0,480},{32,0},{64,32},{96,64},{128,96},{160,128},{192,160},{224,1... | collective-permute-start | bytes 786440 | tf_op jit(solution)/shard_map/ppermute | solution.py:169
  78.6 3.0 %collective-permute-start.14 = (bf16[32,4096]{1,0:T(8,128)(2,1)S(1)}, bf16[32,4096]{1,0:T(8,128)(2,1)S(1)}, u32[]{:S(2)}, u32[]{:S(2)}) collective-permute-start(bf16[32,4096]{1,0:T(8,128)(2,1)S(1)} %collective-permute-done.13.refs_11_), channel_id=1, source_target_pairs={{0,32},{32,64},{64,96},{96,128},{128,160},{160,192},{192,224},{224... | collective-permute-start | bytes 786440 | tf_op jit(solution)/shard_map/ppermute | solution.py:166
  83.6 4.6 %collective-permute-start.7 = (bf16[32,4096]{1,0:T(8,128)(2,1)S(1)}, bf16[32,4096]{1,0:T(8,128)(2,1)}, u32[]{:S(2)}, u32[]{:S(2)}) collective-permute-start(bf16[32,4096]{1,0:T(8,128)(2,1)S(1)} %collective-permute-done.6.refs_5_), channel_id=1, source_target_pairs={{0,480},{32,0},{64,32},{96,64},{128,96},{160,128},{192,160},{224,1... | collective-permute-start | bytes 786440 | tf_op jit(solution)/shard_map/ppermute | solution.py:169
  88.2 2.3 %collective-permute-start.23 = (bf16[32,4096]{1,0:T(8,128)(2,1)S(1)}, bf16[32,4096]{1,0:T(8,128)(2,1)}, u32[]{:S(2)}, u32[]{:S(2)}) collective-permute-start(bf16[32,4096]{1,0:T(8,128)(2,1)S(1)} %collective-permute-done.22.refs_21_), channel_id=1, source_target_pairs={{0,480},{32,0},{64,32},{96,64},{128,96},{160,128},{192,160},{224,1... | collective-permute-start | bytes 786440 | tf_op jit(solution)/shard_map/ppermute | solution.py:169
  90.5 3.0 %collective-permute-start.15 = (bf16[32,4096]{1,0:T(8,128)(2,1)S(1)}, bf16[32,4096]{1,0:T(8,128)(2,1)}, u32[]{:S(2)}, u32[]{:S(2)}) collective-permute-start(bf16[32,4096]{1,0:T(8,128)(2,1)S(1)} %collective-permute-done.14.refs_10_), channel_id=1, source_target_pairs={{0,32},{32,64},{64,96},{96,128},{128,160},{160,192},{192,224},{224... | collective-permute-start | bytes 786440 | tf_op jit(solution)/shard_map/ppermute | solution.py:166
  93.6 1.9 collective-permute-start.31
  95.5 4.6 %collective-permute-start.8 = (bf16[32,4096]{1,0:T(8,128)(2,1)}, bf16[32,4096]{1,0:T(8,128)(2,1)}, u32[]{:S(2)}, u32[]{:S(2)}) collective-permute-start(bf16[32,4096]{1,0:T(8,128)(2,1)} %collective-permute-done.7.refs_6_), channel_id=1, source_target_pairs={{0,480},{32,0},{64,32},{96,64},{128,96},{160,128},{192,160},{224,1... | collective-permute-start | bytes 786440 | tf_op jit(solution)/shard_map/ppermute | solution.py:169
  100.1 2.3 %collective-permute-start.24 = (bf16[32,4096]{1,0:T(8,128)(2,1)}, bf16[32,4096]{1,0:T(8,128)(2,1)}, u32[]{:S(2)}, u32[]{:S(2)}) collective-permute-start(bf16[32,4096]{1,0:T(8,128)(2,1)} %collective-permute-done.23.refs_22_), channel_id=1, source_target_pairs={{0,480},{32,0},{64,32},{96,64},{128,96},{160,128},{192,160},{224,1... | collective-permute-start | bytes 786440 | tf_op jit(solution)/shard_map/ppermute | solution.py:169
  102.4 3.0 %collective-permute-start.16 = (bf16[32,4096]{1,0:T(8,128)(2,1)}, bf16[32,4096]{1,0:T(8,128)(2,1)}, u32[]{:S(2)}, u32[]{:S(2)}) collective-permute-start(bf16[32,4096]{1,0:T(8,128)(2,1)} %collective-permute-done.15.refs_9_), channel_id=1, source_target_pairs={{0,32},{32,64},{64,96},{96,128},{128,160},{160,192},{192,224},{224... | collective-permute-start | bytes 786440 | tf_op jit(solution)/shard_map/ppermute | solution.py:166
  108.3 3.5 %collective-permute-done.16.refs_8_ = bf16[32,4096]{1,0:T(8,128)(2,1)} collective-permute-done((bf16[32,4096]{1,0:T(8,128)(2,1)}, bf16[32,4096]{1,0:T(8,128)(2,1)}, u32[]{:S(2)}, u32[]{:S(2)}) %collective-permute-start.16) | collective-permute-done | bytes 262176 | tf_op jit(solution)/shard_map/ppermute | solution.py:166
  111.8 2.8 %collective-permute-done.32.refs_24_ = bf16[32,4096]{1,0:T(8,128)(2,1)} collective-permute-done((bf16[32,4096]{1,0:T(8,128)(2,1)}, bf16[32,4096]{1,0:T(8,128)(2,1)}, u32[]{:S(2)}, u32[]{:S(2)}) %collective-permute-start.32) | collective-permute-done | bytes 262176 | tf_op jit(solution)/shard_map/ppermute | solution.py:166
  114.6 19.3 %sampled_gradient.1 = f32[64,128]{1,0:T(8,128)} custom-call(s32[2]{0:T(128)} %pad_add_fusion.place_ref, s32[64,128]{1,0:T(8,128)} %bitcast.13, bf16[2,1024,128]{2,1,0:T(8,128)(2,1)} %near_act_ref.1, bf16[2,1024,128]{2,1,0:T(8,128)(2,1)} %copy-done.2, s32[128,4096]{1,0:T(8,128)} %copy-done, bf16[2,256,512]{2,1,0:T(8,128)(2,1)} %constant.41.clone.table_ref, ...), custom_call_target="tpu_custom_call" | custom-call | tf_op jit(solution)/shard_map/sampled_gradient/pallas_call | solution.py:126
  133.9 17.3 %all-to-all-start = ((f32[32,1,256]{2,1,0:T(1,128)}), f32[32,1,256]{2,1,0:T(1,128)S(1)}, u32[]{:S(2)}, u32[]{:S(2)}) async-start(f32[32,1,256]{2,1,0:T(1,128)} %bitcast.12), calls=%async_computation | async-start | bytes 65536 | tf_op jit(solution)/shard_map/all_to_all | solution.py:193
  151.8 11.2 %all-to-all-done = f32[32,1,256]{2,1,0:T(1,128)S(1)} async-done(((f32[32,1,256]{2,1,0:T(1,128)}), f32[32,1,256]{2,1,0:T(1,128)S(1)}, u32[]{:S(2)}, u32[]{:S(2)}) %all-to-all-start) | async-done | bytes 32800 | tf_op jit(solution)/shard_map/all_to_all | solution.py:193
  163.3 13.0 %all_to_all.19 = f32[16,2,256]{2,1,0:T(2,128)S(1)} all-to-all(f32[16,2,256]{2,1,0:T(2,128)S(1)} %broadcast_in_dim.4), channel_id=1, replica_groups=mesh['z'=16,'core'=2,'ex'=16] {'ex'}, dimensions={0} | all-to-all | bytes 65536 | tf_op jit(solution)/shard_map/all_to_all | solution.py:175
  176.5 17.6 %all_to_all.20 = f32[32,2,32]{2,1,0:T(2,128)S(1)} all-to-all(f32[32,2,32]{2,1,0:T(2,128)S(1)} %broadcast_in_dim.5), channel_id=1, replica_groups=mesh['z'=16,'core'=2,'ex'=16] {'z','core'}, dimensions={0} | all-to-all | bytes 16384 | tf_op jit(solution)/shard_map/all_to_all | solution.py:175
  (106 shorter events, 21.7 us)
Async XLA Ops:
  1.7 16.5 %collective-permute-start.17 = (bf16[32,4096]{1,0:T(8,128)(2,1)S(1)}, bf16[32,4096]{1,0:T(8,128)(2,1)S(1)}, u32[]{:S(2)}, u32[]{:S(2)}) collective-permute-start(bf16[32,4096]{1,0:T(8,128)(2,1)S(1)} %get-tuple-element.2), channel_id=1, source_target_pairs={{0,16},{16,0},{1,17},{17,1},{2,18},{18,2},{3,19},{19,3},{4,20},{20... | collective-permute-start | bytes 786440 | tf_op jit(solution)/shard_map/ppermute | solution.py:185
  10.5 17.0 %collective-permute-start.9 = (bf16[32,4096]{1,0:T(8,128)(2,1)S(1)}, bf16[32,4096]{1,0:T(8,128)(2,1)S(1)}, u32[]{:S(2)}, u32[]{:S(2)}) collective-permute-start(bf16[32,4096]{1,0:T(8,128)(2,1)S(1)} %get-tuple-element.3.refs_0_), channel_id=1, source_target_pairs={{0,32},{32,64},{64,96},{96,128},{128,160},{160,192},{192,224},{224... | collective-permute-start | bytes 786440 | tf_op jit(solution)/shard_map/ppermute | solution.py:166
  12.4 17.0 %collective-permute-start.2 = (bf16[32,4096]{1,0:T(8,128)(2,1)S(1)}, bf16[32,4096]{1,0:T(8,128)(2,1)S(1)}, u32[]{:S(2)}, u32[]{:S(2)}) collective-permute-start(bf16[32,4096]{1,0:T(8,128)(2,1)S(1)} %get-tuple-element.3.refs_0_), channel_id=1, source_target_pairs={{0,480},{32,0},{64,32},{96,64},{128,96},{160,128},{192,160},{224,1... | collective-permute-start | bytes 786440 | tf_op jit(solution)/shard_map/ppermute | solution.py:169
  18.2 13.2 %collective-permute-start.25 = (bf16[32,4096]{1,0:T(8,128)(2,1)S(1)}, bf16[32,4096]{1,0:T(8,128)(2,1)S(1)}, u32[]{:S(2)}, u32[]{:S(2)}) collective-permute-start(bf16[32,4096]{1,0:T(8,128)(2,1)S(1)} %collective-permute-done.17.refs_16_), channel_id=1, source_target_pairs={{0,32},{32,64},{64,96},{96,128},{128,160},{160,192},{192,224},{224... | collective-permute-start | bytes 786440 | tf_op jit(solution)/shard_map/ppermute | solution.py:166
  20.1 15.9 %collective-permute-start.18 = (bf16[32,4096]{1,0:T(8,128)(2,1)S(1)}, bf16[32,4096]{1,0:T(8,128)(2,1)S(1)}, u32[]{:S(2)}, u32[]{:S(2)}) collective-permute-start(bf16[32,4096]{1,0:T(8,128)(2,1)S(1)} %collective-permute-done.17.refs_16_), channel_id=1, source_target_pairs={{0,480},{32,0},{64,32},{96,64},{128,96},{160,128},{192,160},{224,1... | collective-permute-start | bytes 786440 | tf_op jit(solution)/shard_map/ppermute | solution.py:169
  24.7 87.0 %collective-permute-start.1 = (s32[128,4096]{1,0:T(8,128)}, s32[128,4096]{1,0:T(8,128)S(1)}, u32[]{:S(2)}, u32[]{:S(2)}) collective-permute-start(s32[128,4096]{1,0:T(8,128)} %near_ref.1), channel_id=1, source_target_pairs={{0,16},{16,0},{1,17},{17,1},{2,18},{18,2},{3,19},{19,3},{4,20},{20... | collective-permute-start | bytes 6291464 | tf_op jit(solution)/shard_map/ppermute | solution.py:187
  27.5 20.3 %collective-permute-start = (bf16[2,1024,128]{2,1,0:T(8,128)(2,1)}, bf16[2,1024,128]{2,1,0:T(8,128)(2,1)S(1)}, u32[]{:S(2)}, u32[]{:S(2)}) collective-permute-start(bf16[2,1024,128]{2,1,0:T(8,128)(2,1)} %near_act_ref.1), channel_id=1, source_target_pairs={{0,16},{16,0},{1,17},{17,1},{2,18},{18,2},{3,19},{19,3},{4,20},{20... | collective-permute-start | bytes 1572872 | tf_op jit(solution)/shard_map/ppermute | solution.py:186
  29.5 10.5 %collective-permute-start.10 = (bf16[32,4096]{1,0:T(8,128)(2,1)S(1)}, bf16[32,4096]{1,0:T(8,128)(2,1)S(1)}, u32[]{:S(2)}, u32[]{:S(2)}) collective-permute-start(bf16[32,4096]{1,0:T(8,128)(2,1)S(1)} %collective-permute-done.9.refs_15_), channel_id=1, source_target_pairs={{0,32},{32,64},{64,96},{96,128},{128,160},{160,192},{192,224},{224... | collective-permute-start | bytes 786440 | tf_op jit(solution)/shard_map/ppermute | solution.py:166
  31.4 11.1 %collective-permute-start.3 = (bf16[32,4096]{1,0:T(8,128)(2,1)S(1)}, bf16[32,4096]{1,0:T(8,128)(2,1)S(1)}, u32[]{:S(2)}, u32[]{:S(2)}) collective-permute-start(bf16[32,4096]{1,0:T(8,128)(2,1)S(1)} %collective-permute-done.2.refs_1_), channel_id=1, source_target_pairs={{0,480},{32,0},{64,32},{96,64},{128,96},{160,128},{192,160},{224,1... | collective-permute-start | bytes 786440 | tf_op jit(solution)/shard_map/ppermute | solution.py:169
  36.0 9.8 %collective-permute-start.26 = (bf16[32,4096]{1,0:T(8,128)(2,1)S(1)}, bf16[32,4096]{1,0:T(8,128)(2,1)S(1)}, u32[]{:S(2)}, u32[]{:S(2)}) collective-permute-start(bf16[32,4096]{1,0:T(8,128)(2,1)S(1)} %collective-permute-done.25.refs_31_), channel_id=1, source_target_pairs={{0,32},{32,64},{64,96},{96,128},{128,160},{160,192},{192,224},{224... | collective-permute-start | bytes 786440 | tf_op jit(solution)/shard_map/ppermute | solution.py:166
  39.9 12.5 %collective-permute-start.19 = (bf16[32,4096]{1,0:T(8,128)(2,1)S(1)}, bf16[32,4096]{1,0:T(8,128)(2,1)S(1)}, u32[]{:S(2)}, u32[]{:S(2)}) collective-permute-start(bf16[32,4096]{1,0:T(8,128)(2,1)S(1)} %collective-permute-done.18.refs_17_), channel_id=1, source_target_pairs={{0,480},{32,0},{64,32},{96,64},{128,96},{160,128},{192,160},{224,1... | collective-permute-start | bytes 786440 | tf_op jit(solution)/shard_map/ppermute | solution.py:169
  42.6 11.9 %collective-permute-start.11 = (bf16[32,4096]{1,0:T(8,128)(2,1)S(1)}, bf16[32,4096]{1,0:T(8,128)(2,1)S(1)}, u32[]{:S(2)}, u32[]{:S(2)}) collective-permute-start(bf16[32,4096]{1,0:T(8,128)(2,1)S(1)} %collective-permute-done.10.refs_14_), channel_id=1, source_target_pairs={{0,32},{32,64},{64,96},{96,128},{128,160},{160,192},{192,224},{224... | collective-permute-start | bytes 786440 | tf_op jit(solution)/shard_map/ppermute | solution.py:166
  45.9 11.9 %collective-permute-start.27 = (bf16[32,4096]{1,0:T(8,128)(2,1)S(1)}, bf16[32,4096]{1,0:T(8,128)(2,1)S(1)}, u32[]{:S(2)}, u32[]{:S(2)}) collective-permute-start(bf16[32,4096]{1,0:T(8,128)(2,1)S(1)} %collective-permute-done.26.refs_30_), channel_id=1, source_target_pairs={{0,32},{32,64},{64,96},{96,128},{128,160},{160,192},{192,224},{224... | collective-permute-start | bytes 786440 | tf_op jit(solution)/shard_map/ppermute | solution.py:166
  47.8 11.9 %collective-permute-start.4 = (bf16[32,4096]{1,0:T(8,128)(2,1)S(1)}, bf16[32,4096]{1,0:T(8,128)(2,1)S(1)}, u32[]{:S(2)}, u32[]{:S(2)}) collective-permute-start(bf16[32,4096]{1,0:T(8,128)(2,1)S(1)} %collective-permute-done.3.refs_2_), channel_id=1, source_target_pairs={{0,480},{32,0},{64,32},{96,64},{128,96},{160,128},{192,160},{224,1... | collective-permute-start | bytes 786440 | tf_op jit(solution)/shard_map/ppermute | solution.py:169
  52.4 11.9 %collective-permute-start.20 = (bf16[32,4096]{1,0:T(8,128)(2,1)S(1)}, bf16[32,4096]{1,0:T(8,128)(2,1)S(1)}, u32[]{:S(2)}, u32[]{:S(2)}) collective-permute-start(bf16[32,4096]{1,0:T(8,128)(2,1)S(1)} %collective-permute-done.19.refs_18_), channel_id=1, source_target_pairs={{0,480},{32,0},{64,32},{96,64},{128,96},{160,128},{192,160},{224,1... | collective-permute-start | bytes 786440 | tf_op jit(solution)/shard_map/ppermute | solution.py:169
  54.5 12.1 %collective-permute-start.12 = (bf16[32,4096]{1,0:T(8,128)(2,1)S(1)}, bf16[32,4096]{1,0:T(8,128)(2,1)S(1)}, u32[]{:S(2)}, u32[]{:S(2)}) collective-permute-start(bf16[32,4096]{1,0:T(8,128)(2,1)S(1)} %collective-permute-done.11.refs_13_), channel_id=1, source_target_pairs={{0,32},{32,64},{64,96},{96,128},{128,160},{160,192},{192,224},{224... | collective-permute-start | bytes 786440 | tf_op jit(solution)/shard_map/ppermute | solution.py:166
  57.8 11.9 %collective-permute-start.28 = (bf16[32,4096]{1,0:T(8,128)(2,1)S(1)}, bf16[32,4096]{1,0:T(8,128)(2,1)S(1)}, u32[]{:S(2)}, u32[]{:S(2)}) collective-permute-start(bf16[32,4096]{1,0:T(8,128)(2,1)S(1)} %collective-permute-done.27.refs_29_), channel_id=1, source_target_pairs={{0,32},{32,64},{64,96},{96,128},{128,160},{160,192},{192,224},{224... | collective-permute-start | bytes 786440 | tf_op jit(solution)/shard_map/ppermute | solution.py:166
  59.8 11.9 %collective-permute-start.5 = (bf16[32,4096]{1,0:T(8,128)(2,1)S(1)}, bf16[32,4096]{1,0:T(8,128)(2,1)S(1)}, u32[]{:S(2)}, u32[]{:S(2)}) collective-permute-start(bf16[32,4096]{1,0:T(8,128)(2,1)S(1)} %collective-permute-done.4.refs_3_), channel_id=1, source_target_pairs={{0,480},{32,0},{64,32},{96,64},{128,96},{160,128},{192,160},{224,1... | collective-permute-start | bytes 786440 | tf_op jit(solution)/shard_map/ppermute | solution.py:169
  64.4 11.9 %collective-permute-start.21 = (bf16[32,4096]{1,0:T(8,128)(2,1)S(1)}, bf16[32,4096]{1,0:T(8,128)(2,1)S(1)}, u32[]{:S(2)}, u32[]{:S(2)}) collective-permute-start(bf16[32,4096]{1,0:T(8,128)(2,1)S(1)} %collective-permute-done.20.refs_19_), channel_id=1, source_target_pairs={{0,480},{32,0},{64,32},{96,64},{128,96},{160,128},{192,160},{224,1... | collective-permute-start | bytes 786440 | tf_op jit(solution)/shard_map/ppermute | solution.py:169
  66.7 11.9 %collective-permute-start.13 = (bf16[32,4096]{1,0:T(8,128)(2,1)S(1)}, bf16[32,4096]{1,0:T(8,128)(2,1)S(1)}, u32[]{:S(2)}, u32[]{:S(2)}) collective-permute-start(bf16[32,4096]{1,0:T(8,128)(2,1)S(1)} %collective-permute-done.12.refs_12_), channel_id=1, source_target_pairs={{0,32},{32,64},{64,96},{96,128},{128,160},{160,192},{192,224},{224... | collective-permute-start | bytes 786440 | tf_op jit(solution)/shard_map/ppermute | solution.py:166
  69.7 11.9 %collective-permute-start.29 = (bf16[32,4096]{1,0:T(8,128)(2,1)S(1)}, bf16[32,4096]{1,0:T(8,128)(2,1)S(1)}, u32[]{:S(2)}, u32[]{:S(2)}) collective-permute-start(bf16[32,4096]{1,0:T(8,128)(2,1)S(1)} %collective-permute-done.28.refs_28_), channel_id=1, source_target_pairs={{0,32},{32,64},{64,96},{96,128},{128,160},{160,192},{192,224},{224... | collective-permute-start | bytes 786440 | tf_op jit(solution)/shard_map/ppermute | solution.py:166
  71.7 11.9 %collective-permute-start.6 = (bf16[32,4096]{1,0:T(8,128)(2,1)S(1)}, bf16[32,4096]{1,0:T(8,128)(2,1)S(1)}, u32[]{:S(2)}, u32[]{:S(2)}) collective-permute-start(bf16[32,4096]{1,0:T(8,128)(2,1)S(1)} %collective-permute-done.5.refs_4_), channel_id=1, source_target_pairs={{0,480},{32,0},{64,32},{96,64},{128,96},{160,128},{192,160},{224,1... | collective-permute-start | bytes 786440 | tf_op jit(solution)/shard_map/ppermute | solution.py:169
  76.3 11.9 %collective-permute-start.22 = (bf16[32,4096]{1,0:T(8,128)(2,1)S(1)}, bf16[32,4096]{1,0:T(8,128)(2,1)S(1)}, u32[]{:S(2)}, u32[]{:S(2)}) collective-permute-start(bf16[32,4096]{1,0:T(8,128)(2,1)S(1)} %collective-permute-done.21.refs_20_), channel_id=1, source_target_pairs={{0,480},{32,0},{64,32},{96,64},{128,96},{160,128},{192,160},{224,1... | collective-permute-start | bytes 786440 | tf_op jit(solution)/shard_map/ppermute | solution.py:169
  78.6 11.9 %collective-permute-start.14 = (bf16[32,4096]{1,0:T(8,128)(2,1)S(1)}, bf16[32,4096]{1,0:T(8,128)(2,1)S(1)}, u32[]{:S(2)}, u32[]{:S(2)}) collective-permute-start(bf16[32,4096]{1,0:T(8,128)(2,1)S(1)} %collective-permute-done.13.refs_11_), channel_id=1, source_target_pairs={{0,32},{32,64},{64,96},{96,128},{128,160},{160,192},{192,224},{224... | collective-permute-start | bytes 786440 | tf_op jit(solution)/shard_map/ppermute | solution.py:166
  81.7 11.9 %collective-permute-start.30 = (bf16[32,4096]{1,0:T(8,128)(2,1)S(1)}, bf16[32,4096]{1,0:T(8,128)(2,1)S(1)}, u32[]{:S(2)}, u32[]{:S(2)}) collective-permute-start(bf16[32,4096]{1,0:T(8,128)(2,1)S(1)} %collective-permute-done.29.refs_27_), channel_id=1, source_target_pairs={{0,32},{32,64},{64,96},{96,128},{128,160},{160,192},{192,224},{224... | collective-permute-start | bytes 786440 | tf_op jit(solution)/shard_map/ppermute | solution.py:166
  83.6 11.9 %collective-permute-start.7 = (bf16[32,4096]{1,0:T(8,128)(2,1)S(1)}, bf16[32,4096]{1,0:T(8,128)(2,1)}, u32[]{:S(2)}, u32[]{:S(2)}) collective-permute-start(bf16[32,4096]{1,0:T(8,128)(2,1)S(1)} %collective-permute-done.6.refs_5_), channel_id=1, source_target_pairs={{0,480},{32,0},{64,32},{96,64},{128,96},{160,128},{192,160},{224,1... | collective-permute-start | bytes 786440 | tf_op jit(solution)/shard_map/ppermute | solution.py:169
  88.2 11.9 %collective-permute-start.23 = (bf16[32,4096]{1,0:T(8,128)(2,1)S(1)}, bf16[32,4096]{1,0:T(8,128)(2,1)}, u32[]{:S(2)}, u32[]{:S(2)}) collective-permute-start(bf16[32,4096]{1,0:T(8,128)(2,1)S(1)} %collective-permute-done.22.refs_21_), channel_id=1, source_target_pairs={{0,480},{32,0},{64,32},{96,64},{128,96},{160,128},{192,160},{224,1... | collective-permute-start | bytes 786440 | tf_op jit(solution)/shard_map/ppermute | solution.py:169
  90.5 11.9 %collective-permute-start.15 = (bf16[32,4096]{1,0:T(8,128)(2,1)S(1)}, bf16[32,4096]{1,0:T(8,128)(2,1)}, u32[]{:S(2)}, u32[]{:S(2)}) collective-permute-start(bf16[32,4096]{1,0:T(8,128)(2,1)S(1)} %collective-permute-done.14.refs_10_), channel_id=1, source_target_pairs={{0,32},{32,64},{64,96},{96,128},{128,160},{160,192},{192,224},{224... | collective-permute-start | bytes 786440 | tf_op jit(solution)/shard_map/ppermute | solution.py:166
  93.6 11.9 %collective-permute-start.31 = (bf16[32,4096]{1,0:T(8,128)(2,1)S(1)}, bf16[32,4096]{1,0:T(8,128)(2,1)}, u32[]{:S(2)}, u32[]{:S(2)}) collective-permute-start(bf16[32,4096]{1,0:T(8,128)(2,1)S(1)} %collective-permute-done.30.refs_26_), channel_id=1, source_target_pairs={{0,32},{32,64},{64,96},{96,128},{128,160},{160,192},{192,224},{224... | collective-permute-start | bytes 786440 | tf_op jit(solution)/shard_map/ppermute | solution.py:166
  95.5 12.5 %collective-permute-start.8 = (bf16[32,4096]{1,0:T(8,128)(2,1)}, bf16[32,4096]{1,0:T(8,128)(2,1)}, u32[]{:S(2)}, u32[]{:S(2)}) collective-permute-start(bf16[32,4096]{1,0:T(8,128)(2,1)} %collective-permute-done.7.refs_6_), channel_id=1, source_target_pairs={{0,480},{32,0},{64,32},{96,64},{128,96},{160,128},{192,160},{224,1... | collective-permute-start | bytes 786440 | tf_op jit(solution)/shard_map/ppermute | solution.py:169
  102.4 9.3 %collective-permute-start.16 = (bf16[32,4096]{1,0:T(8,128)(2,1)}, bf16[32,4096]{1,0:T(8,128)(2,1)}, u32[]{:S(2)}, u32[]{:S(2)}) collective-permute-start(bf16[32,4096]{1,0:T(8,128)(2,1)} %collective-permute-done.15.refs_9_), channel_id=1, source_target_pairs={{0,32},{32,64},{64,96},{96,128},{128,160},{160,192},{192,224},{224... | collective-permute-start | bytes 786440 | tf_op jit(solution)/shard_map/ppermute | solution.py:166
  133.9 29.2 %all-to-all-start = ((f32[32,1,256]{2,1,0:T(1,128)}), f32[32,1,256]{2,1,0:T(1,128)S(1)}, u32[]{:S(2)}, u32[]{:S(2)}) async-start(f32[32,1,256]{2,1,0:T(1,128)} %bitcast.12), calls=%async_computation | async-start | bytes 65536 | tf_op jit(solution)/shard_map/all_to_all | solution.py:193
  (29 other events, 648.6 us)

commit v6 on v5

--- a/solution.py
+++ b/solution.py
@@ -8,7 +8,7 @@
 
 LANES = 128
 WIDE = 2048
-BATCH = 1024
+BATCH = 4096
 LOAD = 512
 VMEM_MIB = 60
 
@@ -161,12 +161,13 @@
     up = [(i, (i + 1) % size) for i in range(size)]
     down = [(i, (i - 1) % size) for i in range(size)]
     ups, downs = [[[block] for block in blocks] for _ in range(2)]
-    for step in range(size // 2):
+    for _ in range(size // 2 - 1):
         for chain in ups:
             chain.append(lax.ppermute(chain[-1], axis, up))
-        if step < (size - 1) // 2:
-            for chain in downs:
-                chain.append(lax.ppermute(chain[-1], axis, down))
+        for chain in downs:
+            chain.append(lax.ppermute(chain[-1], axis, down))
+    ups[0].append(lax.ppermute(ups[0][-1], axis, up))
+    downs[1].append(lax.ppermute(downs[1][-1], axis, down))
     return [part for one, two in zip(downs, ups) for part in one + two[:0:-1]]
 
 

time: 196 us -> 196 us (level)
    ppermute x16 -> x14, starting transfers between devices: 37.2 us -> 30.3 us  [around(): chain.append(lax.ppermute(chain[-1], axis, up))]
    ppermute x16 -> x14, waiting for transfers between devices: 8.9 us -> 2.03 us  [around(): chain.append(lax.ppermute(chain[-1], axis, up))]
    ppermute x0 -> x2, starting transfers between devices: none -> 6.5 us  [the longest x1 4.57 us: around(): downs[1].append(lax.ppermute(downs[1][-1], axis, down))]
    ppermute x0 -> x2, waiting for transfers between devices: none -> 4.94 us  [the longest x1 3.07 us: around(): downs[1].append(lax.ppermute(downs[1][-1], axis, down))]
    ppermute x14, starting transfers between devices: 51.5 us -> 53.8 us  [around(): chain.append(lax.ppermute(chain[-1], axis, down))]
    ppermute x14, waiting for transfers between devices: 0.31 us -> 2.67 us  [around(): chain.append(lax.ppermute(chain[-1], axis, down))]
  transfers between devices with their start and end apart: 34 -> 34, of which waited for: 6 -> 5; matrix products, arithmetic and copies ran while one was open for 1% -> 1% of each run, Pallas kernels for 0% -> 0%
where the time goes in v6:
time: 196 us; the launch traced here: 195 us
  starting transfers between devices  120 us (61%)
  blocking collectives  30.6 us (16%)
  waiting for transfers between devices  20.9 us (11%)
  Pallas kernels  18.1 us (9%)
  local copies, waits for them, and re-layouts  1.96 us (1%)
    ppermute x14, starting transfers between devices, around(): chain.append(lax.ppermute(chain[-1], axis, down))  53.8 us
    all_to_all x2, blocking collectives, to_all(): lax.all_to_all(jnp.broadcast_to(value[None], (size,) + value.shape), axes...  30.6 us
    ppermute x14, starting transfers between devices, around(): chain.append(lax.ppermute(chain[-1], axis, up))  30.3 us
    pallas_call x1, Pallas kernels, local_samples(): pl.pallas_call(sampled_gradient, grid=(width // WIDE,), out_shape=jax.Sha...  18.1 us
    all_to_all x1, starting transfers between devices, per_device(): lax.all_to_all(terms.reshape(2 * chips, per), ('z', 'core'), 0, 0, tiled=...  16.2 us
    all_to_all x1, waiting for transfers between devices, per_device(): lax.all_to_all(terms.reshape(2 * chips, per), ('z', 'core'), 0, 0, tiled=...  11.2 us
    ppermute x1, starting transfers between devices, per_device(): lax.ppermute(lax.dynamic_index_in_dim(out_grad, 1 - core, 0, keepdims=Fal...  8.79 us
    ppermute x1, starting transfers between devices, around(): downs[1].append(lax.ppermute(downs[1][-1], axis, down))  4.57 us
  transfers between devices with their start and end apart: 34, of which 5 were waited for; matrix products, arithmetic and copies ran while one was open for 1% of the time, Pallas kernels for 0%

profile of v6, /device:TPU:1, one launch (start us, length us, event | category | flops | bytes accessed | tf_op | source)
XLA Modules:
  0.0 194.8 jit_solution(6230124302794752091)
XLA Ops:
  1.7 8.8 %collective-permute-start.17 = (bf16[32,4096]{1,0:T(8,128)(2,1)S(1)}, bf16[32,4096]{1,0:T(8,128)(2,1)S(1)}, u32[]{:S(2)}, u32[]{:S(2)}) collective-permute-start(bf16[32,4096]{1,0:T(8,128)(2,1)S(1)} %get-tuple-element.2), channel_id=1, source_target_pairs={{0,16},{16,0},{1,17},{17,1},{2,18},{18,2},{3,19},{19,3},{4,20},{20... | collective-permute-start | bytes 786440 | tf_op jit(solution)/shard_map/ppermute | solution.py:186
  12.4 5.7 %collective-permute-start.2 = (bf16[32,4096]{1,0:T(8,128)(2,1)S(1)}, bf16[32,4096]{1,0:T(8,128)(2,1)S(1)}, u32[]{:S(2)}, u32[]{:S(2)}) collective-permute-start(bf16[32,4096]{1,0:T(8,128)(2,1)S(1)} %get-tuple-element.3.refs_0_), channel_id=1, source_target_pairs={{0,480},{32,0},{64,32},{96,64},{128,96},{160,128},{192,160},{224,1... | collective-permute-start | bytes 786440 | tf_op jit(solution)/shard_map/ppermute | solution.py:168
  18.2 1.9 collective-permute-start.26
  20.1 4.6 %collective-permute-start.18 = (bf16[32,4096]{1,0:T(8,128)(2,1)S(1)}, bf16[32,4096]{1,0:T(8,128)(2,1)S(1)}, u32[]{:S(2)}, u32[]{:S(2)}) collective-permute-start(bf16[32,4096]{1,0:T(8,128)(2,1)S(1)} %collective-permute-done.17.refs_16_), channel_id=1, source_target_pairs={{0,480},{32,0},{64,32},{96,64},{128,96},{160,128},{192,160},{224,1... | collective-permute-start | bytes 786440 | tf_op jit(solution)/shard_map/ppermute | solution.py:168
  24.7 2.8 %collective-permute-start.1 = (s32[128,4096]{1,0:T(8,128)}, s32[128,4096]{1,0:T(8,128)S(1)}, u32[]{:S(2)}, u32[]{:S(2)}) collective-permute-start(s32[128,4096]{1,0:T(8,128)} %near_ref.1), channel_id=1, source_target_pairs={{0,16},{16,0},{1,17},{17,1},{2,18},{18,2},{3,19},{19,3},{4,20},{20... | collective-permute-start | bytes 6291464 | tf_op jit(solution)/shard_map/ppermute | solution.py:188
  27.5 1.9 collective-permute-start
  31.4 4.6 %collective-permute-start.3 = (bf16[32,4096]{1,0:T(8,128)(2,1)S(1)}, bf16[32,4096]{1,0:T(8,128)(2,1)S(1)}, u32[]{:S(2)}, u32[]{:S(2)}) collective-permute-start(bf16[32,4096]{1,0:T(8,128)(2,1)S(1)} %collective-permute-done.2.refs_1_), channel_id=1, source_target_pairs={{0,480},{32,0},{64,32},{96,64},{128,96},{160,128},{192,160},{224,1... | collective-permute-start | bytes 786440 | tf_op jit(solution)/shard_map/ppermute | solution.py:168
  37.9 2.0 %collective-permute-done.10.refs_14_ = bf16[32,4096]{1,0:T(8,128)(2,1)S(1)} collective-permute-done((bf16[32,4096]{1,0:T(8,128)(2,1)S(1)}, bf16[32,4096]{1,0:T(8,128)(2,1)S(1)}, u32[]{:S(2)}, u32[]{:S(2)}) %collective-permute-start.10) | collective-permute-done | bytes 262176 | tf_op jit(solution)/shard_map/ppermute | solution.py:166
  43.8 2.6 %collective-permute-done.19.refs_18_ = bf16[32,4096]{1,0:T(8,128)(2,1)S(1)} collective-permute-done((bf16[32,4096]{1,0:T(8,128)(2,1)S(1)}, bf16[32,4096]{1,0:T(8,128)(2,1)S(1)}, u32[]{:S(2)}, u32[]{:S(2)}) %collective-permute-start.19) | collective-permute-done | bytes 262176 | tf_op jit(solution)/shard_map/ppermute | solution.py:168
  46.4 5.3 %collective-permute-start.20 = (bf16[32,4096]{1,0:T(8,128)(2,1)S(1)}, bf16[32,4096]{1,0:T(8,128)(2,1)S(1)}, u32[]{:S(2)}, u32[]{:S(2)}) collective-permute-start(bf16[32,4096]{1,0:T(8,128)(2,1)S(1)} %collective-permute-done.19.refs_18_), channel_id=1, source_target_pairs={{0,480},{32,0},{64,32},{96,64},{128,96},{160,128},{192,160},{224,1... | collective-permute-start | bytes 786440 | tf_op jit(solution)/shard_map/ppermute | solution.py:168
  53.8 3.4 %collective-permute-start.28 = (bf16[32,4096]{1,0:T(8,128)(2,1)S(1)}, bf16[32,4096]{1,0:T(8,128)(2,1)S(1)}, u32[]{:S(2)}, u32[]{:S(2)}) collective-permute-start(bf16[32,4096]{1,0:T(8,128)(2,1)S(1)} %collective-permute-done.27.refs_30_), channel_id=1, source_target_pairs={{0,32},{32,64},{64,96},{96,128},{128,160},{160,192},{192,224},{224... | collective-permute-start | bytes 786440 | tf_op jit(solution)/shard_map/ppermute | solution.py:166
  59.1 4.6 %collective-permute-start.21 = (bf16[32,4096]{1,0:T(8,128)(2,1)S(1)}, bf16[32,4096]{1,0:T(8,128)(2,1)S(1)}, u32[]{:S(2)}, u32[]{:S(2)}) collective-permute-start(bf16[32,4096]{1,0:T(8,128)(2,1)S(1)} %collective-permute-done.20.refs_19_), channel_id=1, source_target_pairs={{0,480},{32,0},{64,32},{96,64},{128,96},{160,128},{192,160},{224,1... | collective-permute-start | bytes 786440 | tf_op jit(solution)/shard_map/ppermute | solution.py:168
  63.7 2.9 %collective-permute-start.5 = (bf16[32,4096]{1,0:T(8,128)(2,1)S(1)}, bf16[32,4096]{1,0:T(8,128)(2,1)S(1)}, u32[]{:S(2)}, u32[]{:S(2)}) collective-permute-start(bf16[32,4096]{1,0:T(8,128)(2,1)S(1)} %collective-permute-done.4.refs_3_), channel_id=1, source_target_pairs={{0,480},{32,0},{64,32},{96,64},{128,96},{160,128},{192,160},{224,1... | collective-permute-start | bytes 786440 | tf_op jit(solution)/shard_map/ppermute | solution.py:168
  66.7 2.4 %collective-permute-start.29 = (bf16[32,4096]{1,0:T(8,128)(2,1)S(1)}, bf16[32,4096]{1,0:T(8,128)(2,1)S(1)}, u32[]{:S(2)}, u32[]{:S(2)}) collective-permute-start(bf16[32,4096]{1,0:T(8,128)(2,1)S(1)} %collective-permute-done.28.refs_29_), channel_id=1, source_target_pairs={{0,32},{32,64},{64,96},{96,128},{128,160},{160,192},{192,224},{224... | collective-permute-start | bytes 786440 | tf_op jit(solution)/shard_map/ppermute | solution.py:166
  71.1 4.6 %collective-permute-start.22 = (bf16[32,4096]{1,0:T(8,128)(2,1)S(1)}, bf16[32,4096]{1,0:T(8,128)(2,1)S(1)}, u32[]{:S(2)}, u32[]{:S(2)}) collective-permute-start(bf16[32,4096]{1,0:T(8,128)(2,1)S(1)} %collective-permute-done.21.refs_20_), channel_id=1, source_target_pairs={{0,480},{32,0},{64,32},{96,64},{128,96},{160,128},{192,160},{224,1... | collective-permute-start | bytes 786440 | tf_op jit(solution)/shard_map/ppermute | solution.py:168
  75.7 2.9 %collective-permute-start.6 = (bf16[32,4096]{1,0:T(8,128)(2,1)S(1)}, bf16[32,4096]{1,0:T(8,128)(2,1)S(1)}, u32[]{:S(2)}, u32[]{:S(2)}) collective-permute-start(bf16[32,4096]{1,0:T(8,128)(2,1)S(1)} %collective-permute-done.5.refs_4_), channel_id=1, source_target_pairs={{0,480},{32,0},{64,32},{96,64},{128,96},{160,128},{192,160},{224,1... | collective-permute-start | bytes 786440 | tf_op jit(solution)/shard_map/ppermute | solution.py:168
  78.6 2.4 %collective-permute-start.30 = (bf16[32,4096]{1,0:T(8,128)(2,1)S(1)}, bf16[32,4096]{1,0:T(8,128)(2,1)S(1)}, u32[]{:S(2)}, u32[]{:S(2)}) collective-permute-start(bf16[32,4096]{1,0:T(8,128)(2,1)S(1)} %collective-permute-done.29.refs_28_), channel_id=1, source_target_pairs={{0,32},{32,64},{64,96},{96,128},{128,160},{160,192},{192,224},{224... | collective-permute-start | bytes 786440 | tf_op jit(solution)/shard_map/ppermute | solution.py:166
  83.0 4.6 %collective-permute-start.23 = (bf16[32,4096]{1,0:T(8,128)(2,1)S(1)}, bf16[32,4096]{1,0:T(8,128)(2,1)S(1)}, u32[]{:S(2)}, u32[]{:S(2)}) collective-permute-start(bf16[32,4096]{1,0:T(8,128)(2,1)S(1)} %collective-permute-done.22.refs_21_), channel_id=1, source_target_pairs={{0,480},{32,0},{64,32},{96,64},{128,96},{160,128},{192,160},{224,1... | collective-permute-start | bytes 786440 | tf_op jit(solution)/shard_map/ppermute | solution.py:168
  87.6 2.9 %collective-permute-start.7 = (bf16[32,4096]{1,0:T(8,128)(2,1)S(1)}, bf16[32,4096]{1,0:T(8,128)(2,1)}, u32[]{:S(2)}, u32[]{:S(2)}) collective-permute-start(bf16[32,4096]{1,0:T(8,128)(2,1)S(1)} %collective-permute-done.6.refs_5_), channel_id=1, source_target_pairs={{0,480},{32,0},{64,32},{96,64},{128,96},{160,128},{192,160},{224,1... | collective-permute-start | bytes 786440 | tf_op jit(solution)/shard_map/ppermute | solution.py:168
  90.5 2.4 %collective-permute-start.31 = (bf16[32,4096]{1,0:T(8,128)(2,1)S(1)}, bf16[32,4096]{1,0:T(8,128)(2,1)}, u32[]{:S(2)}, u32[]{:S(2)}) collective-permute-start(bf16[32,4096]{1,0:T(8,128)(2,1)S(1)} %collective-permute-done.30.refs_27_), channel_id=1, source_target_pairs={{0,32},{32,64},{64,96},{96,128},{128,160},{160,192},{192,224},{224... | collective-permute-start | bytes 786440 | tf_op jit(solution)/shard_map/ppermute | solution.py:166
  93.0 1.9 collective-permute-start.15
  94.9 4.6 %collective-permute-start.24 = (bf16[32,4096]{1,0:T(8,128)(2,1)S(1)}, bf16[32,4096]{1,0:T(8,128)(2,1)}, u32[]{:S(2)}, u32[]{:S(2)}) collective-permute-start(bf16[32,4096]{1,0:T(8,128)(2,1)S(1)} %collective-permute-done.23.refs_22_), channel_id=1, source_target_pairs={{0,480},{32,0},{64,32},{96,64},{128,96},{160,128},{192,160},{224,1... | collective-permute-start | bytes 786440 | tf_op jit(solution)/shard_map/ppermute | solution.py:168
  99.5 2.9 %collective-permute-start.8 = (bf16[32,4096]{1,0:T(8,128)(2,1)}, bf16[32,4096]{1,0:T(8,128)(2,1)}, u32[]{:S(2)}, u32[]{:S(2)}) collective-permute-start(bf16[32,4096]{1,0:T(8,128)(2,1)} %collective-permute-done.7.refs_6_), channel_id=1, source_target_pairs={{0,480},{32,0},{64,32},{96,64},{128,96},{160,128},{192,160},{224,1... | collective-permute-start | bytes 786440 | tf_op jit(solution)/shard_map/ppermute | solution.py:168
  102.4 2.4 %collective-permute-start.32 = (bf16[32,4096]{1,0:T(8,128)(2,1)}, bf16[32,4096]{1,0:T(8,128)(2,1)}, u32[]{:S(2)}, u32[]{:S(2)}) collective-permute-start(bf16[32,4096]{1,0:T(8,128)(2,1)} %collective-permute-done.31.refs_26_), channel_id=1, source_target_pairs={{0,32},{32,64},{64,96},{96,128},{128,160},{160,192},{192,224},{224... | collective-permute-start | bytes 786440 | tf_op jit(solution)/shard_map/ppermute | solution.py:166
  104.9 1.9 collective-permute-start.16
  106.8 4.6 %collective-permute-start.25 = (bf16[32,4096]{1,0:T(8,128)(2,1)}, bf16[32,4096]{1,0:T(8,128)(2,1)}, u32[]{:S(2)}, u32[]{:S(2)}) collective-permute-start(bf16[32,4096]{1,0:T(8,128)(2,1)} %collective-permute-done.24.refs_23_), channel_id=1, source_target_pairs={{0,480},{32,0},{64,32},{96,64},{128,96},{160,128},{192,160},{224,1... | collective-permute-start | bytes 786440 | tf_op jit(solution)/shard_map/ppermute | solution.py:170
  113.9 3.1 %collective-permute-done.25.refs_24_ = bf16[32,4096]{1,0:T(8,128)(2,1)} collective-permute-done((bf16[32,4096]{1,0:T(8,128)(2,1)}, bf16[32,4096]{1,0:T(8,128)(2,1)}, u32[]{:S(2)}, u32[]{:S(2)}) %collective-permute-start.25) | collective-permute-done | bytes 262176 | tf_op jit(solution)/shard_map/ppermute | solution.py:170
  117.0 18.1 %sampled_gradient.1 = f32[64,128]{1,0:T(8,128)} custom-call(s32[2]{0:T(128)} %pad_add_fusion.place_ref, s32[64,128]{1,0:T(8,128)} %bitcast.13, bf16[2,1024,128]{2,1,0:T(8,128)(2,1)} %near_act_ref.1, bf16[2,1024,128]{2,1,0:T(8,128)(2,1)} %copy-done.2, s32[128,4096]{1,0:T(8,128)} %copy-done, bf16[2,256,512]{2,1,0:T(8,128)(2,1)} %constant.41.clone.table_ref, ...), custom_call_target="tpu_custom_call" | custom-call | tf_op jit(solution)/shard_map/sampled_gradient/pallas_call | solution.py:126
  135.1 16.2 %all-to-all-start = ((f32[32,1,256]{2,1,0:T(1,128)}), f32[32,1,256]{2,1,0:T(1,128)S(1)}, u32[]{:S(2)}, u32[]{:S(2)}) async-start(f32[32,1,256]{2,1,0:T(1,128)} %bitcast.12), calls=%async_computation | async-start | bytes 65536 | tf_op jit(solution)/shard_map/all_to_all | solution.py:194
  152.0 11.2 %all-to-all-done = f32[32,1,256]{2,1,0:T(1,128)S(1)} async-done(((f32[32,1,256]{2,1,0:T(1,128)}), f32[32,1,256]{2,1,0:T(1,128)S(1)}, u32[]{:S(2)}, u32[]{:S(2)}) %all-to-all-start) | async-done | bytes 32800 | tf_op jit(solution)/shard_map/all_to_all | solution.py:194
  163.4 13.0 %all_to_all.19 = f32[16,2,256]{2,1,0:T(2,128)S(1)} all-to-all(f32[16,2,256]{2,1,0:T(2,128)S(1)} %broadcast_in_dim.4), channel_id=1, replica_groups=mesh['z'=16,'core'=2,'ex'=16] {'ex'}, dimensions={0} | all-to-all | bytes 65536 | tf_op jit(solution)/shard_map/all_to_all | solution.py:176
  176.6 17.6 %all_to_all.20 = f32[32,2,32]{2,1,0:T(2,128)S(1)} all-to-all(f32[32,2,32]{2,1,0:T(2,128)S(1)} %broadcast_in_dim.5), channel_id=1, replica_groups=mesh['z'=16,'core'=2,'ex'=16] {'z','core'}, dimensions={0} | all-to-all | bytes 16384 | tf_op jit(solution)/shard_map/all_to_all | solution.py:176
  (106 shorter events, 22.7 us)
Async XLA Ops:
  1.7 16.5 %collective-permute-start.17 = (bf16[32,4096]{1,0:T(8,128)(2,1)S(1)}, bf16[32,4096]{1,0:T(8,128)(2,1)S(1)}, u32[]{:S(2)}, u32[]{:S(2)}) collective-permute-start(bf16[32,4096]{1,0:T(8,128)(2,1)S(1)} %get-tuple-element.2), channel_id=1, source_target_pairs={{0,16},{16,0},{1,17},{17,1},{2,18},{18,2},{3,19},{19,3},{4,20},{20... | collective-permute-start | bytes 786440 | tf_op jit(solution)/shard_map/ppermute | solution.py:186
  10.5 17.0 %collective-permute-start.9 = (bf16[32,4096]{1,0:T(8,128)(2,1)S(1)}, bf16[32,4096]{1,0:T(8,128)(2,1)S(1)}, u32[]{:S(2)}, u32[]{:S(2)}) collective-permute-start(bf16[32,4096]{1,0:T(8,128)(2,1)S(1)} %get-tuple-element.3.refs_0_), channel_id=1, source_target_pairs={{0,32},{32,64},{64,96},{96,128},{128,160},{160,192},{192,224},{224... | collective-permute-start | bytes 786440 | tf_op jit(solution)/shard_map/ppermute | solution.py:166
  12.4 17.0 %collective-permute-start.2 = (bf16[32,4096]{1,0:T(8,128)(2,1)S(1)}, bf16[32,4096]{1,0:T(8,128)(2,1)S(1)}, u32[]{:S(2)}, u32[]{:S(2)}) collective-permute-start(bf16[32,4096]{1,0:T(8,128)(2,1)S(1)} %get-tuple-element.3.refs_0_), channel_id=1, source_target_pairs={{0,480},{32,0},{64,32},{96,64},{128,96},{160,128},{192,160},{224,1... | collective-permute-start | bytes 786440 | tf_op jit(solution)/shard_map/ppermute | solution.py:168
  18.2 13.2 %collective-permute-start.26 = (bf16[32,4096]{1,0:T(8,128)(2,1)S(1)}, bf16[32,4096]{1,0:T(8,128)(2,1)S(1)}, u32[]{:S(2)}, u32[]{:S(2)}) collective-permute-start(bf16[32,4096]{1,0:T(8,128)(2,1)S(1)} %collective-permute-done.17.refs_16_), channel_id=1, source_target_pairs={{0,32},{32,64},{64,96},{96,128},{128,160},{160,192},{192,224},{224... | collective-permute-start | bytes 786440 | tf_op jit(solution)/shard_map/ppermute | solution.py:166
  20.1 15.9 %collective-permute-start.18 = (bf16[32,4096]{1,0:T(8,128)(2,1)S(1)}, bf16[32,4096]{1,0:T(8,128)(2,1)S(1)}, u32[]{:S(2)}, u32[]{:S(2)}) collective-permute-start(bf16[32,4096]{1,0:T(8,128)(2,1)S(1)} %collective-permute-done.17.refs_16_), channel_id=1, source_target_pairs={{0,480},{32,0},{64,32},{96,64},{128,96},{160,128},{192,160},{224,1... | collective-permute-start | bytes 786440 | tf_op jit(solution)/shard_map/ppermute | solution.py:168
  24.7 89.2 %collective-permute-start.1 = (s32[128,4096]{1,0:T(8,128)}, s32[128,4096]{1,0:T(8,128)S(1)}, u32[]{:S(2)}, u32[]{:S(2)}) collective-permute-start(s32[128,4096]{1,0:T(8,128)} %near_ref.1), channel_id=1, source_target_pairs={{0,16},{16,0},{1,17},{17,1},{2,18},{18,2},{3,19},{19,3},{4,20},{20... | collective-permute-start | bytes 6291464 | tf_op jit(solution)/shard_map/ppermute | solution.py:188
  27.5 24.2 %collective-permute-start = (bf16[2,1024,128]{2,1,0:T(8,128)(2,1)}, bf16[2,1024,128]{2,1,0:T(8,128)(2,1)S(1)}, u32[]{:S(2)}, u32[]{:S(2)}) collective-permute-start(bf16[2,1024,128]{2,1,0:T(8,128)(2,1)} %near_act_ref.1), channel_id=1, source_target_pairs={{0,16},{16,0},{1,17},{17,1},{2,18},{18,2},{3,19},{19,3},{4,20},{20... | collective-permute-start | bytes 1572872 | tf_op jit(solution)/shard_map/ppermute | solution.py:187
  29.5 10.5 %collective-permute-start.10 = (bf16[32,4096]{1,0:T(8,128)(2,1)S(1)}, bf16[32,4096]{1,0:T(8,128)(2,1)S(1)}, u32[]{:S(2)}, u32[]{:S(2)}) collective-permute-start(bf16[32,4096]{1,0:T(8,128)(2,1)S(1)} %collective-permute-done.9.refs_15_), channel_id=1, source_target_pairs={{0,32},{32,64},{64,96},{96,128},{128,160},{160,192},{192,224},{224... | collective-permute-start | bytes 786440 | tf_op jit(solution)/shard_map/ppermute | solution.py:166
  31.4 10.4 %collective-permute-start.3 = (bf16[32,4096]{1,0:T(8,128)(2,1)S(1)}, bf16[32,4096]{1,0:T(8,128)(2,1)S(1)}, u32[]{:S(2)}, u32[]{:S(2)}) collective-permute-start(bf16[32,4096]{1,0:T(8,128)(2,1)S(1)} %collective-permute-done.2.refs_1_), channel_id=1, source_target_pairs={{0,480},{32,0},{64,32},{96,64},{128,96},{160,128},{192,160},{224,1... | collective-permute-start | bytes 786440 | tf_op jit(solution)/shard_map/ppermute | solution.py:168
  36.0 10.4 %collective-permute-start.19 = (bf16[32,4096]{1,0:T(8,128)(2,1)S(1)}, bf16[32,4096]{1,0:T(8,128)(2,1)S(1)}, u32[]{:S(2)}, u32[]{:S(2)}) collective-permute-start(bf16[32,4096]{1,0:T(8,128)(2,1)S(1)} %collective-permute-done.18.refs_17_), channel_id=1, source_target_pairs={{0,480},{32,0},{64,32},{96,64},{128,96},{160,128},{192,160},{224,1... | collective-permute-start | bytes 786440 | tf_op jit(solution)/shard_map/ppermute | solution.py:168
  39.9 13.8 %collective-permute-start.27 = (bf16[32,4096]{1,0:T(8,128)(2,1)S(1)}, bf16[32,4096]{1,0:T(8,128)(2,1)S(1)}, u32[]{:S(2)}, u32[]{:S(2)}) collective-permute-start(bf16[32,4096]{1,0:T(8,128)(2,1)S(1)} %collective-permute-done.26.refs_31_), channel_id=1, source_target_pairs={{0,32},{32,64},{64,96},{96,128},{128,160},{160,192},{192,224},{224... | collective-permute-start | bytes 786440 | tf_op jit(solution)/shard_map/ppermute | solution.py:166
  41.9 15.3 %collective-permute-start.11 = (bf16[32,4096]{1,0:T(8,128)(2,1)S(1)}, bf16[32,4096]{1,0:T(8,128)(2,1)S(1)}, u32[]{:S(2)}, u32[]{:S(2)}) collective-permute-start(bf16[32,4096]{1,0:T(8,128)(2,1)S(1)} %collective-permute-done.10.refs_14_), channel_id=1, source_target_pairs={{0,32},{32,64},{64,96},{96,128},{128,160},{160,192},{192,224},{224... | collective-permute-start | bytes 786440 | tf_op jit(solution)/shard_map/ppermute | solution.py:166
  46.4 12.7 %collective-permute-start.20 = (bf16[32,4096]{1,0:T(8,128)(2,1)S(1)}, bf16[32,4096]{1,0:T(8,128)(2,1)S(1)}, u32[]{:S(2)}, u32[]{:S(2)}) collective-permute-start(bf16[32,4096]{1,0:T(8,128)(2,1)S(1)} %collective-permute-done.19.refs_18_), channel_id=1, source_target_pairs={{0,480},{32,0},{64,32},{96,64},{128,96},{160,128},{192,160},{224,1... | collective-permute-start | bytes 786440 | tf_op jit(solution)/shard_map/ppermute | solution.py:168
  51.8 11.9 %collective-permute-start.4 = (bf16[32,4096]{1,0:T(8,128)(2,1)S(1)}, bf16[32,4096]{1,0:T(8,128)(2,1)S(1)}, u32[]{:S(2)}, u32[]{:S(2)}) collective-permute-start(bf16[32,4096]{1,0:T(8,128)(2,1)S(1)} %collective-permute-done.3.refs_2_), channel_id=1, source_target_pairs={{0,480},{32,0},{64,32},{96,64},{128,96},{160,128},{192,160},{224,1... | collective-permute-start | bytes 786440 | tf_op jit(solution)/shard_map/ppermute | solution.py:168
  53.8 12.9 %collective-permute-start.28 = (bf16[32,4096]{1,0:T(8,128)(2,1)S(1)}, bf16[32,4096]{1,0:T(8,128)(2,1)S(1)}, u32[]{:S(2)}, u32[]{:S(2)}) collective-permute-start(bf16[32,4096]{1,0:T(8,128)(2,1)S(1)} %collective-permute-done.27.refs_30_), channel_id=1, source_target_pairs={{0,32},{32,64},{64,96},{96,128},{128,160},{160,192},{192,224},{224... | collective-permute-start | bytes 786440 | tf_op jit(solution)/shard_map/ppermute | solution.py:166
  57.2 11.9 %collective-permute-start.12 = (bf16[32,4096]{1,0:T(8,128)(2,1)S(1)}, bf16[32,4096]{1,0:T(8,128)(2,1)S(1)}, u32[]{:S(2)}, u32[]{:S(2)}) collective-permute-start(bf16[32,4096]{1,0:T(8,128)(2,1)S(1)} %collective-permute-done.11.refs_13_), channel_id=1, source_target_pairs={{0,32},{32,64},{64,96},{96,128},{128,160},{160,192},{192,224},{224... | collective-permute-start | bytes 786440 | tf_op jit(solution)/shard_map/ppermute | solution.py:166
  59.1 11.9 %collective-permute-start.21 = (bf16[32,4096]{1,0:T(8,128)(2,1)S(1)}, bf16[32,4096]{1,0:T(8,128)(2,1)S(1)}, u32[]{:S(2)}, u32[]{:S(2)}) collective-permute-start(bf16[32,4096]{1,0:T(8,128)(2,1)S(1)} %collective-permute-done.20.refs_19_), channel_id=1, source_target_pairs={{0,480},{32,0},{64,32},{96,64},{128,96},{160,128},{192,160},{224,1... | collective-permute-start | bytes 786440 | tf_op jit(solution)/shard_map/ppermute | solution.py:168
  63.7 11.9 %collective-permute-start.5 = (bf16[32,4096]{1,0:T(8,128)(2,1)S(1)}, bf16[32,4096]{1,0:T(8,128)(2,1)S(1)}, u32[]{:S(2)}, u32[]{:S(2)}) collective-permute-start(bf16[32,4096]{1,0:T(8,128)(2,1)S(1)} %collective-permute-done.4.refs_3_), channel_id=1, source_target_pairs={{0,480},{32,0},{64,32},{96,64},{128,96},{160,128},{192,160},{224,1... | collective-permute-start | bytes 786440 | tf_op jit(solution)/shard_map/ppermute | solution.py:168
  66.7 11.9 %collective-permute-start.29 = (bf16[32,4096]{1,0:T(8,128)(2,1)S(1)}, bf16[32,4096]{1,0:T(8,128)(2,1)S(1)}, u32[]{:S(2)}, u32[]{:S(2)}) collective-permute-start(bf16[32,4096]{1,0:T(8,128)(2,1)S(1)} %collective-permute-done.28.refs_29_), channel_id=1, source_target_pairs={{0,32},{32,64},{64,96},{96,128},{128,160},{160,192},{192,224},{224... | collective-permute-start | bytes 786440 | tf_op jit(solution)/shard_map/ppermute | solution.py:166
  69.1 11.9 %collective-permute-start.13 = (bf16[32,4096]{1,0:T(8,128)(2,1)S(1)}, bf16[32,4096]{1,0:T(8,128)(2,1)S(1)}, u32[]{:S(2)}, u32[]{:S(2)}) collective-permute-start(bf16[32,4096]{1,0:T(8,128)(2,1)S(1)} %collective-permute-done.12.refs_12_), channel_id=1, source_target_pairs={{0,32},{32,64},{64,96},{96,128},{128,160},{160,192},{192,224},{224... | collective-permute-start | bytes 786440 | tf_op jit(solution)/shard_map/ppermute | solution.py:166
  71.1 11.9 %collective-permute-start.22 = (bf16[32,4096]{1,0:T(8,128)(2,1)S(1)}, bf16[32,4096]{1,0:T(8,128)(2,1)S(1)}, u32[]{:S(2)}, u32[]{:S(2)}) collective-permute-start(bf16[32,4096]{1,0:T(8,128)(2,1)S(1)} %collective-permute-done.21.refs_20_), channel_id=1, source_target_pairs={{0,480},{32,0},{64,32},{96,64},{128,96},{160,128},{192,160},{224,1... | collective-permute-start | bytes 786440 | tf_op jit(solution)/shard_map/ppermute | solution.py:168
  75.7 11.9 %collective-permute-start.6 = (bf16[32,4096]{1,0:T(8,128)(2,1)S(1)}, bf16[32,4096]{1,0:T(8,128)(2,1)S(1)}, u32[]{:S(2)}, u32[]{:S(2)}) collective-permute-start(bf16[32,4096]{1,0:T(8,128)(2,1)S(1)} %collective-permute-done.5.refs_4_), channel_id=1, source_target_pairs={{0,480},{32,0},{64,32},{96,64},{128,96},{160,128},{192,160},{224,1... | collective-permute-start | bytes 786440 | tf_op jit(solution)/shard_map/ppermute | solution.py:168
  78.6 11.9 %collective-permute-start.30 = (bf16[32,4096]{1,0:T(8,128)(2,1)S(1)}, bf16[32,4096]{1,0:T(8,128)(2,1)S(1)}, u32[]{:S(2)}, u32[]{:S(2)}) collective-permute-start(bf16[32,4096]{1,0:T(8,128)(2,1)S(1)} %collective-permute-done.29.refs_28_), channel_id=1, source_target_pairs={{0,32},{32,64},{64,96},{96,128},{128,160},{160,192},{192,224},{224... | collective-permute-start | bytes 786440 | tf_op jit(solution)/shard_map/ppermute | solution.py:166
  81.0 11.9 %collective-permute-start.14 = (bf16[32,4096]{1,0:T(8,128)(2,1)S(1)}, bf16[32,4096]{1,0:T(8,128)(2,1)S(1)}, u32[]{:S(2)}, u32[]{:S(2)}) collective-permute-start(bf16[32,4096]{1,0:T(8,128)(2,1)S(1)} %collective-permute-done.13.refs_11_), channel_id=1, source_target_pairs={{0,32},{32,64},{64,96},{96,128},{128,160},{160,192},{192,224},{224... | collective-permute-start | bytes 786440 | tf_op jit(solution)/shard_map/ppermute | solution.py:166
  83.0 11.9 %collective-permute-start.23 = (bf16[32,4096]{1,0:T(8,128)(2,1)S(1)}, bf16[32,4096]{1,0:T(8,128)(2,1)S(1)}, u32[]{:S(2)}, u32[]{:S(2)}) collective-permute-start(bf16[32,4096]{1,0:T(8,128)(2,1)S(1)} %collective-permute-done.22.refs_21_), channel_id=1, source_target_pairs={{0,480},{32,0},{64,32},{96,64},{128,96},{160,128},{192,160},{224,1... | collective-permute-start | bytes 786440 | tf_op jit(solution)/shard_map/ppermute | solution.py:168
  87.6 11.9 %collective-permute-start.7 = (bf16[32,4096]{1,0:T(8,128)(2,1)S(1)}, bf16[32,4096]{1,0:T(8,128)(2,1)}, u32[]{:S(2)}, u32[]{:S(2)}) collective-permute-start(bf16[32,4096]{1,0:T(8,128)(2,1)S(1)} %collective-permute-done.6.refs_5_), channel_id=1, source_target_pairs={{0,480},{32,0},{64,32},{96,64},{128,96},{160,128},{192,160},{224,1... | collective-permute-start | bytes 786440 | tf_op jit(solution)/shard_map/ppermute | solution.py:168
  90.5 11.9 %collective-permute-start.31 = (bf16[32,4096]{1,0:T(8,128)(2,1)S(1)}, bf16[32,4096]{1,0:T(8,128)(2,1)}, u32[]{:S(2)}, u32[]{:S(2)}) collective-permute-start(bf16[32,4096]{1,0:T(8,128)(2,1)S(1)} %collective-permute-done.30.refs_27_), channel_id=1, source_target_pairs={{0,32},{32,64},{64,96},{96,128},{128,160},{160,192},{192,224},{224... | collective-permute-start | bytes 786440 | tf_op jit(solution)/shard_map/ppermute | solution.py:166
  93.0 11.9 %collective-permute-start.15 = (bf16[32,4096]{1,0:T(8,128)(2,1)S(1)}, bf16[32,4096]{1,0:T(8,128)(2,1)}, u32[]{:S(2)}, u32[]{:S(2)}) collective-permute-start(bf16[32,4096]{1,0:T(8,128)(2,1)S(1)} %collective-permute-done.14.refs_10_), channel_id=1, source_target_pairs={{0,32},{32,64},{64,96},{96,128},{128,160},{160,192},{192,224},{224... | collective-permute-start | bytes 786440 | tf_op jit(solution)/shard_map/ppermute | solution.py:166
  94.9 11.9 %collective-permute-start.24 = (bf16[32,4096]{1,0:T(8,128)(2,1)S(1)}, bf16[32,4096]{1,0:T(8,128)(2,1)}, u32[]{:S(2)}, u32[]{:S(2)}) collective-permute-start(bf16[32,4096]{1,0:T(8,128)(2,1)S(1)} %collective-permute-done.23.refs_22_), channel_id=1, source_target_pairs={{0,480},{32,0},{64,32},{96,64},{128,96},{160,128},{192,160},{224,1... | collective-permute-start | bytes 786440 | tf_op jit(solution)/shard_map/ppermute | solution.py:168
  99.5 12.5 %collective-permute-start.8 = (bf16[32,4096]{1,0:T(8,128)(2,1)}, bf16[32,4096]{1,0:T(8,128)(2,1)}, u32[]{:S(2)}, u32[]{:S(2)}) collective-permute-start(bf16[32,4096]{1,0:T(8,128)(2,1)} %collective-permute-done.7.refs_6_), channel_id=1, source_target_pairs={{0,480},{32,0},{64,32},{96,64},{128,96},{160,128},{192,160},{224,1... | collective-permute-start | bytes 786440 | tf_op jit(solution)/shard_map/ppermute | solution.py:168
  106.8 10.1 %collective-permute-start.25 = (bf16[32,4096]{1,0:T(8,128)(2,1)}, bf16[32,4096]{1,0:T(8,128)(2,1)}, u32[]{:S(2)}, u32[]{:S(2)}) collective-permute-start(bf16[32,4096]{1,0:T(8,128)(2,1)} %collective-permute-done.24.refs_23_), channel_id=1, source_target_pairs={{0,480},{32,0},{64,32},{96,64},{128,96},{160,128},{192,160},{224,1... | collective-permute-start | bytes 786440 | tf_op jit(solution)/shard_map/ppermute | solution.py:170
  135.1 28.1 %all-to-all-start = ((f32[32,1,256]{2,1,0:T(1,128)}), f32[32,1,256]{2,1,0:T(1,128)S(1)}, u32[]{:S(2)}, u32[]{:S(2)}) async-start(f32[32,1,256]{2,1,0:T(1,128)} %bitcast.12), calls=%async_computation | async-start | bytes 65536 | tf_op jit(solution)/shard_map/all_to_all | solution.py:194
  (29 other events, 673.4 us)

commit v7 on v6

--- a/solution.py
+++ b/solution.py
@@ -57,8 +57,8 @@
     value = jnp.dot(act[...], grd, preferred_element_type=jnp.float32)
     near, far = value[: rows // 2], value[rows // 2:]
     columns = pl.ds(pl.multiple_of(piece * WIDE, WIDE), WIDE)
-    near = jnp.where(near_ref[...] == 1, near, -near)
-    far = jnp.where(far_ref[:, columns] == 1, far, -far)
+    near = near * near_ref[...].astype(jnp.float32)
+    far = far * far_ref[:, columns].astype(jnp.float32)
     parts = [part for half in zip(halves(near), halves(far)) for part in half]
     out = jnp.dot(table_ref[core], jnp.concatenate(parts, axis=0), preferred_element_type=jnp.float32)
     for t in range(WIDE // LANES):
@@ -185,10 +185,11 @@
     mine = lax.dynamic_index_in_dim(out_grad, core, 0, keepdims=False)
     other = lax.ppermute(lax.dynamic_index_in_dim(out_grad, 1 - core, 0, keepdims=False), "core", swap)
     far_act = lax.ppermute(activations, "core", swap)
-    far = lax.ppermute(sign_bits, "core", swap)
+    near = jnp.where(sign_bits == 1, 1.0, -1.0).astype(jnp.bfloat16)
+    far = lax.ppermute(near, "core", swap)
     blocks = around([mine, other], "z")
 
-    terms = local_samples(activations, far_act, blocks, sign_bits, far, core, here, sample_index)
+    terms = local_samples(activations, far_act, blocks, near, far, core, here, sample_index)
     feature_count = sample_index.shape[0]
     per = feature_count // (2 * chips)
     terms = lax.all_to_all(terms.reshape(2 * chips, per), ("z", "core"), 0, 0, tiled=True)

time: 196 us -> 195 us (level)
  waiting for transfers between devices: 20.9 us -> 18.5 us
    all_to_all x1, starting transfers between devices: 16.2 us -> 12.2 us  [per_device(): lax.all_to_all(terms.reshape(2 * chips, per), ('z', 'core'), 0, 0, tiled=...]
    ppermute x1, waiting for transfers between devices: 1.87 us -> 5.03 us  [around(): ups[0].append(lax.ppermute(ups[0][-1], axis, up))]
    ppermute x1, waiting for transfers between devices: 3.07 us -> 0.01 us  [around(): downs[1].append(lax.ppermute(downs[1][-1], axis, down))]
    ppermute x14, waiting for transfers between devices: 2.67 us -> 0.04 us  [around(): chain.append(lax.ppermute(chain[-1], axis, down))]
    ppermute x1, starting transfers between devices: 1.92 us -> 4.23 us  [per_device(): far_act = lax.ppermute(activations, 'core', swap)]
  transfers between devices with their start and end apart: 34 -> 34, of which waited for: 5 -> 4; matrix products, arithmetic and copies ran while one was open for 1% -> 2% of each run, Pallas kernels for 0% -> 0%
where the time goes in v7:
time: 195 us; the launch traced here: 193 us
  starting transfers between devices  120 us (62%)
  blocking collectives  30.5 us (16%)
  waiting for transfers between devices  18.5 us (9%)
  Pallas kernels  17.6 us (9%)
  other arithmetic  3.19 us (2%)
  local copies, waits for them, and re-layouts  1.97 us (1%)
    ppermute x14, starting transfers between devices, around(): chain.append(lax.ppermute(chain[-1], axis, down))  54.3 us
    ppermute x14, starting transfers between devices, around(): chain.append(lax.ppermute(chain[-1], axis, up))  30.7 us
    all_to_all x2, blocking collectives, to_all(): lax.all_to_all(jnp.broadcast_to(value[None], (size,) + value.shape), axes...  30.5 us
    pallas_call x1, Pallas kernels, local_samples(): pl.pallas_call(sampled_gradient, grid=(width // WIDE,), out_shape=jax.Sha...  17.6 us
    all_to_all x1, starting transfers between devices, per_device(): lax.all_to_all(terms.reshape(2 * chips, per), ('z', 'core'), 0, 0, tiled=...  12.2 us
    all_to_all x1, waiting for transfers between devices, per_device(): lax.all_to_all(terms.reshape(2 * chips, per), ('z', 'core'), 0, 0, tiled=...  11.3 us
    ppermute x1, starting transfers between devices, per_device(): lax.ppermute(lax.dynamic_index_in_dim(out_grad, 1 - core, 0, keepdims=Fal...  8.79 us
    ppermute x1, waiting for transfers between devices, around(): ups[0].append(lax.ppermute(ups[0][-1], axis, up))  5.03 us
  transfers between devices with their start and end apart: 34, of which 4 were waited for; matrix products, arithmetic and copies ran while one was open for 2% of the time, Pallas kernels for 0%

profile of v7, /device:TPU:1, one launch (start us, length us, event | category | flops | bytes accessed | tf_op | source)
XLA Modules:
  0.0 193.3 jit_solution(16957494416281408121)
XLA Ops:
  1.7 8.8 %collective-permute-start.17 = (bf16[32,4096]{1,0:T(8,128)(2,1)S(1)}, bf16[32,4096]{1,0:T(8,128)(2,1)S(1)}, u32[]{:S(2)}, u32[]{:S(2)}) collective-permute-start(bf16[32,4096]{1,0:T(8,128)(2,1)S(1)} %get-tuple-element.2), channel_id=1, source_target_pairs={{0,16},{16,0},{1,17},{17,1},{2,18},{18,2},{3,19},{19,3},{4,20},{20... | collective-permute-start | bytes 786440 | tf_op jit(solution)/shard_map/ppermute | solution.py:186
  12.5 5.7 %collective-permute-start.18 = (bf16[32,4096]{1,0:T(8,128)(2,1)S(1)}, bf16[32,4096]{1,0:T(8,128)(2,1)S(1)}, u32[]{:S(2)}, u32[]{:S(2)}) collective-permute-start(bf16[32,4096]{1,0:T(8,128)(2,1)S(1)} %collective-permute-done.17.refs_16_), channel_id=1, source_target_pairs={{0,480},{32,0},{64,32},{96,64},{128,96},{160,128},{192,160},{224,1... | collective-permute-start | bytes 786440 | tf_op jit(solution)/shard_map/ppermute | solution.py:168
  18.2 3.4 %collective-permute-start.2 = (bf16[32,4096]{1,0:T(8,128)(2,1)S(1)}, bf16[32,4096]{1,0:T(8,128)(2,1)S(1)}, u32[]{:S(2)}, u32[]{:S(2)}) collective-permute-start(bf16[32,4096]{1,0:T(8,128)(2,1)S(1)} %get-tuple-element.3.refs_0_), channel_id=1, source_target_pairs={{0,480},{32,0},{64,32},{96,64},{128,96},{160,128},{192,160},{224,1... | collective-permute-start | bytes 786440 | tf_op jit(solution)/shard_map/ppermute | solution.py:168
  21.6 1.9 collective-permute-start.26
  25.5 4.6 %collective-permute-start.19 = (bf16[32,4096]{1,0:T(8,128)(2,1)S(1)}, bf16[32,4096]{1,0:T(8,128)(2,1)S(1)}, u32[]{:S(2)}, u32[]{:S(2)}) collective-permute-start(bf16[32,4096]{1,0:T(8,128)(2,1)S(1)} %collective-permute-done.18.refs_17_), channel_id=1, source_target_pairs={{0,480},{32,0},{64,32},{96,64},{128,96},{160,128},{192,160},{224,1... | collective-permute-start | bytes 786440 | tf_op jit(solution)/shard_map/ppermute | solution.py:168
  30.1 4.8 %collective-permute-start.3 = (bf16[32,4096]{1,0:T(8,128)(2,1)S(1)}, bf16[32,4096]{1,0:T(8,128)(2,1)S(1)}, u32[]{:S(2)}, u32[]{:S(2)}) collective-permute-start(bf16[32,4096]{1,0:T(8,128)(2,1)S(1)} %collective-permute-done.2.refs_1_), channel_id=1, source_target_pairs={{0,480},{32,0},{64,32},{96,64},{128,96},{160,128},{192,160},{224,1... | collective-permute-start | bytes 786440 | tf_op jit(solution)/shard_map/ppermute | solution.py:168
  39.2 4.6 %collective-permute-start.20 = (bf16[32,4096]{1,0:T(8,128)(2,1)S(1)}, bf16[32,4096]{1,0:T(8,128)(2,1)S(1)}, u32[]{:S(2)}, u32[]{:S(2)}) collective-permute-start(bf16[32,4096]{1,0:T(8,128)(2,1)S(1)} %collective-permute-done.19.refs_18_), channel_id=1, source_target_pairs={{0,480},{32,0},{64,32},{96,64},{128,96},{160,128},{192,160},{224,1... | collective-permute-start | bytes 786440 | tf_op jit(solution)/shard_map/ppermute | solution.py:168
  43.8 4.2 %collective-permute-start = (bf16[2,1024,128]{2,1,0:T(8,128)(2,1)}, bf16[2,1024,128]{2,1,0:T(8,128)(2,1)S(1)}, u32[]{:S(2)}, u32[]{:S(2)}) collective-permute-start(bf16[2,1024,128]{2,1,0:T(8,128)(2,1)} %near_act_ref.1), channel_id=1, source_target_pairs={{0,16},{16,0},{1,17},{17,1},{2,18},{18,2},{3,19},{19,3},{4,20},{20... | collective-permute-start | bytes 1572872 | tf_op jit(solution)/shard_map/ppermute | solution.py:187
  48.1 2.5 %collective-permute-start.4 = (bf16[32,4096]{1,0:T(8,128)(2,1)S(1)}, bf16[32,4096]{1,0:T(8,128)(2,1)S(1)}, u32[]{:S(2)}, u32[]{:S(2)}) collective-permute-start(bf16[32,4096]{1,0:T(8,128)(2,1)S(1)} %collective-permute-done.3.refs_2_), channel_id=1, source_target_pairs={{0,480},{32,0},{64,32},{96,64},{128,96},{160,128},{192,160},{224,1... | collective-permute-start | bytes 786440 | tf_op jit(solution)/shard_map/ppermute | solution.py:168
  50.6 2.8 %collective-permute-start.28 = (bf16[32,4096]{1,0:T(8,128)(2,1)S(1)}, bf16[32,4096]{1,0:T(8,128)(2,1)S(1)}, u32[]{:S(2)}, u32[]{:S(2)}) collective-permute-start(bf16[32,4096]{1,0:T(8,128)(2,1)S(1)} %collective-permute-done.27.refs_30_), channel_id=1, source_target_pairs={{0,32},{32,64},{64,96},{96,128},{128,160},{160,192},{192,224},{224... | collective-permute-start | bytes 786440 | tf_op jit(solution)/shard_map/ppermute | solution.py:166
  55.4 4.6 %collective-permute-start.21 = (bf16[32,4096]{1,0:T(8,128)(2,1)S(1)}, bf16[32,4096]{1,0:T(8,128)(2,1)S(1)}, u32[]{:S(2)}, u32[]{:S(2)}) collective-permute-start(bf16[32,4096]{1,0:T(8,128)(2,1)S(1)} %collective-permute-done.20.refs_19_), channel_id=1, source_target_pairs={{0,480},{32,0},{64,32},{96,64},{128,96},{160,128},{192,160},{224,1... | collective-permute-start | bytes 786440 | tf_op jit(solution)/shard_map/ppermute | solution.py:168
  61.8 3.0 %collective-permute-start.1 = (bf16[128,4096]{1,0:T(8,128)(2,1)S(1)}, bf16[128,4096]{1,0:T(8,128)(2,1)S(1)}, u32[]{:S(2)}, u32[]{:S(2)}) collective-permute-start(bf16[128,4096]{1,0:T(8,128)(2,1)S(1)} %select_convert_fusion.near_ref), channel_id=1, source_target_pairs={{0,16},{16,0},{1,17},{17,1},{2,18},{18,2},{3,19},{19,3},{4,20},{20... | collective-permute-start | bytes 3145736 | tf_op jit(solution)/shard_map/ppermute | solution.py:189
  64.9 2.5 %collective-permute-start.5 = (bf16[32,4096]{1,0:T(8,128)(2,1)S(1)}, bf16[32,4096]{1,0:T(8,128)(2,1)S(1)}, u32[]{:S(2)}, u32[]{:S(2)}) collective-permute-start(bf16[32,4096]{1,0:T(8,128)(2,1)S(1)} %collective-permute-done.4.refs_3_), channel_id=1, source_target_pairs={{0,480},{32,0},{64,32},{96,64},{128,96},{160,128},{192,160},{224,1... | collective-permute-start | bytes 786440 | tf_op jit(solution)/shard_map/ppermute | solution.py:168
  67.5 2.8 %collective-permute-start.29 = (bf16[32,4096]{1,0:T(8,128)(2,1)S(1)}, bf16[32,4096]{1,0:T(8,128)(2,1)S(1)}, u32[]{:S(2)}, u32[]{:S(2)}) collective-permute-start(bf16[32,4096]{1,0:T(8,128)(2,1)S(1)} %collective-permute-done.28.refs_29_), channel_id=1, source_target_pairs={{0,32},{32,64},{64,96},{96,128},{128,160},{160,192},{192,224},{224... | collective-permute-start | bytes 786440 | tf_op jit(solution)/shard_map/ppermute | solution.py:166
  72.2 4.6 %collective-permute-start.22 = (bf16[32,4096]{1,0:T(8,128)(2,1)S(1)}, bf16[32,4096]{1,0:T(8,128)(2,1)S(1)}, u32[]{:S(2)}, u32[]{:S(2)}) collective-permute-start(bf16[32,4096]{1,0:T(8,128)(2,1)S(1)} %collective-permute-done.21.refs_20_), channel_id=1, source_target_pairs={{0,480},{32,0},{64,32},{96,64},{128,96},{160,128},{192,160},{224,1... | collective-permute-start | bytes 786440 | tf_op jit(solution)/shard_map/ppermute | solution.py:168
  76.8 2.5 %collective-permute-start.6 = (bf16[32,4096]{1,0:T(8,128)(2,1)S(1)}, bf16[32,4096]{1,0:T(8,128)(2,1)S(1)}, u32[]{:S(2)}, u32[]{:S(2)}) collective-permute-start(bf16[32,4096]{1,0:T(8,128)(2,1)S(1)} %collective-permute-done.5.refs_4_), channel_id=1, source_target_pairs={{0,480},{32,0},{64,32},{96,64},{128,96},{160,128},{192,160},{224,1... | collective-permute-start | bytes 786440 | tf_op jit(solution)/shard_map/ppermute | solution.py:168
  79.4 2.8 %collective-permute-start.30 = (bf16[32,4096]{1,0:T(8,128)(2,1)S(1)}, bf16[32,4096]{1,0:T(8,128)(2,1)S(1)}, u32[]{:S(2)}, u32[]{:S(2)}) collective-permute-start(bf16[32,4096]{1,0:T(8,128)(2,1)S(1)} %collective-permute-done.29.refs_28_), channel_id=1, source_target_pairs={{0,32},{32,64},{64,96},{96,128},{128,160},{160,192},{192,224},{224... | collective-permute-start | bytes 786440 | tf_op jit(solution)/shard_map/ppermute | solution.py:166
  85.7 4.6 %collective-permute-start.23 = (bf16[32,4096]{1,0:T(8,128)(2,1)S(1)}, bf16[32,4096]{1,0:T(8,128)(2,1)S(1)}, u32[]{:S(2)}, u32[]{:S(2)}) collective-permute-start(bf16[32,4096]{1,0:T(8,128)(2,1)S(1)} %collective-permute-done.22.refs_21_), channel_id=1, source_target_pairs={{0,480},{32,0},{64,32},{96,64},{128,96},{160,128},{192,160},{224,1... | collective-permute-start | bytes 786440 | tf_op jit(solution)/shard_map/ppermute | solution.py:168
  90.3 2.1 %collective-permute-start.7 = (bf16[32,4096]{1,0:T(8,128)(2,1)S(1)}, bf16[32,4096]{1,0:T(8,128)(2,1)}, u32[]{:S(2)}, u32[]{:S(2)}) collective-permute-start(bf16[32,4096]{1,0:T(8,128)(2,1)S(1)} %collective-permute-done.6.refs_5_), channel_id=1, source_target_pairs={{0,480},{32,0},{64,32},{96,64},{128,96},{160,128},{192,160},{224,1... | collective-permute-start | bytes 786440 | tf_op jit(solution)/shard_map/ppermute | solution.py:168
  92.5 3.2 %collective-permute-start.31 = (bf16[32,4096]{1,0:T(8,128)(2,1)S(1)}, bf16[32,4096]{1,0:T(8,128)(2,1)}, u32[]{:S(2)}, u32[]{:S(2)}) collective-permute-start(bf16[32,4096]{1,0:T(8,128)(2,1)S(1)} %collective-permute-done.30.refs_27_), channel_id=1, source_target_pairs={{0,32},{32,64},{64,96},{96,128},{128,160},{160,192},{192,224},{224... | collective-permute-start | bytes 786440 | tf_op jit(solution)/shard_map/ppermute | solution.py:166
  95.7 1.9 collective-permute-start.15
  97.7 4.6 %collective-permute-start.24 = (bf16[32,4096]{1,0:T(8,128)(2,1)S(1)}, bf16[32,4096]{1,0:T(8,128)(2,1)}, u32[]{:S(2)}, u32[]{:S(2)}) collective-permute-start(bf16[32,4096]{1,0:T(8,128)(2,1)S(1)} %collective-permute-done.23.refs_22_), channel_id=1, source_target_pairs={{0,480},{32,0},{64,32},{96,64},{128,96},{160,128},{192,160},{224,1... | collective-permute-start | bytes 786440 | tf_op jit(solution)/shard_map/ppermute | solution.py:168
  102.3 3.3 %collective-permute-start.8 = (bf16[32,4096]{1,0:T(8,128)(2,1)}, bf16[32,4096]{1,0:T(8,128)(2,1)}, u32[]{:S(2)}, u32[]{:S(2)}) collective-permute-start(bf16[32,4096]{1,0:T(8,128)(2,1)} %collective-permute-done.7.refs_6_), channel_id=1, source_target_pairs={{0,480},{32,0},{64,32},{96,64},{128,96},{160,128},{192,160},{224,1... | collective-permute-start | bytes 786440 | tf_op jit(solution)/shard_map/ppermute | solution.py:168
  105.6 2.0 %collective-permute-start.32 = (bf16[32,4096]{1,0:T(8,128)(2,1)}, bf16[32,4096]{1,0:T(8,128)(2,1)}, u32[]{:S(2)}, u32[]{:S(2)}) collective-permute-start(bf16[32,4096]{1,0:T(8,128)(2,1)} %collective-permute-done.31.refs_26_), channel_id=1, source_target_pairs={{0,32},{32,64},{64,96},{96,128},{128,160},{160,192},{192,224},{224... | collective-permute-start | bytes 786440 | tf_op jit(solution)/shard_map/ppermute | solution.py:166
  107.6 1.9 collective-permute-start.16
  109.5 4.6 %collective-permute-start.25 = (bf16[32,4096]{1,0:T(8,128)(2,1)}, bf16[32,4096]{1,0:T(8,128)(2,1)}, u32[]{:S(2)}, u32[]{:S(2)}) collective-permute-start(bf16[32,4096]{1,0:T(8,128)(2,1)} %collective-permute-done.24.refs_23_), channel_id=1, source_target_pairs={{0,480},{32,0},{64,32},{96,64},{128,96},{160,128},{192,160},{224,1... | collective-permute-start | bytes 786440 | tf_op jit(solution)/shard_map/ppermute | solution.py:170
  114.8 5.0 %collective-permute-done.16.refs_8_ = bf16[32,4096]{1,0:T(8,128)(2,1)} collective-permute-done((bf16[32,4096]{1,0:T(8,128)(2,1)}, bf16[32,4096]{1,0:T(8,128)(2,1)}, u32[]{:S(2)}, u32[]{:S(2)}) %collective-permute-start.16) | collective-permute-done | bytes 262176 | tf_op jit(solution)/shard_map/ppermute | solution.py:169
  119.9 17.6 %sampled_gradient.1 = f32[64,128]{1,0:T(8,128)} custom-call(s32[2]{0:T(128)} %pad_add_fusion.place_ref, s32[64,128]{1,0:T(8,128)} %bitcast.13, bf16[2,1024,128]{2,1,0:T(8,128)(2,1)} %near_act_ref.1, bf16[2,1024,128]{2,1,0:T(8,128)(2,1)} %copy-done.3, bf16[128,4096]{1,0:T(8,128)(2,1)} %copy-done.1, bf16[2,256,512]{2,1,0:T(8,128)(2,1)} %constant.46.clone.table_ref, ...), custom_call_target="tpu_custom_call" | custom-call | tf_op jit(solution)/shard_map/sampled_gradient/pallas_call | solution.py:126
  137.5 12.2 %all-to-all-start = ((f32[32,1,256]{2,1,0:T(1,128)}), f32[32,1,256]{2,1,0:T(1,128)S(1)}, u32[]{:S(2)}, u32[]{:S(2)}) async-start(f32[32,1,256]{2,1,0:T(1,128)} %bitcast.12), calls=%async_computation | async-start | bytes 65536 | tf_op jit(solution)/shard_map/all_to_all | solution.py:195
  150.4 11.3 %all-to-all-done = f32[32,1,256]{2,1,0:T(1,128)S(1)} async-done(((f32[32,1,256]{2,1,0:T(1,128)}), f32[32,1,256]{2,1,0:T(1,128)S(1)}, u32[]{:S(2)}, u32[]{:S(2)}) %all-to-all-start) | async-done | bytes 32800 | tf_op jit(solution)/shard_map/all_to_all | solution.py:195
  162.0 13.0 %all_to_all.19 = f32[16,2,256]{2,1,0:T(2,128)S(1)} all-to-all(f32[16,2,256]{2,1,0:T(2,128)S(1)} %broadcast_in_dim.23), channel_id=1, replica_groups=mesh['z'=16,'core'=2,'ex'=16] {'ex'}, dimensions={0} | all-to-all | bytes 65536 | tf_op jit(solution)/shard_map/all_to_all | solution.py:176
  175.2 17.5 %all_to_all.20 = f32[32,2,32]{2,1,0:T(2,128)S(1)} all-to-all(f32[32,2,32]{2,1,0:T(2,128)S(1)} %broadcast_in_dim.24), channel_id=1, replica_groups=mesh['z'=16,'core'=2,'ex'=16] {'z','core'}, dimensions={0} | all-to-all | bytes 16384 | tf_op jit(solution)/shard_map/all_to_all | solution.py:176
  (109 shorter events, 20.9 us)
Async XLA Ops:
  1.7 10.7 %collective-permute-start.17 = (bf16[32,4096]{1,0:T(8,128)(2,1)S(1)}, bf16[32,4096]{1,0:T(8,128)(2,1)S(1)}, u32[]{:S(2)}, u32[]{:S(2)}) collective-permute-start(bf16[32,4096]{1,0:T(8,128)(2,1)S(1)} %get-tuple-element.2), channel_id=1, source_target_pairs={{0,16},{16,0},{1,17},{17,1},{2,18},{18,2},{3,19},{19,3},{4,20},{20... | collective-permute-start | bytes 786440 | tf_op jit(solution)/shard_map/ppermute | solution.py:186
  10.5 13.0 %collective-permute-start.9 = (bf16[32,4096]{1,0:T(8,128)(2,1)S(1)}, bf16[32,4096]{1,0:T(8,128)(2,1)S(1)}, u32[]{:S(2)}, u32[]{:S(2)}) collective-permute-start(bf16[32,4096]{1,0:T(8,128)(2,1)S(1)} %get-tuple-element.3.refs_0_), channel_id=1, source_target_pairs={{0,32},{32,64},{64,96},{96,128},{128,160},{160,192},{192,224},{224... | collective-permute-start | bytes 786440 | tf_op jit(solution)/shard_map/ppermute | solution.py:166
  12.5 13.0 %collective-permute-start.18 = (bf16[32,4096]{1,0:T(8,128)(2,1)S(1)}, bf16[32,4096]{1,0:T(8,128)(2,1)S(1)}, u32[]{:S(2)}, u32[]{:S(2)}) collective-permute-start(bf16[32,4096]{1,0:T(8,128)(2,1)S(1)} %collective-permute-done.17.refs_16_), channel_id=1, source_target_pairs={{0,480},{32,0},{64,32},{96,64},{128,96},{160,128},{192,160},{224,1... | collective-permute-start | bytes 786440 | tf_op jit(solution)/shard_map/ppermute | solution.py:168
  18.2 11.9 %collective-permute-start.2 = (bf16[32,4096]{1,0:T(8,128)(2,1)S(1)}, bf16[32,4096]{1,0:T(8,128)(2,1)S(1)}, u32[]{:S(2)}, u32[]{:S(2)}) collective-permute-start(bf16[32,4096]{1,0:T(8,128)(2,1)S(1)} %get-tuple-element.3.refs_0_), channel_id=1, source_target_pairs={{0,480},{32,0},{64,32},{96,64},{128,96},{160,128},{192,160},{224,1... | collective-permute-start | bytes 786440 | tf_op jit(solution)/shard_map/ppermute | solution.py:168
  21.6 13.3 %collective-permute-start.26 = (bf16[32,4096]{1,0:T(8,128)(2,1)S(1)}, bf16[32,4096]{1,0:T(8,128)(2,1)S(1)}, u32[]{:S(2)}, u32[]{:S(2)}) collective-permute-start(bf16[32,4096]{1,0:T(8,128)(2,1)S(1)} %collective-permute-done.17.refs_16_), channel_id=1, source_target_pairs={{0,32},{32,64},{64,96},{96,128},{128,160},{160,192},{192,224},{224... | collective-permute-start | bytes 786440 | tf_op jit(solution)/shard_map/ppermute | solution.py:166
  23.5 13.7 %collective-permute-start.10 = (bf16[32,4096]{1,0:T(8,128)(2,1)S(1)}, bf16[32,4096]{1,0:T(8,128)(2,1)S(1)}, u32[]{:S(2)}, u32[]{:S(2)}) collective-permute-start(bf16[32,4096]{1,0:T(8,128)(2,1)S(1)} %collective-permute-done.9.refs_15_), channel_id=1, source_target_pairs={{0,32},{32,64},{64,96},{96,128},{128,160},{160,192},{192,224},{224... | collective-permute-start | bytes 786440 | tf_op jit(solution)/shard_map/ppermute | solution.py:166
  25.5 13.7 %collective-permute-start.19 = (bf16[32,4096]{1,0:T(8,128)(2,1)S(1)}, bf16[32,4096]{1,0:T(8,128)(2,1)S(1)}, u32[]{:S(2)}, u32[]{:S(2)}) collective-permute-start(bf16[32,4096]{1,0:T(8,128)(2,1)S(1)} %collective-permute-done.18.refs_17_), channel_id=1, source_target_pairs={{0,480},{32,0},{64,32},{96,64},{128,96},{160,128},{192,160},{224,1... | collective-permute-start | bytes 786440 | tf_op jit(solution)/shard_map/ppermute | solution.py:168
  30.1 18.0 %collective-permute-start.3 = (bf16[32,4096]{1,0:T(8,128)(2,1)S(1)}, bf16[32,4096]{1,0:T(8,128)(2,1)S(1)}, u32[]{:S(2)}, u32[]{:S(2)}) collective-permute-start(bf16[32,4096]{1,0:T(8,128)(2,1)S(1)} %collective-permute-done.2.refs_1_), channel_id=1, source_target_pairs={{0,480},{32,0},{64,32},{96,64},{128,96},{160,128},{192,160},{224,1... | collective-permute-start | bytes 786440 | tf_op jit(solution)/shard_map/ppermute | solution.py:168
  34.9 15.7 %collective-permute-start.27 = (bf16[32,4096]{1,0:T(8,128)(2,1)S(1)}, bf16[32,4096]{1,0:T(8,128)(2,1)S(1)}, u32[]{:S(2)}, u32[]{:S(2)}) collective-permute-start(bf16[32,4096]{1,0:T(8,128)(2,1)S(1)} %collective-permute-done.26.refs_31_), channel_id=1, source_target_pairs={{0,32},{32,64},{64,96},{96,128},{128,160},{160,192},{192,224},{224... | collective-permute-start | bytes 786440 | tf_op jit(solution)/shard_map/ppermute | solution.py:166
  37.3 16.1 %collective-permute-start.11 = (bf16[32,4096]{1,0:T(8,128)(2,1)S(1)}, bf16[32,4096]{1,0:T(8,128)(2,1)S(1)}, u32[]{:S(2)}, u32[]{:S(2)}) collective-permute-start(bf16[32,4096]{1,0:T(8,128)(2,1)S(1)} %collective-permute-done.10.refs_14_), channel_id=1, source_target_pairs={{0,32},{32,64},{64,96},{96,128},{128,160},{160,192},{192,224},{224... | collective-permute-start | bytes 786440 | tf_op jit(solution)/shard_map/ppermute | solution.py:166
  39.2 16.1 %collective-permute-start.20 = (bf16[32,4096]{1,0:T(8,128)(2,1)S(1)}, bf16[32,4096]{1,0:T(8,128)(2,1)S(1)}, u32[]{:S(2)}, u32[]{:S(2)}) collective-permute-start(bf16[32,4096]{1,0:T(8,128)(2,1)S(1)} %collective-permute-done.19.refs_18_), channel_id=1, source_target_pairs={{0,480},{32,0},{64,32},{96,64},{128,96},{160,128},{192,160},{224,1... | collective-permute-start | bytes 786440 | tf_op jit(solution)/shard_map/ppermute | solution.py:168
  43.8 18.0 %collective-permute-start = (bf16[2,1024,128]{2,1,0:T(8,128)(2,1)}, bf16[2,1024,128]{2,1,0:T(8,128)(2,1)S(1)}, u32[]{:S(2)}, u32[]{:S(2)}) collective-permute-start(bf16[2,1024,128]{2,1,0:T(8,128)(2,1)} %near_act_ref.1), channel_id=1, source_target_pairs={{0,16},{16,0},{1,17},{17,1},{2,18},{18,2},{3,19},{19,3},{4,20},{20... | collective-permute-start | bytes 1572872 | tf_op jit(solution)/shard_map/ppermute | solution.py:187
  48.1 16.8 %collective-permute-start.4 = (bf16[32,4096]{1,0:T(8,128)(2,1)S(1)}, bf16[32,4096]{1,0:T(8,128)(2,1)S(1)}, u32[]{:S(2)}, u32[]{:S(2)}) collective-permute-start(bf16[32,4096]{1,0:T(8,128)(2,1)S(1)} %collective-permute-done.3.refs_2_), channel_id=1, source_target_pairs={{0,480},{32,0},{64,32},{96,64},{128,96},{160,128},{192,160},{224,1... | collective-permute-start | bytes 786440 | tf_op jit(solution)/shard_map/ppermute | solution.py:168
  50.6 16.8 %collective-permute-start.28 = (bf16[32,4096]{1,0:T(8,128)(2,1)S(1)}, bf16[32,4096]{1,0:T(8,128)(2,1)S(1)}, u32[]{:S(2)}, u32[]{:S(2)}) collective-permute-start(bf16[32,4096]{1,0:T(8,128)(2,1)S(1)} %collective-permute-done.27.refs_30_), channel_id=1, source_target_pairs={{0,32},{32,64},{64,96},{96,128},{128,160},{160,192},{192,224},{224... | collective-permute-start | bytes 786440 | tf_op jit(solution)/shard_map/ppermute | solution.py:166
  53.4 16.8 %collective-permute-start.12 = (bf16[32,4096]{1,0:T(8,128)(2,1)S(1)}, bf16[32,4096]{1,0:T(8,128)(2,1)S(1)}, u32[]{:S(2)}, u32[]{:S(2)}) collective-permute-start(bf16[32,4096]{1,0:T(8,128)(2,1)S(1)} %collective-permute-done.11.refs_13_), channel_id=1, source_target_pairs={{0,32},{32,64},{64,96},{96,128},{128,160},{160,192},{192,224},{224... | collective-permute-start | bytes 786440 | tf_op jit(solution)/shard_map/ppermute | solution.py:166
  55.4 16.8 %collective-permute-start.21 = (bf16[32,4096]{1,0:T(8,128)(2,1)S(1)}, bf16[32,4096]{1,0:T(8,128)(2,1)S(1)}, u32[]{:S(2)}, u32[]{:S(2)}) collective-permute-start(bf16[32,4096]{1,0:T(8,128)(2,1)S(1)} %collective-permute-done.20.refs_19_), channel_id=1, source_target_pairs={{0,480},{32,0},{64,32},{96,64},{128,96},{160,128},{192,160},{224,1... | collective-permute-start | bytes 786440 | tf_op jit(solution)/shard_map/ppermute | solution.py:168
  61.8 52.9 %collective-permute-start.1 = (bf16[128,4096]{1,0:T(8,128)(2,1)S(1)}, bf16[128,4096]{1,0:T(8,128)(2,1)S(1)}, u32[]{:S(2)}, u32[]{:S(2)}) collective-permute-start(bf16[128,4096]{1,0:T(8,128)(2,1)S(1)} %select_convert_fusion.near_ref), channel_id=1, source_target_pairs={{0,16},{16,0},{1,17},{17,1},{2,18},{18,2},{3,19},{19,3},{4,20},{20... | collective-permute-start | bytes 3145736 | tf_op jit(solution)/shard_map/ppermute | solution.py:189
  64.9 11.9 %collective-permute-start.5 = (bf16[32,4096]{1,0:T(8,128)(2,1)S(1)}, bf16[32,4096]{1,0:T(8,128)(2,1)S(1)}, u32[]{:S(2)}, u32[]{:S(2)}) collective-permute-start(bf16[32,4096]{1,0:T(8,128)(2,1)S(1)} %collective-permute-done.4.refs_3_), channel_id=1, source_target_pairs={{0,480},{32,0},{64,32},{96,64},{128,96},{160,128},{192,160},{224,1... | collective-permute-start | bytes 786440 | tf_op jit(solution)/shard_map/ppermute | solution.py:168
  67.5 11.9 %collective-permute-start.29 = (bf16[32,4096]{1,0:T(8,128)(2,1)S(1)}, bf16[32,4096]{1,0:T(8,128)(2,1)S(1)}, u32[]{:S(2)}, u32[]{:S(2)}) collective-permute-start(bf16[32,4096]{1,0:T(8,128)(2,1)S(1)} %collective-permute-done.28.refs_29_), channel_id=1, source_target_pairs={{0,32},{32,64},{64,96},{96,128},{128,160},{160,192},{192,224},{224... | collective-permute-start | bytes 786440 | tf_op jit(solution)/shard_map/ppermute | solution.py:166
  70.2 13.5 %collective-permute-start.13 = (bf16[32,4096]{1,0:T(8,128)(2,1)S(1)}, bf16[32,4096]{1,0:T(8,128)(2,1)S(1)}, u32[]{:S(2)}, u32[]{:S(2)}) collective-permute-start(bf16[32,4096]{1,0:T(8,128)(2,1)S(1)} %collective-permute-done.12.refs_12_), channel_id=1, source_target_pairs={{0,32},{32,64},{64,96},{96,128},{128,160},{160,192},{192,224},{224... | collective-permute-start | bytes 786440 | tf_op jit(solution)/shard_map/ppermute | solution.py:166
  72.2 13.5 %collective-permute-start.22 = (bf16[32,4096]{1,0:T(8,128)(2,1)S(1)}, bf16[32,4096]{1,0:T(8,128)(2,1)S(1)}, u32[]{:S(2)}, u32[]{:S(2)}) collective-permute-start(bf16[32,4096]{1,0:T(8,128)(2,1)S(1)} %collective-permute-done.21.refs_20_), channel_id=1, source_target_pairs={{0,480},{32,0},{64,32},{96,64},{128,96},{160,128},{192,160},{224,1... | collective-permute-start | bytes 786440 | tf_op jit(solution)/shard_map/ppermute | solution.py:168
  76.8 13.5 %collective-permute-start.6 = (bf16[32,4096]{1,0:T(8,128)(2,1)S(1)}, bf16[32,4096]{1,0:T(8,128)(2,1)S(1)}, u32[]{:S(2)}, u32[]{:S(2)}) collective-permute-start(bf16[32,4096]{1,0:T(8,128)(2,1)S(1)} %collective-permute-done.5.refs_4_), channel_id=1, source_target_pairs={{0,480},{32,0},{64,32},{96,64},{128,96},{160,128},{192,160},{224,1... | collective-permute-start | bytes 786440 | tf_op jit(solution)/shard_map/ppermute | solution.py:168
  79.4 13.1 %collective-permute-start.30 = (bf16[32,4096]{1,0:T(8,128)(2,1)S(1)}, bf16[32,4096]{1,0:T(8,128)(2,1)S(1)}, u32[]{:S(2)}, u32[]{:S(2)}) collective-permute-start(bf16[32,4096]{1,0:T(8,128)(2,1)S(1)} %collective-permute-done.29.refs_28_), channel_id=1, source_target_pairs={{0,32},{32,64},{64,96},{96,128},{128,160},{160,192},{192,224},{224... | collective-permute-start | bytes 786440 | tf_op jit(solution)/shard_map/ppermute | solution.py:166
  83.8 11.9 %collective-permute-start.14 = (bf16[32,4096]{1,0:T(8,128)(2,1)S(1)}, bf16[32,4096]{1,0:T(8,128)(2,1)S(1)}, u32[]{:S(2)}, u32[]{:S(2)}) collective-permute-start(bf16[32,4096]{1,0:T(8,128)(2,1)S(1)} %collective-permute-done.13.refs_11_), channel_id=1, source_target_pairs={{0,32},{32,64},{64,96},{96,128},{128,160},{160,192},{192,224},{224... | collective-permute-start | bytes 786440 | tf_op jit(solution)/shard_map/ppermute | solution.py:166
  85.7 11.9 %collective-permute-start.23 = (bf16[32,4096]{1,0:T(8,128)(2,1)S(1)}, bf16[32,4096]{1,0:T(8,128)(2,1)S(1)}, u32[]{:S(2)}, u32[]{:S(2)}) collective-permute-start(bf16[32,4096]{1,0:T(8,128)(2,1)S(1)} %collective-permute-done.22.refs_21_), channel_id=1, source_target_pairs={{0,480},{32,0},{64,32},{96,64},{128,96},{160,128},{192,160},{224,1... | collective-permute-start | bytes 786440 | tf_op jit(solution)/shard_map/ppermute | solution.py:168
  90.3 11.9 %collective-permute-start.7 = (bf16[32,4096]{1,0:T(8,128)(2,1)S(1)}, bf16[32,4096]{1,0:T(8,128)(2,1)}, u32[]{:S(2)}, u32[]{:S(2)}) collective-permute-start(bf16[32,4096]{1,0:T(8,128)(2,1)S(1)} %collective-permute-done.6.refs_5_), channel_id=1, source_target_pairs={{0,480},{32,0},{64,32},{96,64},{128,96},{160,128},{192,160},{224,1... | collective-permute-start | bytes 786440 | tf_op jit(solution)/shard_map/ppermute | solution.py:168
  92.5 13.0 %collective-permute-start.31 = (bf16[32,4096]{1,0:T(8,128)(2,1)S(1)}, bf16[32,4096]{1,0:T(8,128)(2,1)}, u32[]{:S(2)}, u32[]{:S(2)}) collective-permute-start(bf16[32,4096]{1,0:T(8,128)(2,1)S(1)} %collective-permute-done.30.refs_27_), channel_id=1, source_target_pairs={{0,32},{32,64},{64,96},{96,128},{128,160},{160,192},{192,224},{224... | collective-permute-start | bytes 786440 | tf_op jit(solution)/shard_map/ppermute | solution.py:166
  95.7 11.9 %collective-permute-start.15 = (bf16[32,4096]{1,0:T(8,128)(2,1)S(1)}, bf16[32,4096]{1,0:T(8,128)(2,1)}, u32[]{:S(2)}, u32[]{:S(2)}) collective-permute-start(bf16[32,4096]{1,0:T(8,128)(2,1)S(1)} %collective-permute-done.14.refs_10_), channel_id=1, source_target_pairs={{0,32},{32,64},{64,96},{96,128},{128,160},{160,192},{192,224},{224... | collective-permute-start | bytes 786440 | tf_op jit(solution)/shard_map/ppermute | solution.py:166
  97.7 11.9 %collective-permute-start.24 = (bf16[32,4096]{1,0:T(8,128)(2,1)S(1)}, bf16[32,4096]{1,0:T(8,128)(2,1)}, u32[]{:S(2)}, u32[]{:S(2)}) collective-permute-start(bf16[32,4096]{1,0:T(8,128)(2,1)S(1)} %collective-permute-done.23.refs_22_), channel_id=1, source_target_pairs={{0,480},{32,0},{64,32},{96,64},{128,96},{160,128},{192,160},{224,1... | collective-permute-start | bytes 786440 | tf_op jit(solution)/shard_map/ppermute | solution.py:168
  102.3 12.5 %collective-permute-start.8 = (bf16[32,4096]{1,0:T(8,128)(2,1)}, bf16[32,4096]{1,0:T(8,128)(2,1)}, u32[]{:S(2)}, u32[]{:S(2)}) collective-permute-start(bf16[32,4096]{1,0:T(8,128)(2,1)} %collective-permute-done.7.refs_6_), channel_id=1, source_target_pairs={{0,480},{32,0},{64,32},{96,64},{128,96},{160,128},{192,160},{224,1... | collective-permute-start | bytes 786440 | tf_op jit(solution)/shard_map/ppermute | solution.py:168
  107.6 12.2 %collective-permute-start.16 = (bf16[32,4096]{1,0:T(8,128)(2,1)}, bf16[32,4096]{1,0:T(8,128)(2,1)}, u32[]{:S(2)}, u32[]{:S(2)}) collective-permute-start(bf16[32,4096]{1,0:T(8,128)(2,1)} %collective-permute-done.15.refs_9_), channel_id=1, source_target_pairs={{0,32},{32,64},{64,96},{96,128},{128,160},{160,192},{192,224},{224... | collective-permute-start | bytes 786440 | tf_op jit(solution)/shard_map/ppermute | solution.py:169
  137.5 24.3 %all-to-all-start = ((f32[32,1,256]{2,1,0:T(1,128)}), f32[32,1,256]{2,1,0:T(1,128)S(1)}, u32[]{:S(2)}, u32[]{:S(2)}) async-start(f32[32,1,256]{2,1,0:T(1,128)} %bitcast.12), calls=%async_computation | async-start | bytes 65536 | tf_op jit(solution)/shard_map/all_to_all | solution.py:195
  (30 other events, 757.2 us)

commit v8 on v5

--- a/solution.py
+++ b/solution.py
@@ -8,7 +8,7 @@
 
 LANES = 128
 WIDE = 2048
-BATCH = 1024
+BATCH = 4096
 LOAD = 512
 VMEM_MIB = 60
 
@@ -33,7 +33,7 @@
     outer = mixed.shape[0] // rows
     width = outer * LANES
     piece, last = pl.program_id(0), pl.num_programs(0) - 1
-    core = place_ref[0]
+    here, core = lax.div(place_ref[0], 2), lax.rem(place_ref[0], 2)
     row_copy = pltpu.make_async_copy(rows_v, rows_s, sem)
 
     @pl.when(piece == 0)
@@ -46,7 +46,7 @@
         depth = grd_refs[0].shape[0]
         for which in range(2):
             for j in range(chips):
-                source = lax.rem(place_ref[1] + j, chips) * (2 * depth) + lax.rem(core + which, 2) * depth
+                source = lax.rem(here + j, chips) * (2 * depth) + lax.rem(core + which, 2) * depth
                 source = pl.ds(pl.multiple_of(source, depth), depth)
                 target = pl.ds((which * chips + j) * depth, depth)
                 tokens[target, :rows // 2] = near_act_ref[core, source, :]
@@ -114,7 +114,7 @@
         lax.fori_loop(0, stage.shape[0] // BATCH, inner_step, 0)
 
 
-def local_samples(near_act, far_act, blocks, near, far, core, here, sample_index):
+def local_samples(near_act, far_act, blocks, near, far, place, sample_index):
     tokens = near_act.shape[1]
     rows = 2 * near_act.shape[2]
     width = near.shape[1]
@@ -144,7 +144,7 @@
         compiler_params=pltpu.CompilerParams(vmem_limit_bytes=VMEM_MIB * 1024 * 1024),
         name="sampled_gradient",
     )(
-        jnp.stack([core, here]).astype(jnp.int32),
+        place[None],
         sample_index.reshape(count // LANES, LANES),
         near_act,
         far_act,
@@ -187,7 +187,7 @@
     far = lax.ppermute(sign_bits, "core", swap)
     blocks = around([mine, other], "z")
 
-    terms = local_samples(activations, far_act, blocks, sign_bits, far, core, here, sample_index)
+    terms = local_samples(activations, far_act, blocks, sign_bits, far, lax.axis_index(("z", "core")), sample_index)
     feature_count = sample_index.shape[0]
     per = feature_count // (2 * chips)
     terms = lax.all_to_all(terms.reshape(2 * chips, per), ("z", "core"), 0, 0, tiled=True)

time: 196 us -> 195 us (level)
  transfers between devices with their start and end apart: 34 -> 34, of which waited for: 6 -> 6; matrix products, arithmetic and copies ran while one was open for 1% -> 0% of each run, Pallas kernels for 0% -> 0%
where the time goes in v8:
time: 195 us; the launch traced here: 193 us
  starting transfers between devices  119 us (61%)
  blocking collectives  30.6 us (16%)
  waiting for transfers between devices  21 us (11%)
  Pallas kernels  18.1 us (9%)
  local copies, waits for them, and re-layouts  1.96 us (1%)
    ppermute x14, starting transfers between devices, around(): chain.append(lax.ppermute(chain[-1], axis, down))  51.5 us
    ppermute x16, starting transfers between devices, around(): chain.append(lax.ppermute(chain[-1], axis, up))  37.2 us
    all_to_all x2, blocking collectives, to_all(): lax.all_to_all(jnp.broadcast_to(value[None], (size,) + value.shape), axes...  30.6 us
    pallas_call x1, Pallas kernels, local_samples(): pl.pallas_call(sampled_gradient, grid=(width // WIDE,), out_shape=jax.Sha...  18.1 us
    all_to_all x1, starting transfers between devices, per_device(): lax.all_to_all(terms.reshape(2 * chips, per), ('z', 'core'), 0, 0, tiled=...  17.3 us
    all_to_all x1, waiting for transfers between devices, per_device(): lax.all_to_all(terms.reshape(2 * chips, per), ('z', 'core'), 0, 0, tiled=...  11.2 us
    ppermute x16, waiting for transfers between devices, around(): chain.append(lax.ppermute(chain[-1], axis, up))  8.9 us
    ppermute x1, starting transfers between devices, per_device(): lax.ppermute(lax.dynamic_index_in_dim(out_grad, 1 - core, 0, keepdims=Fal...  8.79 us
  transfers between devices with their start and end apart: 34, of which 6 were waited for; matrix products, arithmetic and copies ran while one was open for 0% of the time, Pallas kernels for 0%

profile of v8, /device:TPU:1, one launch (start us, length us, event | category | flops | bytes accessed | tf_op | source)
XLA Modules:
  0.0 193.5 jit_solution(15863683308669019552)
XLA Ops:
  1.7 8.8 %collective-permute-start.17 = (bf16[32,4096]{1,0:T(8,128)(2,1)S(1)}, bf16[32,4096]{1,0:T(8,128)(2,1)S(1)}, u32[]{:S(2)}, u32[]{:S(2)}) collective-permute-start(bf16[32,4096]{1,0:T(8,128)(2,1)S(1)} %get-tuple-element.2), channel_id=1, source_target_pairs={{0,16},{16,0},{1,17},{17,1},{2,18},{18,2},{3,19},{19,3},{4,20},{20... | collective-permute-start | bytes 786440 | tf_op jit(solution)/shard_map/ppermute | solution.py:185
  12.4 5.7 %collective-permute-start.2 = (bf16[32,4096]{1,0:T(8,128)(2,1)S(1)}, bf16[32,4096]{1,0:T(8,128)(2,1)S(1)}, u32[]{:S(2)}, u32[]{:S(2)}) collective-permute-start(bf16[32,4096]{1,0:T(8,128)(2,1)S(1)} %get-tuple-element.3.refs_0_), channel_id=1, source_target_pairs={{0,480},{32,0},{64,32},{96,64},{128,96},{160,128},{192,160},{224,1... | collective-permute-start | bytes 786440 | tf_op jit(solution)/shard_map/ppermute | solution.py:169
  20.1 4.6 %collective-permute-start.18 = (bf16[32,4096]{1,0:T(8,128)(2,1)S(1)}, bf16[32,4096]{1,0:T(8,128)(2,1)S(1)}, u32[]{:S(2)}, u32[]{:S(2)}) collective-permute-start(bf16[32,4096]{1,0:T(8,128)(2,1)S(1)} %collective-permute-done.17.refs_16_), channel_id=1, source_target_pairs={{0,480},{32,0},{64,32},{96,64},{128,96},{160,128},{192,160},{224,1... | collective-permute-start | bytes 786440 | tf_op jit(solution)/shard_map/ppermute | solution.py:169
  24.7 2.8 %collective-permute-start.1 = (s32[128,4096]{1,0:T(8,128)}, s32[128,4096]{1,0:T(8,128)S(1)}, u32[]{:S(2)}, u32[]{:S(2)}) collective-permute-start(s32[128,4096]{1,0:T(8,128)} %near_ref.1), channel_id=1, source_target_pairs={{0,16},{16,0},{1,17},{17,1},{2,18},{18,2},{3,19},{19,3},{4,20},{20... | collective-permute-start | bytes 6291464 | tf_op jit(solution)/shard_map/ppermute | solution.py:187
  27.5 1.9 collective-permute-start
  31.4 4.6 %collective-permute-start.3 = (bf16[32,4096]{1,0:T(8,128)(2,1)S(1)}, bf16[32,4096]{1,0:T(8,128)(2,1)S(1)}, u32[]{:S(2)}, u32[]{:S(2)}) collective-permute-start(bf16[32,4096]{1,0:T(8,128)(2,1)S(1)} %collective-permute-done.2.refs_1_), channel_id=1, source_target_pairs={{0,480},{32,0},{64,32},{96,64},{128,96},{160,128},{192,160},{224,1... | collective-permute-start | bytes 786440 | tf_op jit(solution)/shard_map/ppermute | solution.py:169
  37.9 2.0 %collective-permute-done.10.refs_14_ = bf16[32,4096]{1,0:T(8,128)(2,1)S(1)} collective-permute-done((bf16[32,4096]{1,0:T(8,128)(2,1)S(1)}, bf16[32,4096]{1,0:T(8,128)(2,1)S(1)}, u32[]{:S(2)}, u32[]{:S(2)}) %collective-permute-start.10) | collective-permute-done | bytes 262176 | tf_op jit(solution)/shard_map/ppermute | solution.py:166
  39.9 2.6 %collective-permute-start.19 = (bf16[32,4096]{1,0:T(8,128)(2,1)S(1)}, bf16[32,4096]{1,0:T(8,128)(2,1)S(1)}, u32[]{:S(2)}, u32[]{:S(2)}) collective-permute-start(bf16[32,4096]{1,0:T(8,128)(2,1)S(1)} %collective-permute-done.18.refs_17_), channel_id=1, source_target_pairs={{0,480},{32,0},{64,32},{96,64},{128,96},{160,128},{192,160},{224,1... | collective-permute-start | bytes 786440 | tf_op jit(solution)/shard_map/ppermute | solution.py:169
  42.6 2.7 %collective-permute-start.11 = (bf16[32,4096]{1,0:T(8,128)(2,1)S(1)}, bf16[32,4096]{1,0:T(8,128)(2,1)S(1)}, u32[]{:S(2)}, u32[]{:S(2)}) collective-permute-start(bf16[32,4096]{1,0:T(8,128)(2,1)S(1)} %collective-permute-done.10.refs_14_), channel_id=1, source_target_pairs={{0,32},{32,64},{64,96},{96,128},{128,160},{160,192},{192,224},{224... | collective-permute-start | bytes 786440 | tf_op jit(solution)/shard_map/ppermute | solution.py:166
  47.8 4.6 %collective-permute-start.4 = (bf16[32,4096]{1,0:T(8,128)(2,1)S(1)}, bf16[32,4096]{1,0:T(8,128)(2,1)S(1)}, u32[]{:S(2)}, u32[]{:S(2)}) collective-permute-start(bf16[32,4096]{1,0:T(8,128)(2,1)S(1)} %collective-permute-done.3.refs_2_), channel_id=1, source_target_pairs={{0,480},{32,0},{64,32},{96,64},{128,96},{160,128},{192,160},{224,1... | collective-permute-start | bytes 786440 | tf_op jit(solution)/shard_map/ppermute | solution.py:169
  52.4 2.0 %collective-permute-start.20 = (bf16[32,4096]{1,0:T(8,128)(2,1)S(1)}, bf16[32,4096]{1,0:T(8,128)(2,1)S(1)}, u32[]{:S(2)}, u32[]{:S(2)}) collective-permute-start(bf16[32,4096]{1,0:T(8,128)(2,1)S(1)} %collective-permute-done.19.refs_18_), channel_id=1, source_target_pairs={{0,480},{32,0},{64,32},{96,64},{128,96},{160,128},{192,160},{224,1... | collective-permute-start | bytes 786440 | tf_op jit(solution)/shard_map/ppermute | solution.py:169
  54.5 3.3 %collective-permute-start.12 = (bf16[32,4096]{1,0:T(8,128)(2,1)S(1)}, bf16[32,4096]{1,0:T(8,128)(2,1)S(1)}, u32[]{:S(2)}, u32[]{:S(2)}) collective-permute-start(bf16[32,4096]{1,0:T(8,128)(2,1)S(1)} %collective-permute-done.11.refs_13_), channel_id=1, source_target_pairs={{0,32},{32,64},{64,96},{96,128},{128,160},{160,192},{192,224},{224... | collective-permute-start | bytes 786440 | tf_op jit(solution)/shard_map/ppermute | solution.py:166
  59.8 4.6 %collective-permute-start.5 = (bf16[32,4096]{1,0:T(8,128)(2,1)S(1)}, bf16[32,4096]{1,0:T(8,128)(2,1)S(1)}, u32[]{:S(2)}, u32[]{:S(2)}) collective-permute-start(bf16[32,4096]{1,0:T(8,128)(2,1)S(1)} %collective-permute-done.4.refs_3_), channel_id=1, source_target_pairs={{0,480},{32,0},{64,32},{96,64},{128,96},{160,128},{192,160},{224,1... | collective-permute-start | bytes 786440 | tf_op jit(solution)/shard_map/ppermute | solution.py:169
  64.4 2.3 %collective-permute-start.21 = (bf16[32,4096]{1,0:T(8,128)(2,1)S(1)}, bf16[32,4096]{1,0:T(8,128)(2,1)S(1)}, u32[]{:S(2)}, u32[]{:S(2)}) collective-permute-start(bf16[32,4096]{1,0:T(8,128)(2,1)S(1)} %collective-permute-done.20.refs_19_), channel_id=1, source_target_pairs={{0,480},{32,0},{64,32},{96,64},{128,96},{160,128},{192,160},{224,1... | collective-permute-start | bytes 786440 | tf_op jit(solution)/shard_map/ppermute | solution.py:169
  66.7 3.0 %collective-permute-start.13 = (bf16[32,4096]{1,0:T(8,128)(2,1)S(1)}, bf16[32,4096]{1,0:T(8,128)(2,1)S(1)}, u32[]{:S(2)}, u32[]{:S(2)}) collective-permute-start(bf16[32,4096]{1,0:T(8,128)(2,1)S(1)} %collective-permute-done.12.refs_12_), channel_id=1, source_target_pairs={{0,32},{32,64},{64,96},{96,128},{128,160},{160,192},{192,224},{224... | collective-permute-start | bytes 786440 | tf_op jit(solution)/shard_map/ppermute | solution.py:166
  71.7 4.6 %collective-permute-start.6 = (bf16[32,4096]{1,0:T(8,128)(2,1)S(1)}, bf16[32,4096]{1,0:T(8,128)(2,1)S(1)}, u32[]{:S(2)}, u32[]{:S(2)}) collective-permute-start(bf16[32,4096]{1,0:T(8,128)(2,1)S(1)} %collective-permute-done.5.refs_4_), channel_id=1, source_target_pairs={{0,480},{32,0},{64,32},{96,64},{128,96},{160,128},{192,160},{224,1... | collective-permute-start | bytes 786440 | tf_op jit(solution)/shard_map/ppermute | solution.py:169
  76.3 2.3 %collective-permute-start.22 = (bf16[32,4096]{1,0:T(8,128)(2,1)S(1)}, bf16[32,4096]{1,0:T(8,128)(2,1)S(1)}, u32[]{:S(2)}, u32[]{:S(2)}) collective-permute-start(bf16[32,4096]{1,0:T(8,128)(2,1)S(1)} %collective-permute-done.21.refs_20_), channel_id=1, source_target_pairs={{0,480},{32,0},{64,32},{96,64},{128,96},{160,128},{192,160},{224,1... | collective-permute-start | bytes 786440 | tf_op jit(solution)/shard_map/ppermute | solution.py:169
  78.6 3.0 %collective-permute-start.14 = (bf16[32,4096]{1,0:T(8,128)(2,1)S(1)}, bf16[32,4096]{1,0:T(8,128)(2,1)S(1)}, u32[]{:S(2)}, u32[]{:S(2)}) collective-permute-start(bf16[32,4096]{1,0:T(8,128)(2,1)S(1)} %collective-permute-done.13.refs_11_), channel_id=1, source_target_pairs={{0,32},{32,64},{64,96},{96,128},{128,160},{160,192},{192,224},{224... | collective-permute-start | bytes 786440 | tf_op jit(solution)/shard_map/ppermute | solution.py:166
  83.6 4.6 %collective-permute-start.7 = (bf16[32,4096]{1,0:T(8,128)(2,1)S(1)}, bf16[32,4096]{1,0:T(8,128)(2,1)}, u32[]{:S(2)}, u32[]{:S(2)}) collective-permute-start(bf16[32,4096]{1,0:T(8,128)(2,1)S(1)} %collective-permute-done.6.refs_5_), channel_id=1, source_target_pairs={{0,480},{32,0},{64,32},{96,64},{128,96},{160,128},{192,160},{224,1... | collective-permute-start | bytes 786440 | tf_op jit(solution)/shard_map/ppermute | solution.py:169
  88.2 2.3 %collective-permute-start.23 = (bf16[32,4096]{1,0:T(8,128)(2,1)S(1)}, bf16[32,4096]{1,0:T(8,128)(2,1)}, u32[]{:S(2)}, u32[]{:S(2)}) collective-permute-start(bf16[32,4096]{1,0:T(8,128)(2,1)S(1)} %collective-permute-done.22.refs_21_), channel_id=1, source_target_pairs={{0,480},{32,0},{64,32},{96,64},{128,96},{160,128},{192,160},{224,1... | collective-permute-start | bytes 786440 | tf_op jit(solution)/shard_map/ppermute | solution.py:169
  90.5 3.0 %collective-permute-start.15 = (bf16[32,4096]{1,0:T(8,128)(2,1)S(1)}, bf16[32,4096]{1,0:T(8,128)(2,1)}, u32[]{:S(2)}, u32[]{:S(2)}) collective-permute-start(bf16[32,4096]{1,0:T(8,128)(2,1)S(1)} %collective-permute-done.14.refs_10_), channel_id=1, source_target_pairs={{0,32},{32,64},{64,96},{96,128},{128,160},{160,192},{192,224},{224... | collective-permute-start | bytes 786440 | tf_op jit(solution)/shard_map/ppermute | solution.py:166
  93.6 1.9 collective-permute-start.31
  95.5 4.6 %collective-permute-start.8 = (bf16[32,4096]{1,0:T(8,128)(2,1)}, bf16[32,4096]{1,0:T(8,128)(2,1)}, u32[]{:S(2)}, u32[]{:S(2)}) collective-permute-start(bf16[32,4096]{1,0:T(8,128)(2,1)} %collective-permute-done.7.refs_6_), channel_id=1, source_target_pairs={{0,480},{32,0},{64,32},{96,64},{128,96},{160,128},{192,160},{224,1... | collective-permute-start | bytes 786440 | tf_op jit(solution)/shard_map/ppermute | solution.py:169
  100.1 2.3 %collective-permute-start.24 = (bf16[32,4096]{1,0:T(8,128)(2,1)}, bf16[32,4096]{1,0:T(8,128)(2,1)}, u32[]{:S(2)}, u32[]{:S(2)}) collective-permute-start(bf16[32,4096]{1,0:T(8,128)(2,1)} %collective-permute-done.23.refs_22_), channel_id=1, source_target_pairs={{0,480},{32,0},{64,32},{96,64},{128,96},{160,128},{192,160},{224,1... | collective-permute-start | bytes 786440 | tf_op jit(solution)/shard_map/ppermute | solution.py:169
  102.4 3.0 %collective-permute-start.16 = (bf16[32,4096]{1,0:T(8,128)(2,1)}, bf16[32,4096]{1,0:T(8,128)(2,1)}, u32[]{:S(2)}, u32[]{:S(2)}) collective-permute-start(bf16[32,4096]{1,0:T(8,128)(2,1)} %collective-permute-done.15.refs_9_), channel_id=1, source_target_pairs={{0,32},{32,64},{64,96},{96,128},{128,160},{160,192},{192,224},{224... | collective-permute-start | bytes 786440 | tf_op jit(solution)/shard_map/ppermute | solution.py:166
  108.3 3.5 %collective-permute-done.16.refs_8_ = bf16[32,4096]{1,0:T(8,128)(2,1)} collective-permute-done((bf16[32,4096]{1,0:T(8,128)(2,1)}, bf16[32,4096]{1,0:T(8,128)(2,1)}, u32[]{:S(2)}, u32[]{:S(2)}) %collective-permute-start.16) | collective-permute-done | bytes 262176 | tf_op jit(solution)/shard_map/ppermute | solution.py:166
  111.8 2.8 %collective-permute-done.32.refs_24_ = bf16[32,4096]{1,0:T(8,128)(2,1)} collective-permute-done((bf16[32,4096]{1,0:T(8,128)(2,1)}, bf16[32,4096]{1,0:T(8,128)(2,1)}, u32[]{:S(2)}, u32[]{:S(2)}) %collective-permute-start.32) | collective-permute-done | bytes 262176 | tf_op jit(solution)/shard_map/ppermute | solution.py:166
  114.6 18.1 %sampled_gradient.1 = f32[64,128]{1,0:T(8,128)} custom-call(s32[1]{0:T(128)} %bitcast.place_ref, s32[64,128]{1,0:T(8,128)} %bitcast.12, bf16[2,1024,128]{2,1,0:T(8,128)(2,1)} %near_act_ref.1, bf16[2,1024,128]{2,1,0:T(8,128)(2,1)} %copy-done.2, s32[128,4096]{1,0:T(8,128)} %copy-done, bf16[2,256,512]{2,1,0:T(8,128)(2,1)} %constant.42.clone.table_ref, ...), custom_call_target="tpu_custom_call" | custom-call | tf_op jit(solution)/shard_map/sampled_gradient/pallas_call | solution.py:126
  132.7 17.3 %all-to-all-start = ((f32[32,1,256]{2,1,0:T(1,128)}), f32[32,1,256]{2,1,0:T(1,128)S(1)}, u32[]{:S(2)}, u32[]{:S(2)}) async-start(f32[32,1,256]{2,1,0:T(1,128)} %bitcast.11), calls=%async_computation | async-start | bytes 65536 | tf_op jit(solution)/shard_map/all_to_all | solution.py:193
  150.6 11.2 %all-to-all-done = f32[32,1,256]{2,1,0:T(1,128)S(1)} async-done(((f32[32,1,256]{2,1,0:T(1,128)}), f32[32,1,256]{2,1,0:T(1,128)S(1)}, u32[]{:S(2)}, u32[]{:S(2)}) %all-to-all-start) | async-done | bytes 32800 | tf_op jit(solution)/shard_map/all_to_all | solution.py:193
  162.1 13.0 %all_to_all.19 = f32[16,2,256]{2,1,0:T(2,128)S(1)} all-to-all(f32[16,2,256]{2,1,0:T(2,128)S(1)} %broadcast_in_dim.7), channel_id=1, replica_groups=mesh['z'=16,'core'=2,'ex'=16] {'ex'}, dimensions={0} | all-to-all | bytes 65536 | tf_op jit(solution)/shard_map/all_to_all | solution.py:175
  175.3 17.6 %all_to_all.20 = f32[32,2,32]{2,1,0:T(2,128)S(1)} all-to-all(f32[32,2,32]{2,1,0:T(2,128)S(1)} %broadcast_in_dim.8), channel_id=1, replica_groups=mesh['z'=16,'core'=2,'ex'=16] {'z','core'}, dimensions={0} | all-to-all | bytes 16384 | tf_op jit(solution)/shard_map/all_to_all | solution.py:175
  (105 shorter events, 21.7 us)
Async XLA Ops:
  1.7 16.5 %collective-permute-start.17 = (bf16[32,4096]{1,0:T(8,128)(2,1)S(1)}, bf16[32,4096]{1,0:T(8,128)(2,1)S(1)}, u32[]{:S(2)}, u32[]{:S(2)}) collective-permute-start(bf16[32,4096]{1,0:T(8,128)(2,1)S(1)} %get-tuple-element.2), channel_id=1, source_target_pairs={{0,16},{16,0},{1,17},{17,1},{2,18},{18,2},{3,19},{19,3},{4,20},{20... | collective-permute-start | bytes 786440 | tf_op jit(solution)/shard_map/ppermute | solution.py:185
  10.5 17.0 %collective-permute-start.9 = (bf16[32,4096]{1,0:T(8,128)(2,1)S(1)}, bf16[32,4096]{1,0:T(8,128)(2,1)S(1)}, u32[]{:S(2)}, u32[]{:S(2)}) collective-permute-start(bf16[32,4096]{1,0:T(8,128)(2,1)S(1)} %get-tuple-element.3.refs_0_), channel_id=1, source_target_pairs={{0,32},{32,64},{64,96},{96,128},{128,160},{160,192},{192,224},{224... | collective-permute-start | bytes 786440 | tf_op jit(solution)/shard_map/ppermute | solution.py:166
  12.4 17.0 %collective-permute-start.2 = (bf16[32,4096]{1,0:T(8,128)(2,1)S(1)}, bf16[32,4096]{1,0:T(8,128)(2,1)S(1)}, u32[]{:S(2)}, u32[]{:S(2)}) collective-permute-start(bf16[32,4096]{1,0:T(8,128)(2,1)S(1)} %get-tuple-element.3.refs_0_), channel_id=1, source_target_pairs={{0,480},{32,0},{64,32},{96,64},{128,96},{160,128},{192,160},{224,1... | collective-permute-start | bytes 786440 | tf_op jit(solution)/shard_map/ppermute | solution.py:169
  18.2 13.2 %collective-permute-start.25 = (bf16[32,4096]{1,0:T(8,128)(2,1)S(1)}, bf16[32,4096]{1,0:T(8,128)(2,1)S(1)}, u32[]{:S(2)}, u32[]{:S(2)}) collective-permute-start(bf16[32,4096]{1,0:T(8,128)(2,1)S(1)} %collective-permute-done.17.refs_16_), channel_id=1, source_target_pairs={{0,32},{32,64},{64,96},{96,128},{128,160},{160,192},{192,224},{224... | collective-permute-start | bytes 786440 | tf_op jit(solution)/shard_map/ppermute | solution.py:166
  20.1 15.9 %collective-permute-start.18 = (bf16[32,4096]{1,0:T(8,128)(2,1)S(1)}, bf16[32,4096]{1,0:T(8,128)(2,1)S(1)}, u32[]{:S(2)}, u32[]{:S(2)}) collective-permute-start(bf16[32,4096]{1,0:T(8,128)(2,1)S(1)} %collective-permute-done.17.refs_16_), channel_id=1, source_target_pairs={{0,480},{32,0},{64,32},{96,64},{128,96},{160,128},{192,160},{224,1... | collective-permute-start | bytes 786440 | tf_op jit(solution)/shard_map/ppermute | solution.py:169
  24.7 87.0 %collective-permute-start.1 = (s32[128,4096]{1,0:T(8,128)}, s32[128,4096]{1,0:T(8,128)S(1)}, u32[]{:S(2)}, u32[]{:S(2)}) collective-permute-start(s32[128,4096]{1,0:T(8,128)} %near_ref.1), channel_id=1, source_target_pairs={{0,16},{16,0},{1,17},{17,1},{2,18},{18,2},{3,19},{19,3},{4,20},{20... | collective-permute-start | bytes 6291464 | tf_op jit(solution)/shard_map/ppermute | solution.py:187
  27.5 20.3 %collective-permute-start = (bf16[2,1024,128]{2,1,0:T(8,128)(2,1)}, bf16[2,1024,128]{2,1,0:T(8,128)(2,1)S(1)}, u32[]{:S(2)}, u32[]{:S(2)}) collective-permute-start(bf16[2,1024,128]{2,1,0:T(8,128)(2,1)} %near_act_ref.1), channel_id=1, source_target_pairs={{0,16},{16,0},{1,17},{17,1},{2,18},{18,2},{3,19},{19,3},{4,20},{20... | collective-permute-start | bytes 1572872 | tf_op jit(solution)/shard_map/ppermute | solution.py:186
  29.5 10.5 %collective-permute-start.10 = (bf16[32,4096]{1,0:T(8,128)(2,1)S(1)}, bf16[32,4096]{1,0:T(8,128)(2,1)S(1)}, u32[]{:S(2)}, u32[]{:S(2)}) collective-permute-start(bf16[32,4096]{1,0:T(8,128)(2,1)S(1)} %collective-permute-done.9.refs_15_), channel_id=1, source_target_pairs={{0,32},{32,64},{64,96},{96,128},{128,160},{160,192},{192,224},{224... | collective-permute-start | bytes 786440 | tf_op jit(solution)/shard_map/ppermute | solution.py:166
  31.4 11.1 %collective-permute-start.3 = (bf16[32,4096]{1,0:T(8,128)(2,1)S(1)}, bf16[32,4096]{1,0:T(8,128)(2,1)S(1)}, u32[]{:S(2)}, u32[]{:S(2)}) collective-permute-start(bf16[32,4096]{1,0:T(8,128)(2,1)S(1)} %collective-permute-done.2.refs_1_), channel_id=1, source_target_pairs={{0,480},{32,0},{64,32},{96,64},{128,96},{160,128},{192,160},{224,1... | collective-permute-start | bytes 786440 | tf_op jit(solution)/shard_map/ppermute | solution.py:169
  36.0 9.8 %collective-permute-start.26 = (bf16[32,4096]{1,0:T(8,128)(2,1)S(1)}, bf16[32,4096]{1,0:T(8,128)(2,1)S(1)}, u32[]{:S(2)}, u32[]{:S(2)}) collective-permute-start(bf16[32,4096]{1,0:T(8,128)(2,1)S(1)} %collective-permute-done.25.refs_31_), channel_id=1, source_target_pairs={{0,32},{32,64},{64,96},{96,128},{128,160},{160,192},{192,224},{224... | collective-permute-start | bytes 786440 | tf_op jit(solution)/shard_map/ppermute | solution.py:166
  39.9 12.5 %collective-permute-start.19 = (bf16[32,4096]{1,0:T(8,128)(2,1)S(1)}, bf16[32,4096]{1,0:T(8,128)(2,1)S(1)}, u32[]{:S(2)}, u32[]{:S(2)}) collective-permute-start(bf16[32,4096]{1,0:T(8,128)(2,1)S(1)} %collective-permute-done.18.refs_17_), channel_id=1, source_target_pairs={{0,480},{32,0},{64,32},{96,64},{128,96},{160,128},{192,160},{224,1... | collective-permute-start | bytes 786440 | tf_op jit(solution)/shard_map/ppermute | solution.py:169
  42.6 11.9 %collective-permute-start.11 = (bf16[32,4096]{1,0:T(8,128)(2,1)S(1)}, bf16[32,4096]{1,0:T(8,128)(2,1)S(1)}, u32[]{:S(2)}, u32[]{:S(2)}) collective-permute-start(bf16[32,4096]{1,0:T(8,128)(2,1)S(1)} %collective-permute-done.10.refs_14_), channel_id=1, source_target_pairs={{0,32},{32,64},{64,96},{96,128},{128,160},{160,192},{192,224},{224... | collective-permute-start | bytes 786440 | tf_op jit(solution)/shard_map/ppermute | solution.py:166
  45.9 11.9 %collective-permute-start.27 = (bf16[32,4096]{1,0:T(8,128)(2,1)S(1)}, bf16[32,4096]{1,0:T(8,128)(2,1)S(1)}, u32[]{:S(2)}, u32[]{:S(2)}) collective-permute-start(bf16[32,4096]{1,0:T(8,128)(2,1)S(1)} %collective-permute-done.26.refs_30_), channel_id=1, source_target_pairs={{0,32},{32,64},{64,96},{96,128},{128,160},{160,192},{192,224},{224... | collective-permute-start | bytes 786440 | tf_op jit(solution)/shard_map/ppermute | solution.py:166
  47.8 11.9 %collective-permute-start.4 = (bf16[32,4096]{1,0:T(8,128)(2,1)S(1)}, bf16[32,4096]{1,0:T(8,128)(2,1)S(1)}, u32[]{:S(2)}, u32[]{:S(2)}) collective-permute-start(bf16[32,4096]{1,0:T(8,128)(2,1)S(1)} %collective-permute-done.3.refs_2_), channel_id=1, source_target_pairs={{0,480},{32,0},{64,32},{96,64},{128,96},{160,128},{192,160},{224,1... | collective-permute-start | bytes 786440 | tf_op jit(solution)/shard_map/ppermute | solution.py:169
  52.4 11.9 %collective-permute-start.20 = (bf16[32,4096]{1,0:T(8,128)(2,1)S(1)}, bf16[32,4096]{1,0:T(8,128)(2,1)S(1)}, u32[]{:S(2)}, u32[]{:S(2)}) collective-permute-start(bf16[32,4096]{1,0:T(8,128)(2,1)S(1)} %collective-permute-done.19.refs_18_), channel_id=1, source_target_pairs={{0,480},{32,0},{64,32},{96,64},{128,96},{160,128},{192,160},{224,1... | collective-permute-start | bytes 786440 | tf_op jit(solution)/shard_map/ppermute | solution.py:169
  54.5 12.1 %collective-permute-start.12 = (bf16[32,4096]{1,0:T(8,128)(2,1)S(1)}, bf16[32,4096]{1,0:T(8,128)(2,1)S(1)}, u32[]{:S(2)}, u32[]{:S(2)}) collective-permute-start(bf16[32,4096]{1,0:T(8,128)(2,1)S(1)} %collective-permute-done.11.refs_13_), channel_id=1, source_target_pairs={{0,32},{32,64},{64,96},{96,128},{128,160},{160,192},{192,224},{224... | collective-permute-start | bytes 786440 | tf_op jit(solution)/shard_map/ppermute | solution.py:166
  57.8 11.9 %collective-permute-start.28 = (bf16[32,4096]{1,0:T(8,128)(2,1)S(1)}, bf16[32,4096]{1,0:T(8,128)(2,1)S(1)}, u32[]{:S(2)}, u32[]{:S(2)}) collective-permute-start(bf16[32,4096]{1,0:T(8,128)(2,1)S(1)} %collective-permute-done.27.refs_29_), channel_id=1, source_target_pairs={{0,32},{32,64},{64,96},{96,128},{128,160},{160,192},{192,224},{224... | collective-permute-start | bytes 786440 | tf_op jit(solution)/shard_map/ppermute | solution.py:166
  59.8 11.9 %collective-permute-start.5 = (bf16[32,4096]{1,0:T(8,128)(2,1)S(1)}, bf16[32,4096]{1,0:T(8,128)(2,1)S(1)}, u32[]{:S(2)}, u32[]{:S(2)}) collective-permute-start(bf16[32,4096]{1,0:T(8,128)(2,1)S(1)} %collective-permute-done.4.refs_3_), channel_id=1, source_target_pairs={{0,480},{32,0},{64,32},{96,64},{128,96},{160,128},{192,160},{224,1... | collective-permute-start | bytes 786440 | tf_op jit(solution)/shard_map/ppermute | solution.py:169
  64.4 11.9 %collective-permute-start.21 = (bf16[32,4096]{1,0:T(8,128)(2,1)S(1)}, bf16[32,4096]{1,0:T(8,128)(2,1)S(1)}, u32[]{:S(2)}, u32[]{:S(2)}) collective-permute-start(bf16[32,4096]{1,0:T(8,128)(2,1)S(1)} %collective-permute-done.20.refs_19_), channel_id=1, source_target_pairs={{0,480},{32,0},{64,32},{96,64},{128,96},{160,128},{192,160},{224,1... | collective-permute-start | bytes 786440 | tf_op jit(solution)/shard_map/ppermute | solution.py:169
  66.7 11.9 %collective-permute-start.13 = (bf16[32,4096]{1,0:T(8,128)(2,1)S(1)}, bf16[32,4096]{1,0:T(8,128)(2,1)S(1)}, u32[]{:S(2)}, u32[]{:S(2)}) collective-permute-start(bf16[32,4096]{1,0:T(8,128)(2,1)S(1)} %collective-permute-done.12.refs_12_), channel_id=1, source_target_pairs={{0,32},{32,64},{64,96},{96,128},{128,160},{160,192},{192,224},{224... | collective-permute-start | bytes 786440 | tf_op jit(solution)/shard_map/ppermute | solution.py:166
  69.7 11.9 %collective-permute-start.29 = (bf16[32,4096]{1,0:T(8,128)(2,1)S(1)}, bf16[32,4096]{1,0:T(8,128)(2,1)S(1)}, u32[]{:S(2)}, u32[]{:S(2)}) collective-permute-start(bf16[32,4096]{1,0:T(8,128)(2,1)S(1)} %collective-permute-done.28.refs_28_), channel_id=1, source_target_pairs={{0,32},{32,64},{64,96},{96,128},{128,160},{160,192},{192,224},{224... | collective-permute-start | bytes 786440 | tf_op jit(solution)/shard_map/ppermute | solution.py:166
  71.7 11.9 %collective-permute-start.6 = (bf16[32,4096]{1,0:T(8,128)(2,1)S(1)}, bf16[32,4096]{1,0:T(8,128)(2,1)S(1)}, u32[]{:S(2)}, u32[]{:S(2)}) collective-permute-start(bf16[32,4096]{1,0:T(8,128)(2,1)S(1)} %collective-permute-done.5.refs_4_), channel_id=1, source_target_pairs={{0,480},{32,0},{64,32},{96,64},{128,96},{160,128},{192,160},{224,1... | collective-permute-start | bytes 786440 | tf_op jit(solution)/shard_map/ppermute | solution.py:169
  76.3 11.9 %collective-permute-start.22 = (bf16[32,4096]{1,0:T(8,128)(2,1)S(1)}, bf16[32,4096]{1,0:T(8,128)(2,1)S(1)}, u32[]{:S(2)}, u32[]{:S(2)}) collective-permute-start(bf16[32,4096]{1,0:T(8,128)(2,1)S(1)} %collective-permute-done.21.refs_20_), channel_id=1, source_target_pairs={{0,480},{32,0},{64,32},{96,64},{128,96},{160,128},{192,160},{224,1... | collective-permute-start | bytes 786440 | tf_op jit(solution)/shard_map/ppermute | solution.py:169
  78.6 11.9 %collective-permute-start.14 = (bf16[32,4096]{1,0:T(8,128)(2,1)S(1)}, bf16[32,4096]{1,0:T(8,128)(2,1)S(1)}, u32[]{:S(2)}, u32[]{:S(2)}) collective-permute-start(bf16[32,4096]{1,0:T(8,128)(2,1)S(1)} %collective-permute-done.13.refs_11_), channel_id=1, source_target_pairs={{0,32},{32,64},{64,96},{96,128},{128,160},{160,192},{192,224},{224... | collective-permute-start | bytes 786440 | tf_op jit(solution)/shard_map/ppermute | solution.py:166
  81.7 11.9 %collective-permute-start.30 = (bf16[32,4096]{1,0:T(8,128)(2,1)S(1)}, bf16[32,4096]{1,0:T(8,128)(2,1)S(1)}, u32[]{:S(2)}, u32[]{:S(2)}) collective-permute-start(bf16[32,4096]{1,0:T(8,128)(2,1)S(1)} %collective-permute-done.29.refs_27_), channel_id=1, source_target_pairs={{0,32},{32,64},{64,96},{96,128},{128,160},{160,192},{192,224},{224... | collective-permute-start | bytes 786440 | tf_op jit(solution)/shard_map/ppermute | solution.py:166
  83.6 11.9 %collective-permute-start.7 = (bf16[32,4096]{1,0:T(8,128)(2,1)S(1)}, bf16[32,4096]{1,0:T(8,128)(2,1)}, u32[]{:S(2)}, u32[]{:S(2)}) collective-permute-start(bf16[32,4096]{1,0:T(8,128)(2,1)S(1)} %collective-permute-done.6.refs_5_), channel_id=1, source_target_pairs={{0,480},{32,0},{64,32},{96,64},{128,96},{160,128},{192,160},{224,1... | collective-permute-start | bytes 786440 | tf_op jit(solution)/shard_map/ppermute | solution.py:169
  88.2 11.9 %collective-permute-start.23 = (bf16[32,4096]{1,0:T(8,128)(2,1)S(1)}, bf16[32,4096]{1,0:T(8,128)(2,1)}, u32[]{:S(2)}, u32[]{:S(2)}) collective-permute-start(bf16[32,4096]{1,0:T(8,128)(2,1)S(1)} %collective-permute-done.22.refs_21_), channel_id=1, source_target_pairs={{0,480},{32,0},{64,32},{96,64},{128,96},{160,128},{192,160},{224,1... | collective-permute-start | bytes 786440 | tf_op jit(solution)/shard_map/ppermute | solution.py:169
  90.5 11.9 %collective-permute-start.15 = (bf16[32,4096]{1,0:T(8,128)(2,1)S(1)}, bf16[32,4096]{1,0:T(8,128)(2,1)}, u32[]{:S(2)}, u32[]{:S(2)}) collective-permute-start(bf16[32,4096]{1,0:T(8,128)(2,1)S(1)} %collective-permute-done.14.refs_10_), channel_id=1, source_target_pairs={{0,32},{32,64},{64,96},{96,128},{128,160},{160,192},{192,224},{224... | collective-permute-start | bytes 786440 | tf_op jit(solution)/shard_map/ppermute | solution.py:166
  93.6 11.9 %collective-permute-start.31 = (bf16[32,4096]{1,0:T(8,128)(2,1)S(1)}, bf16[32,4096]{1,0:T(8,128)(2,1)}, u32[]{:S(2)}, u32[]{:S(2)}) collective-permute-start(bf16[32,4096]{1,0:T(8,128)(2,1)S(1)} %collective-permute-done.30.refs_26_), channel_id=1, source_target_pairs={{0,32},{32,64},{64,96},{96,128},{128,160},{160,192},{192,224},{224... | collective-permute-start | bytes 786440 | tf_op jit(solution)/shard_map/ppermute | solution.py:166
  95.5 11.9 %collective-permute-start.8 = (bf16[32,4096]{1,0:T(8,128)(2,1)}, bf16[32,4096]{1,0:T(8,128)(2,1)}, u32[]{:S(2)}, u32[]{:S(2)}) collective-permute-start(bf16[32,4096]{1,0:T(8,128)(2,1)} %collective-permute-done.7.refs_6_), channel_id=1, source_target_pairs={{0,480},{32,0},{64,32},{96,64},{128,96},{160,128},{192,160},{224,1... | collective-permute-start | bytes 786440 | tf_op jit(solution)/shard_map/ppermute | solution.py:169
  102.4 9.3 %collective-permute-start.16 = (bf16[32,4096]{1,0:T(8,128)(2,1)}, bf16[32,4096]{1,0:T(8,128)(2,1)}, u32[]{:S(2)}, u32[]{:S(2)}) collective-permute-start(bf16[32,4096]{1,0:T(8,128)(2,1)} %collective-permute-done.15.refs_9_), channel_id=1, source_target_pairs={{0,32},{32,64},{64,96},{96,128},{128,160},{160,192},{192,224},{224... | collective-permute-start | bytes 786440 | tf_op jit(solution)/shard_map/ppermute | solution.py:166
  132.7 29.2 %all-to-all-start = ((f32[32,1,256]{2,1,0:T(1,128)}), f32[32,1,256]{2,1,0:T(1,128)S(1)}, u32[]{:S(2)}, u32[]{:S(2)}) async-start(f32[32,1,256]{2,1,0:T(1,128)} %bitcast.11), calls=%async_computation | async-start | bytes 65536 | tf_op jit(solution)/shard_map/all_to_all | solution.py:193
  (29 other events, 648.6 us)

commit v9 on v7

--- a/solution.py
+++ b/solution.py
@@ -33,7 +33,7 @@
     outer = mixed.shape[0] // rows
     width = outer * LANES
     piece, last = pl.program_id(0), pl.num_programs(0) - 1
-    core = place_ref[0]
+    here, core = lax.div(place_ref[0], 2), lax.rem(place_ref[0], 2)
     row_copy = pltpu.make_async_copy(rows_v, rows_s, sem)
 
     @pl.when(piece == 0)
@@ -46,7 +46,7 @@
         depth = grd_refs[0].shape[0]
         for which in range(2):
             for j in range(chips):
-                source = lax.rem(place_ref[1] + j, chips) * (2 * depth) + lax.rem(core + which, 2) * depth
+                source = lax.rem(here + j, chips) * (2 * depth) + lax.rem(core + which, 2) * depth
                 source = pl.ds(pl.multiple_of(source, depth), depth)
                 target = pl.ds((which * chips + j) * depth, depth)
                 tokens[target, :rows // 2] = near_act_ref[core, source, :]
@@ -114,7 +114,7 @@
         lax.fori_loop(0, stage.shape[0] // BATCH, inner_step, 0)
 
 
-def local_samples(near_act, far_act, blocks, near, far, core, here, sample_index):
+def local_samples(near_act, far_act, blocks, near, far, place, sample_index):
     tokens = near_act.shape[1]
     rows = 2 * near_act.shape[2]
     width = near.shape[1]
@@ -144,7 +144,7 @@
         compiler_params=pltpu.CompilerParams(vmem_limit_bytes=VMEM_MIB * 1024 * 1024),
         name="sampled_gradient",
     )(
-        jnp.stack([core, here]).astype(jnp.int32),
+        place[None],
         sample_index.reshape(count // LANES, LANES),
         near_act,
         far_act,
@@ -189,7 +189,7 @@
     far = lax.ppermute(near, "core", swap)
     blocks = around([mine, other], "z")
 
-    terms = local_samples(activations, far_act, blocks, near, far, core, here, sample_index)
+    terms = local_samples(activations, far_act, blocks, near, far, lax.axis_index(("z", "core")), sample_index)
     feature_count = sample_index.shape[0]
     per = feature_count // (2 * chips)
     terms = lax.all_to_all(terms.reshape(2 * chips, per), ("z", "core"), 0, 0, tiled=True)

time: 195 us -> 195 us (level)
  transfers between devices with their start and end apart: 34 -> 34, of which waited for: 4 -> 4; matrix products, arithmetic and copies ran while one was open for 2% -> 1% of each run, Pallas kernels for 0% -> 0%
where the time goes in v9:
time: 195 us; the launch traced here: 193 us
  starting transfers between devices  120 us (62%)
  blocking collectives  30.5 us (16%)
  waiting for transfers between devices  19.1 us (10%)
  Pallas kernels  17.6 us (9%)
  other arithmetic  2.58 us (1%)
  local copies, waits for them, and re-layouts  1.97 us (1%)
    ppermute x14, starting transfers between devices, around(): chain.append(lax.ppermute(chain[-1], axis, down))  54.3 us
    ppermute x14, starting transfers between devices, around(): chain.append(lax.ppermute(chain[-1], axis, up))  30.7 us
    all_to_all x2, blocking collectives, to_all(): lax.all_to_all(jnp.broadcast_to(value[None], (size,) + value.shape), axes...  30.5 us
    pallas_call x1, Pallas kernels, local_samples(): pl.pallas_call(sampled_gradient, grid=(width // WIDE,), out_shape=jax.Sha...  17.6 us
    all_to_all x1, starting transfers between devices, per_device(): lax.all_to_all(terms.reshape(2 * chips, per), ('z', 'core'), 0, 0, tiled=...  12.2 us
    all_to_all x1, waiting for transfers between devices, per_device(): lax.all_to_all(terms.reshape(2 * chips, per), ('z', 'core'), 0, 0, tiled=...  11.3 us
    ppermute x1, starting transfers between devices, per_device(): lax.ppermute(lax.dynamic_index_in_dim(out_grad, 1 - core, 0, keepdims=Fal...  8.79 us
    ppermute x1, waiting for transfers between devices, around(): ups[0].append(lax.ppermute(ups[0][-1], axis, up))  5.6 us
  transfers between devices with their start and end apart: 34, of which 4 were waited for; matrix products, arithmetic and copies ran while one was open for 1% of the time, Pallas kernels for 0%

profile of v9, /device:TPU:1, one launch (start us, length us, event | category | flops | bytes accessed | tf_op | source)
XLA Modules:
  0.0 193.2 jit_solution(12005748027765038368)
XLA Ops:
  1.7 8.8 %collective-permute-start.17 = (bf16[32,4096]{1,0:T(8,128)(2,1)S(1)}, bf16[32,4096]{1,0:T(8,128)(2,1)S(1)}, u32[]{:S(2)}, u32[]{:S(2)}) collective-permute-start(bf16[32,4096]{1,0:T(8,128)(2,1)S(1)} %get-tuple-element.2), channel_id=1, source_target_pairs={{0,16},{16,0},{1,17},{17,1},{2,18},{18,2},{3,19},{19,3},{4,20},{20... | collective-permute-start | bytes 786440 | tf_op jit(solution)/shard_map/ppermute | solution.py:186
  12.5 5.7 %collective-permute-start.18 = (bf16[32,4096]{1,0:T(8,128)(2,1)S(1)}, bf16[32,4096]{1,0:T(8,128)(2,1)S(1)}, u32[]{:S(2)}, u32[]{:S(2)}) collective-permute-start(bf16[32,4096]{1,0:T(8,128)(2,1)S(1)} %collective-permute-done.17.refs_16_), channel_id=1, source_target_pairs={{0,480},{32,0},{64,32},{96,64},{128,96},{160,128},{192,160},{224,1... | collective-permute-start | bytes 786440 | tf_op jit(solution)/shard_map/ppermute | solution.py:168
  18.2 3.4 %collective-permute-start.2 = (bf16[32,4096]{1,0:T(8,128)(2,1)S(1)}, bf16[32,4096]{1,0:T(8,128)(2,1)S(1)}, u32[]{:S(2)}, u32[]{:S(2)}) collective-permute-start(bf16[32,4096]{1,0:T(8,128)(2,1)S(1)} %get-tuple-element.3.refs_0_), channel_id=1, source_target_pairs={{0,480},{32,0},{64,32},{96,64},{128,96},{160,128},{192,160},{224,1... | collective-permute-start | bytes 786440 | tf_op jit(solution)/shard_map/ppermute | solution.py:168
  25.5 4.6 %collective-permute-start.19 = (bf16[32,4096]{1,0:T(8,128)(2,1)S(1)}, bf16[32,4096]{1,0:T(8,128)(2,1)S(1)}, u32[]{:S(2)}, u32[]{:S(2)}) collective-permute-start(bf16[32,4096]{1,0:T(8,128)(2,1)S(1)} %collective-permute-done.18.refs_17_), channel_id=1, source_target_pairs={{0,480},{32,0},{64,32},{96,64},{128,96},{160,128},{192,160},{224,1... | collective-permute-start | bytes 786440 | tf_op jit(solution)/shard_map/ppermute | solution.py:168
  30.1 4.8 %collective-permute-start.3 = (bf16[32,4096]{1,0:T(8,128)(2,1)S(1)}, bf16[32,4096]{1,0:T(8,128)(2,1)S(1)}, u32[]{:S(2)}, u32[]{:S(2)}) collective-permute-start(bf16[32,4096]{1,0:T(8,128)(2,1)S(1)} %collective-permute-done.2.refs_1_), channel_id=1, source_target_pairs={{0,480},{32,0},{64,32},{96,64},{128,96},{160,128},{192,160},{224,1... | collective-permute-start | bytes 786440 | tf_op jit(solution)/shard_map/ppermute | solution.py:168
  34.9 1.9 collective-permute-start.27
  39.2 4.6 %collective-permute-start.20 = (bf16[32,4096]{1,0:T(8,128)(2,1)S(1)}, bf16[32,4096]{1,0:T(8,128)(2,1)S(1)}, u32[]{:S(2)}, u32[]{:S(2)}) collective-permute-start(bf16[32,4096]{1,0:T(8,128)(2,1)S(1)} %collective-permute-done.19.refs_18_), channel_id=1, source_target_pairs={{0,480},{32,0},{64,32},{96,64},{128,96},{160,128},{192,160},{224,1... | collective-permute-start | bytes 786440 | tf_op jit(solution)/shard_map/ppermute | solution.py:168
  43.8 4.2 %collective-permute-start = (bf16[2,1024,128]{2,1,0:T(8,128)(2,1)}, bf16[2,1024,128]{2,1,0:T(8,128)(2,1)S(1)}, u32[]{:S(2)}, u32[]{:S(2)}) collective-permute-start(bf16[2,1024,128]{2,1,0:T(8,128)(2,1)} %near_act_ref.1), channel_id=1, source_target_pairs={{0,16},{16,0},{1,17},{17,1},{2,18},{18,2},{3,19},{19,3},{4,20},{20... | collective-permute-start | bytes 1572872 | tf_op jit(solution)/shard_map/ppermute | solution.py:187
  48.1 2.5 %collective-permute-start.4 = (bf16[32,4096]{1,0:T(8,128)(2,1)S(1)}, bf16[32,4096]{1,0:T(8,128)(2,1)S(1)}, u32[]{:S(2)}, u32[]{:S(2)}) collective-permute-start(bf16[32,4096]{1,0:T(8,128)(2,1)S(1)} %collective-permute-done.3.refs_2_), channel_id=1, source_target_pairs={{0,480},{32,0},{64,32},{96,64},{128,96},{160,128},{192,160},{224,1... | collective-permute-start | bytes 786440 | tf_op jit(solution)/shard_map/ppermute | solution.py:168
  50.6 2.8 %collective-permute-start.28 = (bf16[32,4096]{1,0:T(8,128)(2,1)S(1)}, bf16[32,4096]{1,0:T(8,128)(2,1)S(1)}, u32[]{:S(2)}, u32[]{:S(2)}) collective-permute-start(bf16[32,4096]{1,0:T(8,128)(2,1)S(1)} %collective-permute-done.27.refs_30_), channel_id=1, source_target_pairs={{0,32},{32,64},{64,96},{96,128},{128,160},{160,192},{192,224},{224... | collective-permute-start | bytes 786440 | tf_op jit(solution)/shard_map/ppermute | solution.py:166
  55.4 4.6 %collective-permute-start.21 = (bf16[32,4096]{1,0:T(8,128)(2,1)S(1)}, bf16[32,4096]{1,0:T(8,128)(2,1)S(1)}, u32[]{:S(2)}, u32[]{:S(2)}) collective-permute-start(bf16[32,4096]{1,0:T(8,128)(2,1)S(1)} %collective-permute-done.20.refs_19_), channel_id=1, source_target_pairs={{0,480},{32,0},{64,32},{96,64},{128,96},{160,128},{192,160},{224,1... | collective-permute-start | bytes 786440 | tf_op jit(solution)/shard_map/ppermute | solution.py:168
  61.8 3.0 %collective-permute-start.1 = (bf16[128,4096]{1,0:T(8,128)(2,1)S(1)}, bf16[128,4096]{1,0:T(8,128)(2,1)S(1)}, u32[]{:S(2)}, u32[]{:S(2)}) collective-permute-start(bf16[128,4096]{1,0:T(8,128)(2,1)S(1)} %select_convert_fusion.near_ref), channel_id=1, source_target_pairs={{0,16},{16,0},{1,17},{17,1},{2,18},{18,2},{3,19},{19,3},{4,20},{20... | collective-permute-start | bytes 3145736 | tf_op jit(solution)/shard_map/ppermute | solution.py:189
  64.9 2.5 %collective-permute-start.5 = (bf16[32,4096]{1,0:T(8,128)(2,1)S(1)}, bf16[32,4096]{1,0:T(8,128)(2,1)S(1)}, u32[]{:S(2)}, u32[]{:S(2)}) collective-permute-start(bf16[32,4096]{1,0:T(8,128)(2,1)S(1)} %collective-permute-done.4.refs_3_), channel_id=1, source_target_pairs={{0,480},{32,0},{64,32},{96,64},{128,96},{160,128},{192,160},{224,1... | collective-permute-start | bytes 786440 | tf_op jit(solution)/shard_map/ppermute | solution.py:168
  67.5 2.8 %collective-permute-start.29 = (bf16[32,4096]{1,0:T(8,128)(2,1)S(1)}, bf16[32,4096]{1,0:T(8,128)(2,1)S(1)}, u32[]{:S(2)}, u32[]{:S(2)}) collective-permute-start(bf16[32,4096]{1,0:T(8,128)(2,1)S(1)} %collective-permute-done.28.refs_29_), channel_id=1, source_target_pairs={{0,32},{32,64},{64,96},{96,128},{128,160},{160,192},{192,224},{224... | collective-permute-start | bytes 786440 | tf_op jit(solution)/shard_map/ppermute | solution.py:166
  72.2 4.6 %collective-permute-start.22 = (bf16[32,4096]{1,0:T(8,128)(2,1)S(1)}, bf16[32,4096]{1,0:T(8,128)(2,1)S(1)}, u32[]{:S(2)}, u32[]{:S(2)}) collective-permute-start(bf16[32,4096]{1,0:T(8,128)(2,1)S(1)} %collective-permute-done.21.refs_20_), channel_id=1, source_target_pairs={{0,480},{32,0},{64,32},{96,64},{128,96},{160,128},{192,160},{224,1... | collective-permute-start | bytes 786440 | tf_op jit(solution)/shard_map/ppermute | solution.py:168
  76.8 2.5 %collective-permute-start.6 = (bf16[32,4096]{1,0:T(8,128)(2,1)S(1)}, bf16[32,4096]{1,0:T(8,128)(2,1)S(1)}, u32[]{:S(2)}, u32[]{:S(2)}) collective-permute-start(bf16[32,4096]{1,0:T(8,128)(2,1)S(1)} %collective-permute-done.5.refs_4_), channel_id=1, source_target_pairs={{0,480},{32,0},{64,32},{96,64},{128,96},{160,128},{192,160},{224,1... | collective-permute-start | bytes 786440 | tf_op jit(solution)/shard_map/ppermute | solution.py:168
  79.4 2.8 %collective-permute-start.30 = (bf16[32,4096]{1,0:T(8,128)(2,1)S(1)}, bf16[32,4096]{1,0:T(8,128)(2,1)S(1)}, u32[]{:S(2)}, u32[]{:S(2)}) collective-permute-start(bf16[32,4096]{1,0:T(8,128)(2,1)S(1)} %collective-permute-done.29.refs_28_), channel_id=1, source_target_pairs={{0,32},{32,64},{64,96},{96,128},{128,160},{160,192},{192,224},{224... | collective-permute-start | bytes 786440 | tf_op jit(solution)/shard_map/ppermute | solution.py:166
  85.7 4.6 %collective-permute-start.23 = (bf16[32,4096]{1,0:T(8,128)(2,1)S(1)}, bf16[32,4096]{1,0:T(8,128)(2,1)S(1)}, u32[]{:S(2)}, u32[]{:S(2)}) collective-permute-start(bf16[32,4096]{1,0:T(8,128)(2,1)S(1)} %collective-permute-done.22.refs_21_), channel_id=1, source_target_pairs={{0,480},{32,0},{64,32},{96,64},{128,96},{160,128},{192,160},{224,1... | collective-permute-start | bytes 786440 | tf_op jit(solution)/shard_map/ppermute | solution.py:168
  90.3 2.1 %collective-permute-start.7 = (bf16[32,4096]{1,0:T(8,128)(2,1)S(1)}, bf16[32,4096]{1,0:T(8,128)(2,1)}, u32[]{:S(2)}, u32[]{:S(2)}) collective-permute-start(bf16[32,4096]{1,0:T(8,128)(2,1)S(1)} %collective-permute-done.6.refs_5_), channel_id=1, source_target_pairs={{0,480},{32,0},{64,32},{96,64},{128,96},{160,128},{192,160},{224,1... | collective-permute-start | bytes 786440 | tf_op jit(solution)/shard_map/ppermute | solution.py:168
  92.5 3.2 %collective-permute-start.31 = (bf16[32,4096]{1,0:T(8,128)(2,1)S(1)}, bf16[32,4096]{1,0:T(8,128)(2,1)}, u32[]{:S(2)}, u32[]{:S(2)}) collective-permute-start(bf16[32,4096]{1,0:T(8,128)(2,1)S(1)} %collective-permute-done.30.refs_27_), channel_id=1, source_target_pairs={{0,32},{32,64},{64,96},{96,128},{128,160},{160,192},{192,224},{224... | collective-permute-start | bytes 786440 | tf_op jit(solution)/shard_map/ppermute | solution.py:166
  95.7 1.9 collective-permute-start.15
  97.7 4.6 %collective-permute-start.24 = (bf16[32,4096]{1,0:T(8,128)(2,1)S(1)}, bf16[32,4096]{1,0:T(8,128)(2,1)}, u32[]{:S(2)}, u32[]{:S(2)}) collective-permute-start(bf16[32,4096]{1,0:T(8,128)(2,1)S(1)} %collective-permute-done.23.refs_22_), channel_id=1, source_target_pairs={{0,480},{32,0},{64,32},{96,64},{128,96},{160,128},{192,160},{224,1... | collective-permute-start | bytes 786440 | tf_op jit(solution)/shard_map/ppermute | solution.py:168
  102.3 3.3 %collective-permute-start.8 = (bf16[32,4096]{1,0:T(8,128)(2,1)}, bf16[32,4096]{1,0:T(8,128)(2,1)}, u32[]{:S(2)}, u32[]{:S(2)}) collective-permute-start(bf16[32,4096]{1,0:T(8,128)(2,1)} %collective-permute-done.7.refs_6_), channel_id=1, source_target_pairs={{0,480},{32,0},{64,32},{96,64},{128,96},{160,128},{192,160},{224,1... | collective-permute-start | bytes 786440 | tf_op jit(solution)/shard_map/ppermute | solution.py:168
  105.6 2.0 %collective-permute-start.32 = (bf16[32,4096]{1,0:T(8,128)(2,1)}, bf16[32,4096]{1,0:T(8,128)(2,1)}, u32[]{:S(2)}, u32[]{:S(2)}) collective-permute-start(bf16[32,4096]{1,0:T(8,128)(2,1)} %collective-permute-done.31.refs_26_), channel_id=1, source_target_pairs={{0,32},{32,64},{64,96},{96,128},{128,160},{160,192},{192,224},{224... | collective-permute-start | bytes 786440 | tf_op jit(solution)/shard_map/ppermute | solution.py:166
  107.6 1.9 collective-permute-start.16
  109.5 4.6 %collective-permute-start.25 = (bf16[32,4096]{1,0:T(8,128)(2,1)}, bf16[32,4096]{1,0:T(8,128)(2,1)}, u32[]{:S(2)}, u32[]{:S(2)}) collective-permute-start(bf16[32,4096]{1,0:T(8,128)(2,1)} %collective-permute-done.24.refs_23_), channel_id=1, source_target_pairs={{0,480},{32,0},{64,32},{96,64},{128,96},{160,128},{192,160},{224,1... | collective-permute-start | bytes 786440 | tf_op jit(solution)/shard_map/ppermute | solution.py:170
  114.2 5.6 %collective-permute-done.16.refs_8_ = bf16[32,4096]{1,0:T(8,128)(2,1)} collective-permute-done((bf16[32,4096]{1,0:T(8,128)(2,1)}, bf16[32,4096]{1,0:T(8,128)(2,1)}, u32[]{:S(2)}, u32[]{:S(2)}) %collective-permute-start.16) | collective-permute-done | bytes 262176 | tf_op jit(solution)/shard_map/ppermute | solution.py:169
  119.9 17.6 %sampled_gradient.1 = f32[64,128]{1,0:T(8,128)} custom-call(s32[1]{0:T(128)} %bitcast.place_ref, s32[64,128]{1,0:T(8,128)} %bitcast.12, bf16[2,1024,128]{2,1,0:T(8,128)(2,1)} %near_act_ref.1, bf16[2,1024,128]{2,1,0:T(8,128)(2,1)} %copy-done.3, bf16[128,4096]{1,0:T(8,128)(2,1)} %copy-done.1, bf16[2,256,512]{2,1,0:T(8,128)(2,1)} %constant.47.clone.table_ref, ...), custom_call_target="tpu_custom_call" | custom-call | tf_op jit(solution)/shard_map/sampled_gradient/pallas_call | solution.py:126
  137.4 12.2 %all-to-all-start = ((f32[32,1,256]{2,1,0:T(1,128)}), f32[32,1,256]{2,1,0:T(1,128)S(1)}, u32[]{:S(2)}, u32[]{:S(2)}) async-start(f32[32,1,256]{2,1,0:T(1,128)} %bitcast.11), calls=%async_computation | async-start | bytes 65536 | tf_op jit(solution)/shard_map/all_to_all | solution.py:195
  150.4 11.3 %all-to-all-done = f32[32,1,256]{2,1,0:T(1,128)S(1)} async-done(((f32[32,1,256]{2,1,0:T(1,128)}), f32[32,1,256]{2,1,0:T(1,128)S(1)}, u32[]{:S(2)}, u32[]{:S(2)}) %all-to-all-start) | async-done | bytes 32800 | tf_op jit(solution)/shard_map/all_to_all | solution.py:195
  161.9 13.0 %all_to_all.19 = f32[16,2,256]{2,1,0:T(2,128)S(1)} all-to-all(f32[16,2,256]{2,1,0:T(2,128)S(1)} %broadcast_in_dim.27), channel_id=1, replica_groups=mesh['z'=16,'core'=2,'ex'=16] {'ex'}, dimensions={0} | all-to-all | bytes 65536 | tf_op jit(solution)/shard_map/all_to_all | solution.py:176
  175.1 17.5 %all_to_all.20 = f32[32,2,32]{2,1,0:T(2,128)S(1)} all-to-all(f32[32,2,32]{2,1,0:T(2,128)S(1)} %broadcast_in_dim.28), channel_id=1, replica_groups=mesh['z'=16,'core'=2,'ex'=16] {'z','core'}, dimensions={0} | all-to-all | bytes 16384 | tf_op jit(solution)/shard_map/all_to_all | solution.py:176
  (108 shorter events, 20.3 us)
Async XLA Ops:
  1.7 10.7 %collective-permute-start.17 = (bf16[32,4096]{1,0:T(8,128)(2,1)S(1)}, bf16[32,4096]{1,0:T(8,128)(2,1)S(1)}, u32[]{:S(2)}, u32[]{:S(2)}) collective-permute-start(bf16[32,4096]{1,0:T(8,128)(2,1)S(1)} %get-tuple-element.2), channel_id=1, source_target_pairs={{0,16},{16,0},{1,17},{17,1},{2,18},{18,2},{3,19},{19,3},{4,20},{20... | collective-permute-start | bytes 786440 | tf_op jit(solution)/shard_map/ppermute | solution.py:186
  10.5 13.0 %collective-permute-start.9 = (bf16[32,4096]{1,0:T(8,128)(2,1)S(1)}, bf16[32,4096]{1,0:T(8,128)(2,1)S(1)}, u32[]{:S(2)}, u32[]{:S(2)}) collective-permute-start(bf16[32,4096]{1,0:T(8,128)(2,1)S(1)} %get-tuple-element.3.refs_0_), channel_id=1, source_target_pairs={{0,32},{32,64},{64,96},{96,128},{128,160},{160,192},{192,224},{224... | collective-permute-start | bytes 786440 | tf_op jit(solution)/shard_map/ppermute | solution.py:166
  12.5 13.0 %collective-permute-start.18 = (bf16[32,4096]{1,0:T(8,128)(2,1)S(1)}, bf16[32,4096]{1,0:T(8,128)(2,1)S(1)}, u32[]{:S(2)}, u32[]{:S(2)}) collective-permute-start(bf16[32,4096]{1,0:T(8,128)(2,1)S(1)} %collective-permute-done.17.refs_16_), channel_id=1, source_target_pairs={{0,480},{32,0},{64,32},{96,64},{128,96},{160,128},{192,160},{224,1... | collective-permute-start | bytes 786440 | tf_op jit(solution)/shard_map/ppermute | solution.py:168
  18.2 11.9 %collective-permute-start.2 = (bf16[32,4096]{1,0:T(8,128)(2,1)S(1)}, bf16[32,4096]{1,0:T(8,128)(2,1)S(1)}, u32[]{:S(2)}, u32[]{:S(2)}) collective-permute-start(bf16[32,4096]{1,0:T(8,128)(2,1)S(1)} %get-tuple-element.3.refs_0_), channel_id=1, source_target_pairs={{0,480},{32,0},{64,32},{96,64},{128,96},{160,128},{192,160},{224,1... | collective-permute-start | bytes 786440 | tf_op jit(solution)/shard_map/ppermute | solution.py:168
  21.6 13.3 %collective-permute-start.26 = (bf16[32,4096]{1,0:T(8,128)(2,1)S(1)}, bf16[32,4096]{1,0:T(8,128)(2,1)S(1)}, u32[]{:S(2)}, u32[]{:S(2)}) collective-permute-start(bf16[32,4096]{1,0:T(8,128)(2,1)S(1)} %collective-permute-done.17.refs_16_), channel_id=1, source_target_pairs={{0,32},{32,64},{64,96},{96,128},{128,160},{160,192},{192,224},{224... | collective-permute-start | bytes 786440 | tf_op jit(solution)/shard_map/ppermute | solution.py:166
  23.5 13.7 %collective-permute-start.10 = (bf16[32,4096]{1,0:T(8,128)(2,1)S(1)}, bf16[32,4096]{1,0:T(8,128)(2,1)S(1)}, u32[]{:S(2)}, u32[]{:S(2)}) collective-permute-start(bf16[32,4096]{1,0:T(8,128)(2,1)S(1)} %collective-permute-done.9.refs_15_), channel_id=1, source_target_pairs={{0,32},{32,64},{64,96},{96,128},{128,160},{160,192},{192,224},{224... | collective-permute-start | bytes 786440 | tf_op jit(solution)/shard_map/ppermute | solution.py:166
  25.5 13.7 %collective-permute-start.19 = (bf16[32,4096]{1,0:T(8,128)(2,1)S(1)}, bf16[32,4096]{1,0:T(8,128)(2,1)S(1)}, u32[]{:S(2)}, u32[]{:S(2)}) collective-permute-start(bf16[32,4096]{1,0:T(8,128)(2,1)S(1)} %collective-permute-done.18.refs_17_), channel_id=1, source_target_pairs={{0,480},{32,0},{64,32},{96,64},{128,96},{160,128},{192,160},{224,1... | collective-permute-start | bytes 786440 | tf_op jit(solution)/shard_map/ppermute | solution.py:168
  30.1 18.0 %collective-permute-start.3 = (bf16[32,4096]{1,0:T(8,128)(2,1)S(1)}, bf16[32,4096]{1,0:T(8,128)(2,1)S(1)}, u32[]{:S(2)}, u32[]{:S(2)}) collective-permute-start(bf16[32,4096]{1,0:T(8,128)(2,1)S(1)} %collective-permute-done.2.refs_1_), channel_id=1, source_target_pairs={{0,480},{32,0},{64,32},{96,64},{128,96},{160,128},{192,160},{224,1... | collective-permute-start | bytes 786440 | tf_op jit(solution)/shard_map/ppermute | solution.py:168
  34.9 15.7 %collective-permute-start.27 = (bf16[32,4096]{1,0:T(8,128)(2,1)S(1)}, bf16[32,4096]{1,0:T(8,128)(2,1)S(1)}, u32[]{:S(2)}, u32[]{:S(2)}) collective-permute-start(bf16[32,4096]{1,0:T(8,128)(2,1)S(1)} %collective-permute-done.26.refs_31_), channel_id=1, source_target_pairs={{0,32},{32,64},{64,96},{96,128},{128,160},{160,192},{192,224},{224... | collective-permute-start | bytes 786440 | tf_op jit(solution)/shard_map/ppermute | solution.py:166
  37.3 16.1 %collective-permute-start.11 = (bf16[32,4096]{1,0:T(8,128)(2,1)S(1)}, bf16[32,4096]{1,0:T(8,128)(2,1)S(1)}, u32[]{:S(2)}, u32[]{:S(2)}) collective-permute-start(bf16[32,4096]{1,0:T(8,128)(2,1)S(1)} %collective-permute-done.10.refs_14_), channel_id=1, source_target_pairs={{0,32},{32,64},{64,96},{96,128},{128,160},{160,192},{192,224},{224... | collective-permute-start | bytes 786440 | tf_op jit(solution)/shard_map/ppermute | solution.py:166
  39.2 16.1 %collective-permute-start.20 = (bf16[32,4096]{1,0:T(8,128)(2,1)S(1)}, bf16[32,4096]{1,0:T(8,128)(2,1)S(1)}, u32[]{:S(2)}, u32[]{:S(2)}) collective-permute-start(bf16[32,4096]{1,0:T(8,128)(2,1)S(1)} %collective-permute-done.19.refs_18_), channel_id=1, source_target_pairs={{0,480},{32,0},{64,32},{96,64},{128,96},{160,128},{192,160},{224,1... | collective-permute-start | bytes 786440 | tf_op jit(solution)/shard_map/ppermute | solution.py:168
  43.8 18.0 %collective-permute-start = (bf16[2,1024,128]{2,1,0:T(8,128)(2,1)}, bf16[2,1024,128]{2,1,0:T(8,128)(2,1)S(1)}, u32[]{:S(2)}, u32[]{:S(2)}) collective-permute-start(bf16[2,1024,128]{2,1,0:T(8,128)(2,1)} %near_act_ref.1), channel_id=1, source_target_pairs={{0,16},{16,0},{1,17},{17,1},{2,18},{18,2},{3,19},{19,3},{4,20},{20... | collective-permute-start | bytes 1572872 | tf_op jit(solution)/shard_map/ppermute | solution.py:187
  48.1 16.8 %collective-permute-start.4 = (bf16[32,4096]{1,0:T(8,128)(2,1)S(1)}, bf16[32,4096]{1,0:T(8,128)(2,1)S(1)}, u32[]{:S(2)}, u32[]{:S(2)}) collective-permute-start(bf16[32,4096]{1,0:T(8,128)(2,1)S(1)} %collective-permute-done.3.refs_2_), channel_id=1, source_target_pairs={{0,480},{32,0},{64,32},{96,64},{128,96},{160,128},{192,160},{224,1... | collective-permute-start | bytes 786440 | tf_op jit(solution)/shard_map/ppermute | solution.py:168
  50.6 16.8 %collective-permute-start.28 = (bf16[32,4096]{1,0:T(8,128)(2,1)S(1)}, bf16[32,4096]{1,0:T(8,128)(2,1)S(1)}, u32[]{:S(2)}, u32[]{:S(2)}) collective-permute-start(bf16[32,4096]{1,0:T(8,128)(2,1)S(1)} %collective-permute-done.27.refs_30_), channel_id=1, source_target_pairs={{0,32},{32,64},{64,96},{96,128},{128,160},{160,192},{192,224},{224... | collective-permute-start | bytes 786440 | tf_op jit(solution)/shard_map/ppermute | solution.py:166
  53.4 16.8 %collective-permute-start.12 = (bf16[32,4096]{1,0:T(8,128)(2,1)S(1)}, bf16[32,4096]{1,0:T(8,128)(2,1)S(1)}, u32[]{:S(2)}, u32[]{:S(2)}) collective-permute-start(bf16[32,4096]{1,0:T(8,128)(2,1)S(1)} %collective-permute-done.11.refs_13_), channel_id=1, source_target_pairs={{0,32},{32,64},{64,96},{96,128},{128,160},{160,192},{192,224},{224... | collective-permute-start | bytes 786440 | tf_op jit(solution)/shard_map/ppermute | solution.py:166
  55.4 16.8 %collective-permute-start.21 = (bf16[32,4096]{1,0:T(8,128)(2,1)S(1)}, bf16[32,4096]{1,0:T(8,128)(2,1)S(1)}, u32[]{:S(2)}, u32[]{:S(2)}) collective-permute-start(bf16[32,4096]{1,0:T(8,128)(2,1)S(1)} %collective-permute-done.20.refs_19_), channel_id=1, source_target_pairs={{0,480},{32,0},{64,32},{96,64},{128,96},{160,128},{192,160},{224,1... | collective-permute-start | bytes 786440 | tf_op jit(solution)/shard_map/ppermute | solution.py:168
  61.8 52.3 %collective-permute-start.1 = (bf16[128,4096]{1,0:T(8,128)(2,1)S(1)}, bf16[128,4096]{1,0:T(8,128)(2,1)S(1)}, u32[]{:S(2)}, u32[]{:S(2)}) collective-permute-start(bf16[128,4096]{1,0:T(8,128)(2,1)S(1)} %select_convert_fusion.near_ref), channel_id=1, source_target_pairs={{0,16},{16,0},{1,17},{17,1},{2,18},{18,2},{3,19},{19,3},{4,20},{20... | collective-permute-start | bytes 3145736 | tf_op jit(solution)/shard_map/ppermute | solution.py:189
  64.9 11.9 %collective-permute-start.5 = (bf16[32,4096]{1,0:T(8,128)(2,1)S(1)}, bf16[32,4096]{1,0:T(8,128)(2,1)S(1)}, u32[]{:S(2)}, u32[]{:S(2)}) collective-permute-start(bf16[32,4096]{1,0:T(8,128)(2,1)S(1)} %collective-permute-done.4.refs_3_), channel_id=1, source_target_pairs={{0,480},{32,0},{64,32},{96,64},{128,96},{160,128},{192,160},{224,1... | collective-permute-start | bytes 786440 | tf_op jit(solution)/shard_map/ppermute | solution.py:168
  67.5 11.9 %collective-permute-start.29 = (bf16[32,4096]{1,0:T(8,128)(2,1)S(1)}, bf16[32,4096]{1,0:T(8,128)(2,1)S(1)}, u32[]{:S(2)}, u32[]{:S(2)}) collective-permute-start(bf16[32,4096]{1,0:T(8,128)(2,1)S(1)} %collective-permute-done.28.refs_29_), channel_id=1, source_target_pairs={{0,32},{32,64},{64,96},{96,128},{128,160},{160,192},{192,224},{224... | collective-permute-start | bytes 786440 | tf_op jit(solution)/shard_map/ppermute | solution.py:166
  70.2 13.5 %collective-permute-start.13 = (bf16[32,4096]{1,0:T(8,128)(2,1)S(1)}, bf16[32,4096]{1,0:T(8,128)(2,1)S(1)}, u32[]{:S(2)}, u32[]{:S(2)}) collective-permute-start(bf16[32,4096]{1,0:T(8,128)(2,1)S(1)} %collective-permute-done.12.refs_12_), channel_id=1, source_target_pairs={{0,32},{32,64},{64,96},{96,128},{128,160},{160,192},{192,224},{224... | collective-permute-start | bytes 786440 | tf_op jit(solution)/shard_map/ppermute | solution.py:166
  72.2 13.5 %collective-permute-start.22 = (bf16[32,4096]{1,0:T(8,128)(2,1)S(1)}, bf16[32,4096]{1,0:T(8,128)(2,1)S(1)}, u32[]{:S(2)}, u32[]{:S(2)}) collective-permute-start(bf16[32,4096]{1,0:T(8,128)(2,1)S(1)} %collective-permute-done.21.refs_20_), channel_id=1, source_target_pairs={{0,480},{32,0},{64,32},{96,64},{128,96},{160,128},{192,160},{224,1... | collective-permute-start | bytes 786440 | tf_op jit(solution)/shard_map/ppermute | solution.py:168
  76.8 13.5 %collective-permute-start.6 = (bf16[32,4096]{1,0:T(8,128)(2,1)S(1)}, bf16[32,4096]{1,0:T(8,128)(2,1)S(1)}, u32[]{:S(2)}, u32[]{:S(2)}) collective-permute-start(bf16[32,4096]{1,0:T(8,128)(2,1)S(1)} %collective-permute-done.5.refs_4_), channel_id=1, source_target_pairs={{0,480},{32,0},{64,32},{96,64},{128,96},{160,128},{192,160},{224,1... | collective-permute-start | bytes 786440 | tf_op jit(solution)/shard_map/ppermute | solution.py:168
  79.4 13.1 %collective-permute-start.30 = (bf16[32,4096]{1,0:T(8,128)(2,1)S(1)}, bf16[32,4096]{1,0:T(8,128)(2,1)S(1)}, u32[]{:S(2)}, u32[]{:S(2)}) collective-permute-start(bf16[32,4096]{1,0:T(8,128)(2,1)S(1)} %collective-permute-done.29.refs_28_), channel_id=1, source_target_pairs={{0,32},{32,64},{64,96},{96,128},{128,160},{160,192},{192,224},{224... | collective-permute-start | bytes 786440 | tf_op jit(solution)/shard_map/ppermute | solution.py:166
  83.8 11.9 %collective-permute-start.14 = (bf16[32,4096]{1,0:T(8,128)(2,1)S(1)}, bf16[32,4096]{1,0:T(8,128)(2,1)S(1)}, u32[]{:S(2)}, u32[]{:S(2)}) collective-permute-start(bf16[32,4096]{1,0:T(8,128)(2,1)S(1)} %collective-permute-done.13.refs_11_), channel_id=1, source_target_pairs={{0,32},{32,64},{64,96},{96,128},{128,160},{160,192},{192,224},{224... | collective-permute-start | bytes 786440 | tf_op jit(solution)/shard_map/ppermute | solution.py:166
  85.7 11.9 %collective-permute-start.23 = (bf16[32,4096]{1,0:T(8,128)(2,1)S(1)}, bf16[32,4096]{1,0:T(8,128)(2,1)S(1)}, u32[]{:S(2)}, u32[]{:S(2)}) collective-permute-start(bf16[32,4096]{1,0:T(8,128)(2,1)S(1)} %collective-permute-done.22.refs_21_), channel_id=1, source_target_pairs={{0,480},{32,0},{64,32},{96,64},{128,96},{160,128},{192,160},{224,1... | collective-permute-start | bytes 786440 | tf_op jit(solution)/shard_map/ppermute | solution.py:168
  90.3 11.9 %collective-permute-start.7 = (bf16[32,4096]{1,0:T(8,128)(2,1)S(1)}, bf16[32,4096]{1,0:T(8,128)(2,1)}, u32[]{:S(2)}, u32[]{:S(2)}) collective-permute-start(bf16[32,4096]{1,0:T(8,128)(2,1)S(1)} %collective-permute-done.6.refs_5_), channel_id=1, source_target_pairs={{0,480},{32,0},{64,32},{96,64},{128,96},{160,128},{192,160},{224,1... | collective-permute-start | bytes 786440 | tf_op jit(solution)/shard_map/ppermute | solution.py:168
  92.5 13.0 %collective-permute-start.31 = (bf16[32,4096]{1,0:T(8,128)(2,1)S(1)}, bf16[32,4096]{1,0:T(8,128)(2,1)}, u32[]{:S(2)}, u32[]{:S(2)}) collective-permute-start(bf16[32,4096]{1,0:T(8,128)(2,1)S(1)} %collective-permute-done.30.refs_27_), channel_id=1, source_target_pairs={{0,32},{32,64},{64,96},{96,128},{128,160},{160,192},{192,224},{224... | collective-permute-start | bytes 786440 | tf_op jit(solution)/shard_map/ppermute | solution.py:166
  95.7 11.9 %collective-permute-start.15 = (bf16[32,4096]{1,0:T(8,128)(2,1)S(1)}, bf16[32,4096]{1,0:T(8,128)(2,1)}, u32[]{:S(2)}, u32[]{:S(2)}) collective-permute-start(bf16[32,4096]{1,0:T(8,128)(2,1)S(1)} %collective-permute-done.14.refs_10_), channel_id=1, source_target_pairs={{0,32},{32,64},{64,96},{96,128},{128,160},{160,192},{192,224},{224... | collective-permute-start | bytes 786440 | tf_op jit(solution)/shard_map/ppermute | solution.py:166
  97.7 11.9 %collective-permute-start.24 = (bf16[32,4096]{1,0:T(8,128)(2,1)S(1)}, bf16[32,4096]{1,0:T(8,128)(2,1)}, u32[]{:S(2)}, u32[]{:S(2)}) collective-permute-start(bf16[32,4096]{1,0:T(8,128)(2,1)S(1)} %collective-permute-done.23.refs_22_), channel_id=1, source_target_pairs={{0,480},{32,0},{64,32},{96,64},{128,96},{160,128},{192,160},{224,1... | collective-permute-start | bytes 786440 | tf_op jit(solution)/shard_map/ppermute | solution.py:168
  102.3 11.9 %collective-permute-start.8 = (bf16[32,4096]{1,0:T(8,128)(2,1)}, bf16[32,4096]{1,0:T(8,128)(2,1)}, u32[]{:S(2)}, u32[]{:S(2)}) collective-permute-start(bf16[32,4096]{1,0:T(8,128)(2,1)} %collective-permute-done.7.refs_6_), channel_id=1, source_target_pairs={{0,480},{32,0},{64,32},{96,64},{128,96},{160,128},{192,160},{224,1... | collective-permute-start | bytes 786440 | tf_op jit(solution)/shard_map/ppermute | solution.py:168
  107.6 12.2 %collective-permute-start.16 = (bf16[32,4096]{1,0:T(8,128)(2,1)}, bf16[32,4096]{1,0:T(8,128)(2,1)}, u32[]{:S(2)}, u32[]{:S(2)}) collective-permute-start(bf16[32,4096]{1,0:T(8,128)(2,1)} %collective-permute-done.15.refs_9_), channel_id=1, source_target_pairs={{0,32},{32,64},{64,96},{96,128},{128,160},{160,192},{192,224},{224... | collective-permute-start | bytes 786440 | tf_op jit(solution)/shard_map/ppermute | solution.py:169
  137.4 24.3 %all-to-all-start = ((f32[32,1,256]{2,1,0:T(1,128)}), f32[32,1,256]{2,1,0:T(1,128)S(1)}, u32[]{:S(2)}, u32[]{:S(2)}) async-start(f32[32,1,256]{2,1,0:T(1,128)} %bitcast.11), calls=%async_computation | async-start | bytes 65536 | tf_op jit(solution)/shard_map/all_to_all | solution.py:195
  (30 other events, 757.2 us)
